TPU v7x, 768 devices: a whole 4x8x12 slice. The times are simulated.
768 devices in a mesh: panel: 2 (over y_hi), rad: 12 (over z), ang: 32 (over x, y_lo, core).
Axes of the slice: x: 4, y: 8 (y_hi: 2, y_lo: 4; y = y_hi * 4 + y_lo), z: 12, core: 2. Of those that a mesh axis runs over, the one named last changes fastest.
Arguments:
- state: float32 [2, 7, 192, 512, 128], P('panel', None, 'rad', 'ang'), may hold values from -6 to 6
- kappa: float32 [7, 192], P(None, 'rad'), may hold values from 0.3 to 1.5
- buoyancy: float32 [192], P('rad'), may hold values from 0.5 to 2
- donor_lon: int32 [2, 512], replicated, may hold values from 0 to 510, as said below
- donor_lat: int32 [2, 512], replicated, may hold values from 1 to 125
- fractions: float32 [2, 2, 512], replicated, may hold values from 0.05 to 0.95
Outputs:
- state_next: float32 [2, 7, 192, 512, 128], P('panel', None, 'rad', 'ang')
Inputs may be any that keep to these rules, and one draw needn't show every extreme that they name: donor_lon % 16 <= 14, so each donor stencil lies in one tile of 16 longitudes; of the 32 boundary points of one receiving tile of 16 longitudes at most 2 draw on one donor tile, and some draw exactly 2.
All inputs are finite; a program needn't handle non-finite values.
Results may differ from a plain program's by a relative error of at most 0.00002.
Values sent between devices are 32-bit elements; how exact they have to be, the bound alone decides.
No kernel may reach another device: no remote copies, remote signals or barrier semaphores. Data moves between devices by JAX's collectives and lax.ppermute only.
A program may use at most 64 MiB of HBM per device.

v0:
```python
import jax
import jax.numpy as jnp
from jax import lax
from jax.sharding import PartitionSpec as P

step_size = 0.1


def with_halo(block, sides, width):
    for axis, dim in sides:
        count = lax.axis_size(axis)
        forward = [(i, i + 1) for i in range(count - 1)]
        backward = [(target, source) for source, target in forward]
        low = lax.ppermute(
            lax.slice_in_dim(block, block.shape[dim] - width, None, axis=dim), axis, forward
        )
        high = lax.ppermute(lax.slice_in_dim(block, 0, width, axis=dim), axis, backward)
        block = jnp.concatenate([low, block, high], axis=dim)
    return block


def partner(value, axis, apart):
    return lax.ppermute(value, axis, [(i, i ^ 1 << apart) for i in range(lax.axis_size(axis))])


def spatial(padded, kappa, buoyancy):
    grid = jnp.pad(padded, ((0, 0), (0, 0), (0, 0), (1, 1)))
    center = grid[:, 1:-1, 1:-1, 1:-1]
    plus = [grid[:, 2:, 1:-1, 1:-1], grid[:, 1:-1, 2:, 1:-1], grid[:, 1:-1, 1:-1, 2:]]
    minus = [grid[:, :-2, 1:-1, 1:-1], grid[:, 1:-1, :-2, 1:-1], grid[:, 1:-1, 1:-1, :-2]]
    laplace = plus[0] + minus[0] + (plus[1] + minus[1]) + (plus[2] + minus[2]) - 6.0 * center
    grads = [0.5 * (plus[0] - minus[0]), 0.5 * (plus[1] - minus[1]), 0.5 * (plus[2] - minus[2])]
    along_u = center[0] * grads[0] + center[1] * grads[1] + center[2] * grads[2]
    along_b = center[3] * grads[0] + center[4] * grads[1] + center[5] * grads[2]
    forcing = jnp.concatenate([along_b[3:6], along_b[0:3], jnp.zeros_like(center[6:7])], 0)
    lift = jnp.concatenate(
        [buoyancy[None, :, None, None] * center[6:7], jnp.zeros_like(center[1:7])], 0
    )
    return kappa[:, :, None, None] * laplace - along_u + forcing + lift


def blend(local, lon_idx, lat_idx, frac_lon, frac_lat):
    w_one = (1.0 - frac_lon) * (1.0 - frac_lat)
    w_two = frac_lon * (1.0 - frac_lat)
    w_three = (1.0 - frac_lon) * frac_lat
    w_four = frac_lon * frac_lat
    return (
        w_one * local[:, :, lon_idx, lat_idx]
        + w_two * local[:, :, lon_idx + 1, lat_idx]
        + w_three * local[:, :, lon_idx, lat_idx + 1]
        + w_four * local[:, :, lon_idx + 1, lat_idx + 1]
    )


def body(state, kappa, buoyancy, donor_lon, donor_lat, fractions):
    tile = lax.axis_index("ang")
    cells = state.shape[3]
    levels = state.shape[2]
    lat_len = state.shape[4]

    def rates(field):
        padded = with_halo(field, (("rad", 2), ("ang", 3)), 1)
        return spatial(padded[0], kappa, buoyancy)[None]

    def strips_for(local):
        flon_part = fractions[0]
        flat_part = fractions[1]
        owner = donor_lon // cells
        local_lon = jnp.clip(donor_lon - tile * cells, 0, cells - 2)
        values = blend(local, local_lon, donor_lat, flon_part, flat_part)
        values = jnp.where((owner == tile)[None, None], values, 0.0)
        mine = lax.psum_scatter(
            jnp.transpose(values, (3, 2, 0, 1)).reshape(
                cells * lax.axis_size("ang"), 2, 7 * levels
            ),
            "ang",
            scatter_dimension=0,
            tiled=True,
        )
        return jnp.transpose(mine.reshape(cells, 2, 7, levels), (1, 2, 3, 0))

    def couple(field):
        strips = strips_for(field[0])
        received = partner(strips, "panel", 0)
        field = field.at[0, :, :, :, 0].set(received[0])
        return field.at[0, :, :, :, lat_len - 1].set(received[1])

    rates_zero = rates(state)
    first = couple(state + step_size * rates_zero)
    rates_one = rates(first)
    return couple(0.5 * (state + first + step_size * rates_one))


def solution(mesh):
    return jax.shard_map(
        body,
        mesh=mesh,
        in_specs=(P("panel", None, "rad", "ang", None), P(None, "rad"), P("rad"), P(), P(), P()),
        out_specs=P("panel", None, "rad", "ang", None),
        check_vma=False,
    )
```

profile of v0, /device:TPU:64, one launch (start us, length us, event | category | flops | bytes accessed | tf_op | source)
XLA Modules:
  0.0 575.5 jit_solution(6327707391347148921)
XLA Ops:
  6.5 0.9 fusion.54
  7.4 4.3 collective-permute-start
  11.7 7.6 %collective-permute-start.1 = (f32[1,7,1,16,128]{4,3,2,1,0:T(8,128)S(1)}, f32[1,7,1,16,128]{4,3,2,1,0:T(8,128)S(1)}, u32[]{:S(2)}, u32[]{:S(2)}) collective-permute-start(f32[1,7,1,16,128]{4,3,2,1,0:T(8,128)S(1)} %get-tuple-element.77), channel_id=1, source_target_pairs={{32,0},{64,32},{96,64},{128,96},{160,128},{192,160},{224,192},{256... | collective-permute-start | bytes 172040 | tf_op jit(solution)/shard_map/ppermute | solution.py:17
  19.3 0.7 or_bitcast_fusion.3
  20.0 0.7 multiply_bitcast_fusion
  20.8 1.2 constant_dynamic-update-slice_fusion.1
  22.1 1.3 collective-permute-start.2
  23.4 1.3 collective-permute-start.3
  24.7 0.7 compare_bitcast_fusion
  25.6 1.0 collective-permute-done.3
  27.0 0.7 multiply_add_fusion.1
  27.8 0.4 copy-done
  28.2 1.2 fusion.16
  29.4 4.5 copy.135
  33.9 13.0 %gather_fusion = f32[1024,7,16]{2,1,0:T(8,128)} fusion(f32[7,16,16,128]{1,0,3,2:T(8,128)} %copy.135, s32[1024]{0:T(1024)S(1)} %bitcast.154), kind=kCustom, calls=%fused_computation | custom fusion | bytes 925696 | tf_op jit(solution)/shard_map/gather | solution.py:48
  46.9 2.8 copy.161
  49.7 13.0 %gather_fusion.1 = f32[1024,7,16]{2,1,0:T(8,128)} fusion(f32[7,16,16,128]{1,0,3,2:T(8,128)} %copy.135, s32[1024]{0:T(1024)S(1)} %bitcast.156), kind=kCustom, calls=%fused_computation.1 | custom fusion | bytes 925696 | tf_op jit(solution)/shard_map/gather | solution.py:49
  62.7 2.8 copy.162
  65.5 13.0 %gather_fusion.2 = f32[1024,7,16]{2,1,0:T(8,128)} fusion(f32[7,16,16,128]{1,0,3,2:T(8,128)} %copy.135, s32[1024]{0:T(1024)S(1)} %bitcast.158), kind=kCustom, calls=%fused_computation.2 | custom fusion | bytes 925696 | tf_op jit(solution)/shard_map/gather | solution.py:50
  78.5 2.8 copy.163
  81.3 13.0 %gather_fusion.3 = f32[1024,7,16]{2,1,0:T(8,128)} fusion(f32[7,16,16,128]{1,0,3,2:T(8,128)} %copy.135, s32[1024]{0:T(1024)S(1)} %bitcast.160), kind=kCustom, calls=%fused_computation.3 | custom fusion | bytes 925696 | tf_op jit(solution)/shard_map/gather | solution.py:51
  94.4 3.4 copy.164
  97.8 2.3 fusion.24
  100.1 2.0 copy.143
  102.2 0.7 fusion.55
  102.9 1.3 concatenate.58
  104.2 157.8 %reduce-scatter.3.cloned.1.call-done = f32[16,2,112]{2,0,1:T(8,128)} async-done(((f32[512,2,112]{2,0,1:T(8,128)}), f32[16,2,112]{2,0,1:T(8,128)}) %reduce-scatter.3.cloned.1.call-update) | async-done | bytes 14352 | tf_op jit(solution)/shard_map/reduce_scatter | solution.py:72
  262.0 0.8 reshape.251
  262.8 3.7 collective-permute-start.4
  266.5 0.7 and_reduce_fusion
  267.2 6.4 %collective-permute-done.4 = f32[2,7,16,16]{2,1,3,0:T(8,128)S(1)} collective-permute-done((f32[2,7,16,16]{2,1,3,0:T(8,128)S(1)}, f32[2,7,16,16]{2,1,3,0:T(8,128)S(1)}, u32[]{:S(2)}, u32[]{:S(2)}) %collective-permute-start.4) | collective-permute-done | bytes 14368 | tf_op jit(solution)/shard_map/ppermute | solution.py:23
  273.6 0.7 copy.145
  274.3 1.6 copy.147
  276.0 6.8 %scatter.14 = f32[1,7,16,16,128]{4,3,2,1,0:T(8,128)S(1)} dynamic-update-slice(f32[1,7,16,16,128]{4,3,2,1,0:T(8,128)S(1)} %fusion.16, f32[1,7,16,16,1]{4,3,2,1,0:T(8,128)S(1)} %copy.145, s32[]{:T(128)} %constant.132.clone.1, s32[]{:T(128)} %constant.132.clone.1, s32[]{:T(128)} %constant.132.clone.1, s32[]{:T(128)} %constant.132.clone.1, s32[]{:T(128)} %constant.132.clone.1) | dynamic-update-slice | bytes 14340 | tf_op jit(solution)/shard_map/scatter | solution.py:85
  282.8 2.8 dynamic-slice_select_fusion.1
  285.6 14.9 %scatter.15 = f32[1,7,16,16,128]{4,3,2,1,0:T(8,128)S(1)} dynamic-update-slice(f32[1,7,16,16,128]{4,3,2,1,0:T(8,128)S(1)} %scatter.14, f32[1,7,16,16,1]{4,3,2,1,0:T(8,128)S(1)} %dynamic-slice_select_fusion.1, s32[]{:T(128)} %constant.132.clone.1, s32[]{:T(128)} %constant.132.clone.1, s32[]{:T(128)} %constant.132.clone.1, s32[]{:T(128)} %constant.132.clone.1, s32[]{:T(128)} %bitcast.28) | dynamic-update-slice | bytes 14340 | tf_op jit(solution)/shard_map/scatter | solution.py:86
  300.5 3.7 collective-permute-start.5
  304.3 2.3 collective-permute-start.6
  306.8 3.6 collective-permute-done.6
  310.4 1.3 collective-permute-start.7
  311.7 1.3 collective-permute-start.8
  313.0 1.8 collective-permute-done.8
  315.3 0.7 multiply_add_fusion
  316.0 1.4 fusion.8
  317.5 4.5 copy.148
  322.0 13.0 %gather_fusion.4 = f32[1024,7,16]{2,1,0:T(8,128)} fusion(f32[7,16,16,128]{1,0,3,2:T(8,128)} %copy.148, s32[1024]{0:T(1024)S(1)} %bitcast.155), kind=kCustom, calls=%fused_computation.4 | custom fusion | bytes 925696 | tf_op jit(solution)/shard_map/gather | solution.py:48
  335.0 12.9 %gather_fusion.5 = f32[1024,7,16]{2,1,0:T(8,128)} fusion(f32[7,16,16,128]{1,0,3,2:T(8,128)} %copy.148, s32[1024]{0:T(1024)S(1)} %bitcast.157), kind=kCustom, calls=%fused_computation.5 | custom fusion | bytes 925696 | tf_op jit(solution)/shard_map/gather | solution.py:49
  347.9 13.0 %gather_fusion.6 = f32[1024,7,16]{2,1,0:T(8,128)} fusion(f32[7,16,16,128]{1,0,3,2:T(8,128)} %copy.148, s32[1024]{0:T(1024)S(1)} %bitcast.159), kind=kCustom, calls=%fused_computation.6 | custom fusion | bytes 925696 | tf_op jit(solution)/shard_map/gather | solution.py:50
  360.9 13.0 %gather_fusion.7 = f32[1024,7,16]{2,1,0:T(8,128)} fusion(f32[7,16,16,128]{1,0,3,2:T(8,128)} %copy.148, s32[1024]{0:T(1024)S(1)} %bitcast.161), kind=kCustom, calls=%fused_computation.7 | custom fusion | bytes 925696 | tf_op jit(solution)/shard_map/gather | solution.py:51
  374.0 2.8 copy.169
  376.7 2.8 copy.170
  379.5 2.8 copy.171
  382.3 2.8 copy.172
  385.1 0.5 fusion.20
  385.6 1.0 copy.156
  386.7 148.5 %reduce-scatter.5.cloned.1.call-done = f32[16,2,112]{2,0,1:T(8,128)} async-done(((f32[512,2,112]{2,0,1:T(8,128)}), f32[16,2,112]{2,0,1:T(8,128)}) %reduce-scatter.5.cloned.1.call-update) | async-done | bytes 14352 | tf_op jit(solution)/shard_map/reduce_scatter | solution.py:72
  535.2 0.8 reshape.256
  536.0 3.5 collective-permute-start.9
  539.5 7.3 %collective-permute-done.9 = f32[2,7,16,16]{2,1,3,0:T(8,128)S(1)} collective-permute-done((f32[2,7,16,16]{2,1,3,0:T(8,128)S(1)}, f32[2,7,16,16]{2,1,3,0:T(8,128)S(1)}, u32[]{:S(2)}, u32[]{:S(2)}) %collective-permute-start.9) | collective-permute-done | bytes 14368 | tf_op jit(solution)/shard_map/ppermute | solution.py:23
  546.8 0.7 copy.158
  547.5 6.9 %scatter.16 = f32[1,7,16,16,128]{4,3,2,1,0:T(8,128)S(1)} dynamic-update-slice(f32[1,7,16,16,128]{4,3,2,1,0:T(8,128)S(1)} %fusion.8, f32[1,7,16,16,1]{4,3,2,1,0:T(8,128)S(1)} %copy.158, s32[]{:T(128)} %constant.132.clone.1, s32[]{:T(128)} %constant.132.clone.1, s32[]{:T(128)} %constant.132.clone.1, s32[]{:T(128)} %constant.132.clone.1, s32[]{:T(128)} %constant.132.clone.1) | dynamic-update-slice | bytes 14340 | tf_op jit(solution)/shard_map/scatter | solution.py:85
  554.4 0.7 copy.160
  555.1 1.6 dynamic-slice_select_fusion
  556.8 11.9 %scatter.19 = f32[1,7,16,16,128]{4,3,2,1,0:T(8,128)} dynamic-update-slice(f32[1,7,16,16,128]{4,3,2,1,0:T(8,128)} %copy-done.1, f32[1,7,16,16,1]{4,3,2,1,0:T(8,128)S(1)} %dynamic-slice_select_fusion, s32[]{:T(128)} %constant.132.clone.1, s32[]{:T(128)} %constant.132.clone.1, s32[]{:T(128)} %constant.132.clone.1, s32[]{:T(128)} %constant.132.clone.1, s32[]{:T(128)} %bitcast.28) | dynamic-update-slice | bytes 14340 | tf_op jit(solution)/shard_map/scatter | solution.py:86
  (37 shorter events, 1.5 us)
Async XLA Ops:
  6.5 20.3 %copy-start.3 = (f32[16]{0:T(128)S(1)}, f32[16]{0:T(128)}, u32[]{:S(2)}) copy-start(f32[16]{0:T(128)} %param.16) | copy-start | bytes 196
  6.5 255.4 %reduce-scatter.3.cloned.1.call-start = ((), (), s32[]{:S(2)}) async-start(), calls=%async_computation.2 | async-start | bytes 540672 | tf_op jit(solution)/shard_map/reduce_scatter | solution.py:72
  7.4 13.3 %collective-permute-start = (f32[1,7,1,16,128]{4,3,2,1,0:T(8,128)S(1)}, f32[1,7,1,16,128]{4,3,2,1,0:T(8,128)S(1)}, u32[]{:S(2)}, u32[]{:S(2)}) collective-permute-start(f32[1,7,1,16,128]{4,3,2,1,0:T(8,128)S(1)} %get-tuple-element.78), channel_id=1, source_target_pairs={{0,32},{32,64},{64,96},{96,128},{128,160},{160,192},{192,224},{224... | collective-permute-start | bytes 172040 | tf_op jit(solution)/shard_map/ppermute | solution.py:14
  11.7 10.3 %collective-permute-start.1 = (f32[1,7,1,16,128]{4,3,2,1,0:T(8,128)S(1)}, f32[1,7,1,16,128]{4,3,2,1,0:T(8,128)S(1)}, u32[]{:S(2)}, u32[]{:S(2)}) collective-permute-start(f32[1,7,1,16,128]{4,3,2,1,0:T(8,128)S(1)} %get-tuple-element.77), channel_id=1, source_target_pairs={{32,0},{64,32},{96,64},{128,96},{160,128},{192,160},{224,192},{256... | collective-permute-start | bytes 172040 | tf_op jit(solution)/shard_map/ppermute | solution.py:17
  22.1 3.4 collective-permute-start.2
  23.4 3.1 collective-permute-start.3
  27.0 1.2 copy-start
  27.0 1.2 copy-start.2
  94.4 172.1 %copy-start.4 = (s32[5]{0:T(128)S(1)}, s32[5]{0:T(128)}, u32[]{:S(2)}) copy-start(s32[5]{0:T(128)} %constant.145.clone.1) | copy-start | bytes 64
  102.2 433.0 %reduce-scatter.5.cloned.1.call-start = ((), (), s32[]{:S(2)}) async-start(), calls=%async_computation.3 | async-start | bytes 540672 | tf_op jit(solution)/shard_map/reduce_scatter | solution.py:72
  262.8 10.8 %collective-permute-start.4 = (f32[2,7,16,16]{2,1,3,0:T(8,128)S(1)}, f32[2,7,16,16]{2,1,3,0:T(8,128)S(1)}, u32[]{:S(2)}, u32[]{:S(2)}) collective-permute-start(f32[2,7,16,16]{2,1,3,0:T(8,128)S(1)} %bitcast.174), channel_id=1, source_target_pairs={{0,384},{384,0},{1,385},{385,1},{2,386},{386,2},{3,387},{387,3},{4... | collective-permute-start | bytes 43016 | tf_op jit(solution)/shard_map/ppermute | solution.py:23
  300.5 6.3 %collective-permute-start.5 = (f32[1,7,1,16,128]{4,3,2,1,0:T(8,128)S(1)}, f32[1,7,1,16,128]{4,3,2,1,0:T(8,128)S(1)}, u32[]{:S(2)}, u32[]{:S(2)}) collective-permute-start(f32[1,7,1,16,128]{4,3,2,1,0:T(8,128)S(1)} %get-tuple-element.73), channel_id=1, source_target_pairs={{0,32},{32,64},{64,96},{96,128},{128,160},{160,192},{192,224},{224... | collective-permute-start | bytes 172040 | tf_op jit(solution)/shard_map/ppermute | solution.py:14
  304.3 6.1 %collective-permute-start.6 = (f32[1,7,1,16,128]{4,3,2,1,0:T(8,128)S(1)}, f32[1,7,1,16,128]{4,3,2,1,0:T(8,128)S(1)}, u32[]{:S(2)}, u32[]{:S(2)}) collective-permute-start(f32[1,7,1,16,128]{4,3,2,1,0:T(8,128)S(1)} %get-tuple-element.74), channel_id=1, source_target_pairs={{32,0},{64,32},{96,64},{128,96},{160,128},{192,160},{224,192},{256... | collective-permute-start | bytes 172040 | tf_op jit(solution)/shard_map/ppermute | solution.py:17
  310.4 2.6 collective-permute-start.7
  311.7 3.1 collective-permute-start.8
  536.0 10.8 %collective-permute-start.9 = (f32[2,7,16,16]{2,1,3,0:T(8,128)S(1)}, f32[2,7,16,16]{2,1,3,0:T(8,128)S(1)}, u32[]{:S(2)}, u32[]{:S(2)}) collective-permute-start(f32[2,7,16,16]{2,1,3,0:T(8,128)S(1)} %bitcast.175), channel_id=1, source_target_pairs={{0,384},{384,0},{1,385},{385,1},{2,386},{386,2},{3,387},{387,3},{4... | collective-permute-start | bytes 43016 | tf_op jit(solution)/shard_map/ppermute | solution.py:23
  554.4 2.4 copy-start.1
Sparse Core Ops, SparseCore 0:
  102.3 159.6 reduce-scatter.2
  386.8 148.2 reduce-scatter.4
where the time goes:
time: 577 us; the launch traced here: 576 us
  waiting for transfers between devices  327 us (57%)
  local copies, waits for them, and re-layouts  190 us (33%)
  starting transfers between devices  30.3 us (5%)
  other arithmetic  15.1 us (3%)
  between operations  13.8 us (2%)
    reduce_scatter x2, waiting for transfers between devices, strips_for(): lax.psum_scatter(jnp.transpose(values, (3, 2, 0, 1)).reshape(cells * lax....  306 us
    gather x4, local copies, waits for them, and re-layouts, blend(): local[:, :, lon_idx + 1, lat_idx + 1]  32.3 us
    gather x4, local copies, waits for them, and re-layouts, blend(): local[:, :, lon_idx, lat_idx + 1]  31.6 us
    gather x4, local copies, waits for them, and re-layouts, blend(): local[:, :, lon_idx, lat_idx]  31.6 us
    gather x4, local copies, waits for them, and re-layouts, blend(): local[:, :, lon_idx + 1, lat_idx]  31.5 us
    scatter x2, local copies, waits for them, and re-layouts, couple(): return field.at[0, :, :, :, lat_len - 1].set(received[1])  26.8 us
    scatter x2, local copies, waits for them, and re-layouts, couple(): field = field.at[0, :, :, :, 0].set(received[0])  13.7 us
    ppermute x2, waiting for transfers between devices, partner(): lax.ppermute(value, axis, [(i, i ^ 1 << apart) for i in range(lax.axis_si...  13.6 us
  transfers between devices with their start and end apart: 12, of which 8 were waited for; matrix products, arithmetic and copies ran while one was open for 1% of the time, Pallas kernels for 0%

commit v1 on v0

v1 whole, which is shorter than its diff:
```python
import jax
import jax.numpy as jnp
from jax import lax
from jax.experimental import pallas as pl
from jax.experimental.pallas import tpu as pltpu
from jax.sharding import PartitionSpec as P

step_size = 0.1
HIGHEST = lax.Precision.HIGHEST
VMEM = pl.BlockSpec(memory_space=pltpu.VMEM)
F32 = jnp.float32

NF = 7
LV = 16
CP = 16
LAT = 128
ROWS = 24
NPTS = NF * LV


def params(**more):
    return pltpu.CompilerParams(vmem_limit_bytes=40 * 1024 * 1024, **more)


def picks(match, kid, slot):
    low = jnp.min(jnp.where(match, kid, 4096.0), axis=1, keepdims=True)
    high = jnp.max(jnp.where(match, kid, -1.0), axis=1, keepdims=True)
    low_or_none = jnp.where(low < 4096.0, low, -8.0)
    high_or_none = jnp.where(high > low, high, -8.0)
    return jnp.where(slot == 0, low_or_none, high_or_none)


def tables_kernel(where_ref, lon_ref, lat_ref, frac_ref, weights_ref, place_ref):
    n_ang = lon_ref.shape[1] // CP
    nlon = lon_ref.shape[1]
    rows = 2 * n_ang
    points = 2 * nlon
    panel = where_ref[0]
    tile = where_ref[2]

    def flat(ref):
        return jnp.concatenate([ref[0:1, :], ref[1:2, :]], axis=1)

    lon_k = flat(lon_ref)
    owner_k = lon_k >> 4
    off_k = (lon_k & 15).astype(F32)
    lat_k = flat(lat_ref).astype(F32)
    fx_k = jnp.concatenate([frac_ref[0, 0:1, :], frac_ref[0, 1:2, :]], axis=1)
    fy_k = jnp.concatenate([frac_ref[1, 0:1, :], frac_ref[1, 1:2, :]], axis=1)

    kid = lax.broadcasted_iota(jnp.int32, (1, points), 1)
    dest_k = (kid & (nlon - 1)) >> 4
    kid = kid.astype(F32)

    row = lax.broadcasted_iota(jnp.int32, (rows, 1), 0)
    match = (dest_k == (row >> 1)) & (owner_k == tile)
    pick = picks(match, kid, row & 1)
    chosen = kid == pick

    def of(value):
        return jnp.sum(jnp.where(chosen, value, 0.0), axis=1, keepdims=True)

    off, lat, fx, fy = of(off_k), of(lat_k), of(fx_k), of(fy_k)
    lane = lax.broadcasted_iota(jnp.int32, (rows, LAT), 1).astype(F32)
    lat_weight = jnp.where(lane == lat, 1.0 - fy, 0.0) + jnp.where(lane == lat + 1.0, fy, 0.0)
    lat_weight = jnp.where(pick >= 0.0, lat_weight, 0.0)
    for j in range(CP):
        lon_weight = jnp.where(off == j, 1.0 - fx, 0.0) + jnp.where(off == j - 1.0, fx, 0.0)
        weights_ref[:, j * LAT : (j + 1) * LAT] = lon_weight * lat_weight

    row = lax.broadcasted_iota(jnp.int32, (2 * rows, 1), 0)
    donor = (row & (rows - 1)) >> 1
    match = (owner_k == donor) & (dest_k == tile)
    pick = picks(match, kid, row & 1)
    pick = jnp.where(row // rows == 1 - panel, pick, -8.0).astype(jnp.int32)
    target = ((pick >> (nlon.bit_length() - 1)) << 4) + (pick & 15)
    target = jnp.where(pick >= 0, target, -1)
    lane = lax.broadcasted_iota(jnp.int32, (2 * rows, 128), 1)
    place_ref[...] = jnp.where(lane == target, 1.0, 0.0)


def tables(where, donor_lon, donor_lat, fractions):
    n_ang = donor_lon.shape[1] // CP
    return pl.pallas_call(
        tables_kernel,
        out_shape=(
            jax.ShapeDtypeStruct((2 * n_ang, CP * LAT), F32),
            jax.ShapeDtypeStruct((4 * n_ang, 128), F32),
        ),
        in_specs=[pl.BlockSpec(memory_space=pltpu.SMEM), VMEM, VMEM, VMEM],
        out_specs=(VMEM, VMEM),
        compiler_params=params(),
        cost_estimate=pl.CostEstimate(flops=4_000_000, bytes_accessed=1_000_000, transcendentals=0),
        name="tables",
    )(where, donor_lon, donor_lat, fractions)


def rates(load, count):
    along = [load(f, 0) for f in range(NF)]
    center = [a[:count] for a in along]
    half_u = [0.5 * center[d] for d in range(3)]
    half_b = [0.5 * center[3 + d] for d in range(3)]
    lap, adv, mag = [], [], []
    for f in range(NF):
        wide = along[f]
        up, down = load(f, 1)[:count], load(f, -1)[:count]
        east = pltpu.roll(wide, ROWS - 1, 0)[:count]
        west = pltpu.roll(wide, 1, 0)[:count]
        north = pltpu.roll(center[f], LAT - 1, 1)
        south = pltpu.roll(center[f], 1, 1)
        diffs = [up - down, east - west, north - south]
        lap.append((up + down) + (east + west) + (north + south) - 6.0 * center[f])
        adv.append(half_u[0] * diffs[0] + half_u[1] * diffs[1] + half_u[2] * diffs[2])
        if f < 6:
            mag.append(half_b[0] * diffs[0] + half_b[1] * diffs[1] + half_b[2] * diffs[2])
    return center, lap, adv, mag


def rate_of(f, kappa, buoyancy, center, lap, adv, mag):
    rate = kappa * lap[f] - adv[f]
    if f < 6:
        rate = rate + mag[(f + 3) % 6]
    if f == 0:
        rate = rate + buoyancy * center[6]
    return rate


def interpolate(weights_ref, rows_of):
    field = jnp.concatenate([rows_of(j) for j in range(CP)], axis=1)
    values = lax.dot_general(
        weights_ref[...], field, (((1,), (1,)), ((), ())), precision=HIGHEST, preferred_element_type=F32
    )
    return jnp.concatenate([values, jnp.zeros((values.shape[0], 128 - NPTS), F32)], axis=1)


def send(send_ref, values):
    n = values.shape[0]
    send_ref[0:n, :] = values
    send_ref[n : 2 * n, :] = values


def first_kernel(
    where_ref, state_ref, below_ref, above_ref, coef_ref, rad_below_ref, rad_above_ref, weights_ref,
    first_ref, send_ref, wide_ref,
):
    def at(f, level):
        start = (f * (LV + 4) + level) * ROWS
        return pl.ds(pl.multiple_of(start, 8) if not isinstance(start, int) else start, ROWS)

    for f in range(NF):
        for r in range(LV):
            base = (f * (LV + 4) + r + 2) * ROWS
            wide_ref[base : base + 16, :] = state_ref[0, f, r]
            wide_ref[base + 16 : base + 18, :] = above_ref[0, f, r]
            wide_ref[base + 18 : base + 20, :] = coef_ref[f, r]
            wide_ref[base + 22 : base + 24, :] = below_ref[0, f, r]
        for r in range(2):
            wide_ref[at(f, r), :] = rad_below_ref[0, f, r]
            wide_ref[at(f, LV + 2 + r), :] = rad_above_ref[0, f, r]

    def level(r, carry):
        def load(f, d):
            return wide_ref[at(f, r + 1 + d), :]

        center, lap, adv, mag = rates(load, ROWS)
        buoyancy = center[0][19:20]
        for f in range(NF):
            rate = rate_of(f, center[f][18:19], buoyancy, center, lap, adv, mag)
            start = pl.multiple_of((f * (LV + 2) + r) * ROWS, 8)
            first_ref[pl.ds(start, ROWS), :] = center[f] + step_size * rate
        return carry

    lax.fori_loop(0, LV + 2, level, 0)

    rad, ang = where_ref[1], where_ref[2]
    n_rad, n_ang = where_ref[3], where_ref[4]

    @pl.when(rad == 0)
    def _():
        for f in range(NF):
            first_ref[f * (LV + 2) * ROWS : (f * (LV + 2) + 1) * ROWS, :] = jnp.zeros((ROWS, LAT), F32)

    @pl.when(rad == n_rad - 1)
    def _():
        for f in range(NF):
            start = (f * (LV + 2) + LV + 1) * ROWS
            first_ref[start : start + ROWS, :] = jnp.zeros((ROWS, LAT), F32)

    def blank(row):
        for i in range(NF * (LV + 2)):
            first_ref[i * ROWS + row : i * ROWS + row + 1, :] = jnp.zeros((1, LAT), F32)

    @pl.when(ang == 0)
    def _():
        blank(ROWS - 1)

    @pl.when(ang == n_ang - 1)
    def _():
        blank(CP)

    def rows_of(j):
        return jnp.concatenate(
            [first_ref[pl.ds((f * (LV + 2) + 1) * ROWS + j, LV, ROWS), :] for f in range(NF)], axis=0
        )

    send(send_ref, interpolate(weights_ref, rows_of))


def received(place_ref, recv_ref):
    return lax.dot_general(
        place_ref[...], recv_ref[...], (((0,), (0,)), ((), ())), precision=HIGHEST, preferred_element_type=F32
    )


def with_rows(own, values, point, lane):
    low = jnp.broadcast_to(values[0:CP, point : point + 1], (CP, LAT))
    high = jnp.broadcast_to(values[CP : 2 * CP, point : point + 1], (CP, LAT))
    return jnp.where(lane == 0, low, jnp.where(lane == LAT - 1, high, own))


def second_kernel(state_ref, first_ref, coef_ref, recv_ref, place_ref, weights_ref, next_ref, send_ref, work_ref):
    values = received(place_ref, recv_ref)
    lane = lax.broadcasted_iota(jnp.int32, (CP, LAT), 1)
    for f in range(NF):
        for r in range(LV + 2):
            base = (f * (LV + 2) + r) * ROWS
            if 1 <= r <= LV:
                work_ref[base : base + CP, :] = with_rows(
                    first_ref[base : base + CP, :], values, f * LV + r - 1, lane
                )
                work_ref[base + CP : base + ROWS, :] = first_ref[base + CP : base + ROWS, :]
            else:
                work_ref[base : base + ROWS, :] = first_ref[base : base + ROWS, :]

    def level(r, carry):
        def load(f, d):
            start = (f * (LV + 2) + r + 1 + d) * ROWS
            return work_ref[pl.ds(pl.multiple_of(start, 8), ROWS), :]

        center, lap, adv, mag = rates(load, CP)
        buoyancy = coef_ref[0, r, 1:2, :]
        for f in range(NF):
            rate = rate_of(f, coef_ref[f, r, 0:1, :], buoyancy, center, lap, adv, mag)
            start = pl.multiple_of((f * LV + r) * CP, 8)
            next_ref[pl.ds(start, CP), :] = 0.5 * (state_ref[0, f, r] + center[f] + step_size * rate)
        return carry

    lax.fori_loop(0, LV, level, 0)
    send(send_ref, interpolate(weights_ref, lambda j: next_ref[pl.ds(j, NPTS, CP), :]))


def last_kernel(next_ref, recv_ref, place_ref, out_ref):
    values = received(place_ref, recv_ref)
    lane = lax.broadcasted_iota(jnp.int32, (CP, LAT), 1)
    for f in range(NF):
        for r in range(LV):
            base = (f * LV + r) * CP
            out_ref[0, f, r] = with_rows(next_ref[base : base + CP, :], values, f * LV + r, lane)


def shift(value, axis, step):
    count = lax.axis_size(axis)
    pairs = [(i, i + step) for i in range(count) if 0 <= i + step < count]
    return lax.ppermute(value, axis, pairs)


def exchange(values):
    n = values.shape[0] // 2
    got = lax.all_to_all(values.reshape(n, 2, 128), ("panel", "ang"), 0, 0, tiled=True)
    return got.reshape(2 * n, 128)


def body(state, kappa, buoyancy, donor_lon, donor_lat, fractions):
    where = jnp.stack(
        [lax.axis_index(a) for a in ("panel", "rad", "ang")] + [lax.axis_size(a) for a in ("rad", "ang")]
    ).astype(jnp.int32)

    below = shift(state[:, :, :, CP - 2 :], "ang", 1)
    above = shift(state[:, :, :, :2], "ang", -1)
    coef = jnp.stack(
        [
            jnp.broadcast_to(kappa[:, :, None], (NF, LV, LAT)),
            jnp.broadcast_to(buoyancy[None, :, None], (NF, LV, LAT)),
        ],
        axis=2,
    )

    def levels(low):
        part = slice(low, low + 2)
        return jnp.concatenate(
            [
                state[:, :, part],
                above[:, :, part],
                coef[None, :, part],
                jnp.zeros((1, NF, 2, 2, LAT), F32),
                below[:, :, part],
            ],
            axis=3,
        )

    rad_below = shift(levels(LV - 2), "rad", 1)
    rad_above = shift(levels(0), "rad", -1)
    weights, place = tables(where, donor_lon, donor_lat, fractions)
    n_send = 2 * weights.shape[0]
    smem = pl.BlockSpec(memory_space=pltpu.SMEM)

    first, out = pl.pallas_call(
        first_kernel,
        out_shape=(
            jax.ShapeDtypeStruct((NF * (LV + 2) * ROWS, LAT), F32),
            jax.ShapeDtypeStruct((n_send, 128), F32),
        ),
        in_specs=[smem] + [VMEM] * 7,
        out_specs=(VMEM, VMEM),
        scratch_shapes=[pltpu.VMEM((NF * (LV + 4) * ROWS, LAT), F32)],
        compiler_params=params(),
        name="first",
    )(where, state, below, above, coef, rad_below, rad_above, weights)
    got = exchange(out)
    following, out = pl.pallas_call(
        second_kernel,
        out_shape=(
            jax.ShapeDtypeStruct((NPTS * CP, LAT), F32),
            jax.ShapeDtypeStruct((n_send, 128), F32),
        ),
        in_specs=[VMEM] * 6,
        out_specs=(VMEM, VMEM),
        scratch_shapes=[pltpu.VMEM((NF * (LV + 2) * ROWS, LAT), F32)],
        compiler_params=params(),
        name="second",
    )(state, first, coef, got, place, weights)
    got = exchange(out)
    return pl.pallas_call(
        last_kernel,
        out_shape=jax.ShapeDtypeStruct(state.shape, F32),
        in_specs=[VMEM] * 3,
        out_specs=VMEM,
        compiler_params=params(),
        name="last",
    )(following, got, place)


def solution(mesh):
    return jax.shard_map(
        body,
        mesh=mesh,
        in_specs=(P("panel", None, "rad", "ang", None), P(None, "rad"), P("rad"), P(), P(), P()),
        out_specs=P("panel", None, "rad", "ang", None),
        check_vma=False,
    )
```

time: 577 us -> 71.7 us (0.12)
  the two profiles are of different devices: /device:TPU:64 before, /device:TPU:193 now
where the time goes in v1:
time: 71.7 us; the launch traced here: 71.4 us
  blocking collectives  36.8 us (51%)
  starting transfers between devices  12.8 us (18%)
  Pallas kernels  11.1 us (15%)
  waiting for transfers between devices  6.28 us (9%)
  local copies, waits for them, and re-layouts  4.16 us (6%)
    all_to_all x2, blocking collectives, exchange(): lax.all_to_all(values.reshape(n, 2, 128), ('panel', 'ang'), 0, 0, tiled=T...  36.8 us
    ppermute x4, starting transfers between devices, shift(): return lax.ppermute(value, axis, pairs)  12.8 us
    ppermute x4, waiting for transfers between devices, shift(): return lax.ppermute(value, axis, pairs)  6.28 us
    pallas_call x1, Pallas kernels, body(): pl.pallas_call(first_kernel, out_shape=(jax.ShapeDtypeStruct((NF * (LV +...  4.16 us
    pallas_call x1, Pallas kernels, body(): pl.pallas_call(second_kernel, out_shape=(jax.ShapeDtypeStruct((NPTS * CP,...  3.96 us
    pallas_call x1, Pallas kernels, body(): pl.pallas_call(last_kernel, out_shape=jax.ShapeDtypeStruct(state.shape, F...  1.94 us
    another operation x2, local copies, waits for them, and re-layouts, body(): jnp.stack([jnp.broadcast_to(kappa[:, :, None], (NF, LV, LAT)), jnp.broadc...  1.61 us
  transfers between devices with their start and end apart: 4, of which 2 were waited for; matrix products, arithmetic and copies ran while one was open for 4% of the time, Pallas kernels for 1%

profile of v1, /device:TPU:193, one launch (start us, length us, event | category | flops | bytes accessed | tf_op | source)
XLA Modules:
  0.0 71.4 jit_solution(4878973386284129931)
XLA Ops:
  0.0 0.0 copy-start
  0.0 0.0 copy-start.1
  0.0 0.0 copy-start.3
  0.0 0.0 copy-start.2
  0.0 1.3 %fusion.5 = (f32[1,7,16,2,128]{4,3,2,1,0:T(2,128)S(1)}, f32[1,7,16,2,128]{4,3,2,1,0:T(2,128)S(1)}) fusion(f32[1,7,16,16,128]{4,3,2,1,0:T(8,128)} %state_ref.3), kind=kLoop, calls=%fused_computation.10 | loop fusion | bytes 458752 | tf_op jit(solution)/shard_map/slice | solution.py:279
  1.3 2.6 %collective-permute-start.1 = (f32[1,7,16,2,128]{4,3,2,1,0:T(2,128)S(1)}, f32[1,7,16,2,128]{4,3,2,1,0:T(2,128)S(1)}, u32[]{:S(2)}, u32[]{:S(2)}) collective-permute-start(f32[1,7,16,2,128]{4,3,2,1,0:T(2,128)S(1)} %get-tuple-element.19), channel_id=1, source_target_pairs={{1,0},{2,1},{3,2},{4,3},{5,4},{6,5},{7,6},{8,7},{9,8},{10,9},{11,1... | collective-permute-start | bytes 344072 | tf_op jit(solution)/shard_map/ppermute | solution.py:264
  3.9 3.1 %collective-permute-start = (f32[1,7,16,2,128]{4,3,2,1,0:T(2,128)S(1)}, f32[1,7,16,2,128]{4,3,2,1,0:T(2,128)S(1)}, u32[]{:S(2)}, u32[]{:S(2)}) collective-permute-start(f32[1,7,16,2,128]{4,3,2,1,0:T(2,128)S(1)} %get-tuple-element.20), channel_id=1, source_target_pairs={{0,1},{1,2},{2,3},{3,4},{4,5},{5,6},{6,7},{7,8},{8,9},{9,10},{10,1... | collective-permute-start | bytes 344072 | tf_op jit(solution)/shard_map/ppermute | solution.py:264
  7.0 1.0 %fusion.4 = (f32[1,7,2,16,128]{4,3,2,1,0:T(8,128)S(1)}, f32[1,7,2,16,128]{4,3,2,1,0:T(8,128)S(1)}) fusion(f32[1,7,16,16,128]{4,3,2,1,0:T(8,128)} %state_ref.3), kind=kLoop, calls=%fused_computation.9 | loop fusion | bytes 458752 | tf_op jit(solution)/shard_map/slice | solution.py:292
  8.0 0.9 %stack_broadcast_in_dim.4 = f32[7,16,1,128]{3,2,1,0:T(1,128)S(1)} broadcast(f32[7,16]{1,0:T(8,128)} %param.7), dimensions={0,1} | broadcast | bytes 57792 | tf_op jit(solution)/shard_map/stack;broadcast_in_dim | solution.py:280
  8.9 0.8 %stack_broadcast_in_dim.5 = f32[7,16,1,128]{3,2,1,0:T(1,128)S(1)} broadcast(f32[16]{0:T(128)} %param.8), dimensions={1} | broadcast | bytes 57408 | tf_op jit(solution)/shard_map/stack;broadcast_in_dim | solution.py:280
  9.7 0.0 collective-permute-done.1.above_ref
  9.7 0.0 collective-permute-done.below_ref
  9.8 0.1 concatenate.6
  9.8 5.2 %collective-permute-start.2 = (f32[1,7,2,24,128]{4,3,2,1,0:T(8,128)S(1)}, f32[1,7,2,24,128]{4,3,2,1,0:T(8,128)S(1)}, u32[]{:S(2)}, u32[]{:S(2)}) collective-permute-start(f32[1,7,2,24,128]{4,3,2,1,0:T(8,128)S(1)} %concatenate.6), channel_id=1, source_target_pairs={{0,32},{32,64},{64,96},{96,128},{128,160},{160,192},{192,224},{224... | collective-permute-start | bytes 516104 | tf_op jit(solution)/shard_map/ppermute | solution.py:264
  15.0 0.1 concatenate.7
  15.1 1.9 %collective-permute-start.3 = (f32[1,7,2,24,128]{4,3,2,1,0:T(8,128)S(1)}, f32[1,7,2,24,128]{4,3,2,1,0:T(8,128)S(1)}, u32[]{:S(2)}, u32[]{:S(2)}) collective-permute-start(f32[1,7,2,24,128]{4,3,2,1,0:T(8,128)S(1)} %concatenate.7), channel_id=1, source_target_pairs={{32,0},{64,32},{96,64},{128,96},{160,128},{192,160},{224,192},{256... | collective-permute-start | bytes 516104 | tf_op jit(solution)/shard_map/ppermute | solution.py:264
  17.1 0.1 stack.18.where_ref
  17.1 0.0 copy-done.1
  17.1 0.0 copy-done.3
  17.1 0.0 copy-done.2
  17.1 1.0 %tables.1 = (f32[64,2048]{1,0:T(8,128)S(1)}, f32[128,128]{1,0:T(8,128)S(1)}) custom-call(s32[5]{0:T(128)S(1)} %stack.18.where_ref, s32[2,512]{1,0:T(2,128)S(1)} %copy-done.2, s32[2,512]{1,0:T(2,128)S(1)} %copy-done.3, f32[2,2,512]{2,1,0:T(2,128)S(1)} %copy-done.1), custom_call_target="tpu_custom_call" | custom-call | flops 4000000 | bytes 1000000 | tf_op jit(solution)/shard_map/tables/pallas_call | solution.py:84
  18.2 0.1 pad_maximum_fusion.coef_ref
  18.3 0.7 %collective-permute-done.2.rad_below_ref = f32[1,7,2,24,128]{4,3,2,1,0:T(8,128)S(1)} collective-permute-done((f32[1,7,2,24,128]{4,3,2,1,0:T(8,128)S(1)}, f32[1,7,2,24,128]{4,3,2,1,0:T(8,128)S(1)}, u32[]{:S(2)}, u32[]{:S(2)}) %collective-permute-start.2) | collective-permute-done | bytes 172064 | tf_op jit(solution)/shard_map/ppermute | solution.py:264
  19.0 5.6 %collective-permute-done.3.rad_above_ref = f32[1,7,2,24,128]{4,3,2,1,0:T(8,128)S(1)} collective-permute-done((f32[1,7,2,24,128]{4,3,2,1,0:T(8,128)S(1)}, f32[1,7,2,24,128]{4,3,2,1,0:T(8,128)S(1)}, u32[]{:S(2)}, u32[]{:S(2)}) %collective-permute-start.3) | collective-permute-done | bytes 172064 | tf_op jit(solution)/shard_map/ppermute | solution.py:264
  24.5 0.0 copy-done
  24.6 4.2 %first.1 = (f32[3024,128]{1,0:T(8,128)S(1)}, f32[128,128]{1,0:T(8,128)S(1)}) custom-call(s32[5]{0:T(128)S(1)} %stack.18.where_ref, f32[1,7,16,16,128]{4,3,2,1,0:T(8,128)S(1)} %copy-done, f32[1,7,16,2,128]{4,3,2,1,0:T(2,128)S(1)} %collective-permute-done.below_ref, f32[1,7,16,2,128]{4,3,2,1,0:T(2,128)S(1)} %collective-permute-done.1.above_ref, ...), custom_call_target="tpu_custom_call" | custom-call | tf_op jit(solution)/shard_map/first/pallas_call | solution.py:307
  28.7 22.8 %all_to_all.10 = f32[64,2,128]{2,1,0:T(2,128)S(1)} all-to-all(f32[64,2,128]{2,1,0:T(2,128)S(1)} %bitcast.13), channel_id=1, replica_groups=mesh['panel'=2,'rad'=12,'ang'=32] {'panel','ang'}, dimensions={0} | all-to-all | bytes 131072 | tf_op jit(solution)/shard_map/all_to_all | solution.py:269
  51.5 4.0 %second.1 = (f32[1792,128]{1,0:T(8,128)S(1)}, f32[128,128]{1,0:T(8,128)S(1)}) custom-call(f32[1,7,16,16,128]{4,3,2,1,0:T(8,128)S(1)} %copy-done, f32[3024,128]{1,0:T(8,128)S(1)} %get-tuple-element.12.first_ref, f32[7,16,2,128]{3,2,1,0:T(2,128)S(1)} %pad_maximum_fusion.coef_ref, f32[128,128]{1,0:T(8,128)S(1)} %bitcast.11, ...), custom_call_target="tpu_custom_call" | custom-call | tf_op jit(solution)/shard_map/second/pallas_call | solution.py:320
  55.5 14.0 %all_to_all.11 = f32[64,2,128]{2,1,0:T(2,128)S(1)} all-to-all(f32[64,2,128]{2,1,0:T(2,128)S(1)} %bitcast.14), channel_id=1, replica_groups=mesh['panel'=2,'rad'=12,'ang'=32] {'panel','ang'}, dimensions={0} | all-to-all | bytes 131072 | tf_op jit(solution)/shard_map/all_to_all | solution.py:269
  69.5 1.9 %last.1 = f32[1,7,16,16,128]{4,3,2,1,0:T(8,128)} custom-call(f32[1792,128]{1,0:T(8,128)S(1)} %get-tuple-element.15.next_ref, f32[128,128]{1,0:T(8,128)S(1)} %bitcast.12, f32[128,128]{1,0:T(8,128)S(1)} %get-tuple-element.14.place_ref), custom_call_target="tpu_custom_call" | custom-call | tf_op jit(solution)/shard_map/last/pallas_call | solution.py:333
  (4 shorter events, 0.1 us)
Async XLA Ops:
  0.0 24.6 %copy-start = (f32[1,7,16,16,128]{4,3,2,1,0:T(8,128)S(1)}, f32[1,7,16,16,128]{4,3,2,1,0:T(8,128)}, u32[]{:S(2)}) copy-start(f32[1,7,16,16,128]{4,3,2,1,0:T(8,128)} %state_ref.3) | copy-start | bytes 2752516
  0.0 17.1 %copy-start.1 = (f32[2,2,512]{2,1,0:T(2,128)S(1)}, f32[2,2,512]{2,1,0:T(2,128)}, u32[]{:S(2)}) copy-start(f32[2,2,512]{2,1,0:T(2,128)} %frac_ref.1) | copy-start | bytes 24580
  0.0 17.1 %copy-start.3 = (s32[2,512]{1,0:T(2,128)S(1)}, s32[2,512]{1,0:T(2,128)}, u32[]{:S(2)}) copy-start(s32[2,512]{1,0:T(2,128)} %lat_ref.1) | copy-start | bytes 12292
  0.0 17.1 %copy-start.2 = (s32[2,512]{1,0:T(2,128)S(1)}, s32[2,512]{1,0:T(2,128)}, u32[]{:S(2)}) copy-start(s32[2,512]{1,0:T(2,128)} %lon_ref.1) | copy-start | bytes 12292
  1.3 8.4 %collective-permute-start.1 = (f32[1,7,16,2,128]{4,3,2,1,0:T(2,128)S(1)}, f32[1,7,16,2,128]{4,3,2,1,0:T(2,128)S(1)}, u32[]{:S(2)}, u32[]{:S(2)}) collective-permute-start(f32[1,7,16,2,128]{4,3,2,1,0:T(2,128)S(1)} %get-tuple-element.19), channel_id=1, source_target_pairs={{1,0},{2,1},{3,2},{4,3},{5,4},{6,5},{7,6},{8,7},{9,8},{10,9},{11,1... | collective-permute-start | bytes 344072 | tf_op jit(solution)/shard_map/ppermute | solution.py:264
  3.9 5.8 %collective-permute-start = (f32[1,7,16,2,128]{4,3,2,1,0:T(2,128)S(1)}, f32[1,7,16,2,128]{4,3,2,1,0:T(2,128)S(1)}, u32[]{:S(2)}, u32[]{:S(2)}) collective-permute-start(f32[1,7,16,2,128]{4,3,2,1,0:T(2,128)S(1)} %get-tuple-element.20), channel_id=1, source_target_pairs={{0,1},{1,2},{2,3},{3,4},{4,5},{5,6},{6,7},{7,8},{8,9},{9,10},{10,1... | collective-permute-start | bytes 344072 | tf_op jit(solution)/shard_map/ppermute | solution.py:264
  9.8 9.2 %collective-permute-start.2 = (f32[1,7,2,24,128]{4,3,2,1,0:T(8,128)S(1)}, f32[1,7,2,24,128]{4,3,2,1,0:T(8,128)S(1)}, u32[]{:S(2)}, u32[]{:S(2)}) collective-permute-start(f32[1,7,2,24,128]{4,3,2,1,0:T(8,128)S(1)} %concatenate.6), channel_id=1, source_target_pairs={{0,32},{32,64},{64,96},{96,128},{128,160},{160,192},{192,224},{224... | collective-permute-start | bytes 516104 | tf_op jit(solution)/shard_map/ppermute | solution.py:264
  15.1 9.4 %collective-permute-start.3 = (f32[1,7,2,24,128]{4,3,2,1,0:T(8,128)S(1)}, f32[1,7,2,24,128]{4,3,2,1,0:T(8,128)S(1)}, u32[]{:S(2)}, u32[]{:S(2)}) collective-permute-start(f32[1,7,2,24,128]{4,3,2,1,0:T(8,128)S(1)} %concatenate.7), channel_id=1, source_target_pairs={{32,0},{64,32},{96,64},{128,96},{160,128},{192,160},{224,192},{256... | collective-permute-start | bytes 516104 | tf_op jit(solution)/shard_map/ppermute | solution.py:264

commit v2 on v0

v2 whole, which is shorter than its diff:
```python
import jax
import jax.numpy as jnp
from jax import lax
from jax.experimental import pallas as pl
from jax.experimental.pallas import tpu as pltpu
from jax.sharding import PartitionSpec as P

step_size = 0.1
HIGHEST = lax.Precision.HIGHEST
VMEM = pl.BlockSpec(memory_space=pltpu.VMEM)
SMEM = pl.BlockSpec(memory_space=pltpu.SMEM)
F32 = jnp.float32

NF = 7
LV = 16
CP = 16
LAT = 128
TILE = LV * CP
BLOCK = 24
MESSAGE = 40


def params():
    return pltpu.CompilerParams(vmem_limit_bytes=40 * 1024 * 1024)


def cost(flops):
    return pl.CostEstimate(flops=flops, bytes_accessed=2_000_000, transcendentals=0)


def shape(*dims):
    return jax.ShapeDtypeStruct(dims, F32)


def picks(match, kid, slot):
    low = jnp.min(jnp.where(match, kid, 4096.0), axis=1, keepdims=True)
    high = jnp.max(jnp.where(match, kid, -1.0), axis=1, keepdims=True)
    low_or_none = jnp.where(low < 4096.0, low, -8.0)
    high_or_none = jnp.where(high > low, high, -8.0)
    return jnp.where(slot == 0, low_or_none, high_or_none)


def tables_kernel(where_ref, lon_ref, lat_ref, frac_ref, lat_weight_ref, lon_weight_ref, place_ref):
    nlon = lon_ref.shape[1]
    half = 2 * nlon // CP
    points = 2 * nlon
    panel = where_ref[0]
    tile = where_ref[2]

    def flat(low, high):
        return jnp.concatenate([low, high], axis=1)

    lon_k = flat(lon_ref[0:1, :], lon_ref[1:2, :])
    owner_k = lon_k >> 4
    off_k = (lon_k & 15).astype(F32)
    lat_k = flat(lat_ref[0:1, :], lat_ref[1:2, :]).astype(F32)
    fx_k = flat(frac_ref[0, 0:1, :], frac_ref[0, 1:2, :])
    fy_k = flat(frac_ref[1, 0:1, :], frac_ref[1, 1:2, :])

    kid = lax.broadcasted_iota(jnp.int32, (1, points), 1)
    dest_k = (kid & (nlon - 1)) >> 4
    kid = kid.astype(F32)

    row = lax.broadcasted_iota(jnp.int32, (half, 1), 0)
    match = (dest_k == (row >> 1)) & (owner_k == tile)
    pick = picks(match, kid, row & 1)
    chosen = kid == pick

    def of(value):
        return jnp.sum(jnp.where(chosen, value, 0.0), axis=1, keepdims=True)

    off, lat, fx, fy = of(off_k), of(lat_k), of(fx_k), of(fy_k)
    lane = lax.broadcasted_iota(jnp.int32, (half, LAT), 1).astype(F32)
    lat_weight = jnp.where(lane == lat, 1.0 - fy, 0.0) + jnp.where(lane == lat + 1.0, fy, 0.0)
    lat_weight = jnp.where(pick >= 0.0, lat_weight, 0.0)
    lon_weight = jnp.where(lane == off, 1.0 - fx, 0.0) + jnp.where(lane == off + 1.0, fx, 0.0)
    lat_weight_ref[...] = jnp.transpose(jnp.concatenate([lat_weight, lat_weight], axis=0))
    lon_weight_ref[...] = jnp.transpose(jnp.concatenate([lon_weight, lon_weight], axis=0))[0:CP]

    row = lax.broadcasted_iota(jnp.int32, (half, 1), 0)
    match = (owner_k == (row >> 1)) & (dest_k == tile)
    pick = picks(match, kid, row & 1).astype(jnp.int32)
    target = ((pick >> (nlon.bit_length() - 1)) << 4) + (pick & 15)
    target = jnp.where(pick >= 0, target, -1)
    lane = lax.broadcasted_iota(jnp.int32, (half, 128), 1)
    place = jnp.where(lane == target, 1.0, 0.0)
    place_ref[0:half, :] = place * panel.astype(F32)
    place_ref[half : 2 * half, :] = place * (1 - panel).astype(F32)


def increments(center, neighbours, kappa, buoyancy, scale):
    u = [(0.5 * scale) * center[d] for d in range(3)]
    b = [(0.5 * scale) * center[3 + d] for d in range(3)]
    lap, adv, mag = [], [], []
    for f in range(NF):
        up, down, east, west = neighbours(f)
        north = pltpu.roll(center[f], LAT - 1, 1)
        south = pltpu.roll(center[f], 1, 1)
        diffs = [up - down, east - west, north - south]
        lap.append((scale * kappa(f)) * ((up + down) + (east + west) + (north + south) - 6.0 * center[f]))
        adv.append(u[0] * diffs[0] + u[1] * diffs[1] + u[2] * diffs[2])
        if f < 6:
            mag.append(b[0] * diffs[0] + b[1] * diffs[1] + b[2] * diffs[2])
    rates = [lap[f] - adv[f] + mag[(f + 3) % 6] for f in range(6)] + [lap[6] - adv[6]]
    rates[0] = rates[0] + (scale * buoyancy) * center[6]
    return rates


def interpolate(rows, lat_weight_ref, lon_weight_ref):
    along = jnp.dot(rows, lat_weight_ref[...], precision=HIGHEST, preferred_element_type=F32)
    n = rows.shape[0] // CP
    return jnp.sum(along.reshape(n, CP, along.shape[1]) * lon_weight_ref[...][None], axis=1)


def pack_kernel(state_ref, below_ref, above_ref, coef_ref, up_ref, down_ref):
    for ref, near, far in ((up_ref, LV - 1, LV - 2), (down_ref, 0, 1)):
        for f in range(NF):
            start = f * TILE
            ref[f, 0:CP, :] = state_ref[start + near * CP : start + (near + 1) * CP, :]
            ref[f, CP : 2 * CP, :] = state_ref[start + far * CP : start + (far + 1) * CP, :]
            ref[f, 32:33, :] = above_ref[0, f, near : near + 1, :]
            ref[f, 33:34, :] = below_ref[1, f, near : near + 1, :]
            ref[f, 34:35, :] = coef_ref[f, near : near + 1, :]
            ref[f, 35:36, :] = coef_ref[NF, near : near + 1, :]
            ref[f, 36:40, :] = jnp.zeros((4, LAT), F32)


def first_a_kernel(
    state_ref, below_ref, above_ref, coef_ref, lat_weight_ref, lon_weight_ref, inner_ref, values_ref, line_ref
):
    for f in range(NF):
        for r in range(LV):
            base = (f * LV + r) * BLOCK + 8
            line_ref[base : base + CP, :] = state_ref[f * TILE + r * CP : f * TILE + (r + 1) * CP, :]
        line_ref[pl.ds(f * LV * BLOCK + 7, LV, BLOCK), :] = below_ref[1, f]
        line_ref[pl.ds(f * LV * BLOCK + 24, LV, BLOCK), :] = above_ref[0, f]
        for r in (0, LV - 1):
            inner_ref[f * TILE + r * CP : f * TILE + (r + 1) * CP, :] = jnp.zeros((CP, LAT), F32)
    for r in range(1, LV - 1):
        for t in range(2):

            def row(f, level=r):
                return f * TILE + level * CP + 8 * t

            def neighbours(f):
                line = (f * LV + r) * BLOCK + 8 + 8 * t
                return (
                    state_ref[row(f, r + 1) : row(f, r + 1) + 8, :],
                    state_ref[row(f, r - 1) : row(f, r - 1) + 8, :],
                    line_ref[line + 1 : line + 9, :],
                    line_ref[line - 1 : line + 7, :],
                )

            center = [state_ref[row(f) : row(f) + 8, :] for f in range(NF)]
            rates = increments(
                center, neighbours, lambda f: coef_ref[f, r : r + 1, :], coef_ref[NF, r : r + 1, :], step_size
            )
            for f in range(NF):
                inner_ref[row(f) : row(f) + 8, :] = center[f] + rates[f]
    values_ref[...] = interpolate(inner_ref[...], lat_weight_ref, lon_weight_ref)


def first_b_kernel(
    where_ref, state_ref, below_ref, above_ref, coef_ref, rad_below_ref, rad_above_ref, lat_weight_ref,
    lon_weight_ref, values_ref, edge_ref, ring_ref, send_ref, line_ref, column_ref,
):
    rad, ang, n_rad, n_ang = where_ref[1], where_ref[2], where_ref[3], where_ref[4]
    keep_rad = [jnp.where(rad == 0, 0.0, 1.0), jnp.where(rad == n_rad - 1, 0.0, 1.0)]
    keep_ang = [jnp.where(ang == 0, 0.0, 1.0), jnp.where(ang == n_ang - 1, 0.0, 1.0)]
    radial = (rad_below_ref, rad_above_ref)

    for f in range(NF):
        for e, r in ((1, 0), (2, LV - 1)):
            base = (e * NF + f) * BLOCK + 8
            line_ref[base : base + CP, :] = state_ref[f * TILE + r * CP : f * TILE + (r + 1) * CP, :]
            line_ref[base - 1 : base, :] = below_ref[1, f, r : r + 1, :]
            line_ref[base + CP : base + CP + 1, :] = above_ref[0, f, r : r + 1, :]
        for e, ref in ((0, rad_below_ref), (3, rad_above_ref)):
            base = (e * NF + f) * BLOCK + 8
            line_ref[base : base + CP, :] = ref[f, 0:CP, :]
            line_ref[base - 1 : base, :] = ref[f, 33:34, :]
            line_ref[base + CP : base + CP + 1, :] = ref[f, 32:33, :]
        for side, ref in ((0, below_ref.at[1]), (1, above_ref.at[0])):
            base = (side * NF + f) * BLOCK + 8
            column_ref[base : base + LV, :] = ref[f]
            column_ref[base - 1 : base, :] = rad_below_ref[f, 33 - side : 34 - side, :]
            column_ref[base + LV : base + LV + 1, :] = rad_above_ref[f, 33 - side : 34 - side, :]

    for e in range(4):
        for t in range(2):
            part = slice(8 * t, 8 * t + 8)

            def own(f, r):
                return state_ref[f * TILE + r * CP + 8 * t : f * TILE + r * CP + 8 * t + 8, :]

            def neighbours(f):
                line = (e * NF + f) * BLOCK + 8 + 8 * t
                if e == 0:
                    up, down = own(f, 0), rad_below_ref[f, CP + 8 * t : CP + 8 * t + 8, :]
                elif e == 1:
                    up, down = own(f, 1), rad_below_ref[f, part, :]
                elif e == 2:
                    up, down = rad_above_ref[f, part, :], own(f, LV - 2)
                else:
                    up, down = rad_above_ref[f, CP + 8 * t : CP + 8 * t + 8, :], own(f, LV - 1)
                return up, down, line_ref[line + 1 : line + 9, :], line_ref[line - 1 : line + 7, :]

            center = [line_ref[(e * NF + f) * BLOCK + 8 + 8 * t : (e * NF + f) * BLOCK + 16 + 8 * t, :] for f in range(NF)]
            if e in (0, 3):
                source = radial[e // 3]
                rates = increments(center, neighbours, lambda f: source[f, 34:35, :], source[0, 35:36, :], step_size)
            else:
                r = (e - 1) * (LV - 1)
                rates = increments(
                    center, neighbours, lambda f: coef_ref[f, r : r + 1, :], coef_ref[NF, r : r + 1, :], step_size
                )
            for f in range(NF):
                value = center[f] + rates[f]
                if e in (0, 3):
                    value = keep_rad[e // 3] * value
                base = (e * 8 + f) * CP + 8 * t
                edge_ref[base : base + 8, :] = value
        edge_ref[(e * 8 + NF) * CP : (e * 8 + 8) * CP, :] = jnp.zeros((CP, LAT), F32)

    for side in range(2):
        for t in range(2):
            part = slice(8 * t, 8 * t + 8)

            def neighbours(f):
                column = (side * NF + f) * BLOCK + 8 + 8 * t
                near = state_ref[pl.ds(f * TILE + 8 * t * CP + side * (CP - 1), 8, CP), :]
                if side == 0:
                    east, west = near, below_ref[0, f, part, :]
                else:
                    east, west = above_ref[1, f, part, :], near
                return column_ref[column + 1 : column + 9, :], column_ref[column - 1 : column + 7, :], east, west

            center = [(below_ref[1, f, part, :] if side == 0 else above_ref[0, f, part, :]) for f in range(NF)]
            rates = increments(center, neighbours, lambda f: coef_ref[f, part, :], coef_ref[NF, part, :], step_size)
            for f in range(NF):
                ring_ref[side, f, part, :] = keep_ang[side] * (center[f] + rates[f])

    edges = interpolate(edge_ref[8 * CP : 24 * CP, :], lat_weight_ref, lon_weight_ref)
    send_ref[...] = jnp.transpose(jnp.concatenate([values_ref[...], edges], axis=0))


def received(place_ref, recv_ref):
    values = lax.dot_general(
        place_ref[...], recv_ref[...], (((0,), (0,)), ((), ())), precision=HIGHEST, preferred_element_type=F32
    )
    low, high = values[0:CP], pltpu.roll(values[CP : 2 * CP], LAT - 1, 1)
    even = (lax.broadcasted_iota(jnp.int32, (CP, LAT), 1) & 1) == 0
    return jnp.where(even, low, high), jnp.where(even, high, low)


def with_rows(own, values, point, ends):
    rows = values[point % 2]
    if point:
        rows = pltpu.roll(rows, LAT - point, 1)
    return jnp.where(ends, rows, own)


def ends_of():
    lane = lax.broadcasted_iota(jnp.int32, (CP, LAT), 1)
    return (lane == 0) | (lane == LAT - 1)


def second_kernel(
    state_ref, inner_ref, edge_ref, ring_ref, coef_ref, recv_ref, place_ref, lat_weight_ref, lon_weight_ref,
    next_ref, send_ref, line_ref,
):
    values = received(place_ref, recv_ref)
    ends = ends_of()
    for f in range(NF):
        for r in range(-1, LV + 1):
            base = (f * (LV + 2) + r + 1) * BLOCK + 8
            if 1 <= r <= LV - 2:
                own = inner_ref[f * TILE + r * CP : f * TILE + (r + 1) * CP, :]
                point = f * LV + r
            else:
                e = {-1: 0, 0: 1, LV - 1: 2, LV: 3}[r]
                own = edge_ref[(e * 8 + f) * CP : (e * 8 + f + 1) * CP, :]
                point = NF * LV + (e - 1) * 8 + f
            if 0 <= r <= LV - 1:
                own = with_rows(own, values, point, ends)
            line_ref[base : base + CP, :] = own
        start = (f * (LV + 2) + 1) * BLOCK
        line_ref[pl.ds(start + 7, LV, BLOCK), :] = ring_ref[0, f]
        line_ref[pl.ds(start + 24, LV, BLOCK), :] = ring_ref[1, f]

    for r in range(LV):
        for t in range(2):

            def line(f, level=r):
                return (f * (LV + 2) + level + 1) * BLOCK + 8 + 8 * t

            def neighbours(f):
                return (
                    line_ref[line(f, r + 1) : line(f, r + 1) + 8, :],
                    line_ref[line(f, r - 1) : line(f, r - 1) + 8, :],
                    line_ref[line(f) + 1 : line(f) + 9, :],
                    line_ref[line(f) - 1 : line(f) + 7, :],
                )

            center = [line_ref[line(f) : line(f) + 8, :] for f in range(NF)]
            rates = increments(
                center, neighbours, lambda f: coef_ref[f, r : r + 1, :], coef_ref[NF, r : r + 1, :], 0.5 * step_size
            )
            for f in range(NF):
                row = f * TILE + r * CP + 8 * t
                next_ref[row : row + 8, :] = 0.5 * (state_ref[row : row + 8, :] + center[f]) + rates[f]
    donors = interpolate(next_ref[...], lat_weight_ref, lon_weight_ref)
    send_ref[...] = jnp.transpose(jnp.concatenate([donors, jnp.zeros((128 - NF * LV, 128), F32)], axis=0))


def last_kernel(next_ref, recv_ref, place_ref, out_ref, done_ref, sems):
    values = received(place_ref, recv_ref)
    ends = ends_of()
    copies = []
    for f in range(NF):
        for r in range(LV):
            row = f * TILE + r * CP
            done_ref[row : row + CP, :] = with_rows(next_ref[row : row + CP, :], values, f * LV + r, ends)
        part = pl.ds(f * TILE, TILE)
        copies.append(pltpu.make_async_copy(done_ref.at[part, :], out_ref.at[part, :], sems.at[f]))
        copies[-1].start()
    for copy in copies:
        copy.wait()


def shift(value, axis, step):
    count = lax.axis_size(axis)
    pairs = [(i, i + step) for i in range(count) if 0 <= i + step < count]
    return lax.ppermute(value, axis, pairs)


def exchange(values):
    n = values.shape[0] // 2
    got = lax.all_to_all(values.reshape(n, 2, 128), ("panel", "ang"), 0, 0, tiled=True)
    return got.reshape(2 * n, 128)


def body(state, kappa, buoyancy, donor_lon, donor_lat, fractions):
    where = jnp.stack(
        [lax.axis_index(a) for a in ("panel", "rad", "ang")] + [lax.axis_size(a) for a in ("rad", "ang")]
    ).astype(jnp.int32)

    below = shift(jnp.stack([state[0, :, :, CP - 2], state[0, :, :, CP - 1]]), "ang", 1)
    above = shift(jnp.stack([state[0, :, :, 0], state[0, :, :, 1]]), "ang", -1)
    own = state.reshape(NF * TILE, LAT)

    coef = jnp.broadcast_to(jnp.concatenate([kappa, buoyancy[None]])[:, :, None], (NF + 1, LV, LAT))
    n_send = 4 * donor_lon.shape[1] // CP
    lat_weight, lon_weight, place = pl.pallas_call(
        tables_kernel,
        out_shape=(shape(LAT, n_send), shape(CP, n_send), shape(n_send, 128)),
        in_specs=[SMEM] + [VMEM] * 3,
        out_specs=(VMEM,) * 3,
        compiler_params=params(),
        cost_estimate=cost(4_000_000),
        name="tables",
    )(where, donor_lon, donor_lat, fractions)
    coef, lat_weight = lax.optimization_barrier((coef, lat_weight))

    up, down = pl.pallas_call(
        pack_kernel,
        out_shape=(shape(NF, MESSAGE, LAT),) * 2,
        in_specs=[VMEM] * 4,
        out_specs=(VMEM,) * 2,
        compiler_params=params(),
        name="pack",
    )(own, below, above, coef)
    rad_below = shift(up, "rad", 1)
    rad_above = shift(down, "rad", -1)

    inner, inner_values = pl.pallas_call(
        first_a_kernel,
        out_shape=(shape(NF * TILE, LAT), shape(NF * LV, n_send)),
        in_specs=[VMEM] * 6,
        out_specs=(VMEM,) * 2,
        scratch_shapes=[pltpu.VMEM((NF * LV * BLOCK + 8, LAT), F32)],
        compiler_params=params(),
        cost_estimate=cost(60_000_000),
        name="first_a",
    )(own, below, above, coef, lat_weight, lon_weight)
    edge, ring, out = pl.pallas_call(
        first_b_kernel,
        out_shape=(shape(4 * 8 * CP, LAT), shape(2, NF, LV, LAT), shape(n_send, 128)),
        in_specs=[SMEM] + [VMEM] * 9,
        out_specs=(VMEM,) * 3,
        scratch_shapes=[
            pltpu.VMEM((4 * NF * BLOCK + 8, LAT), F32),
            pltpu.VMEM((2 * NF * BLOCK + 8, LAT), F32),
        ],
        compiler_params=params(),
        name="first_b",
    )(where, own, below, above, coef, rad_below, rad_above, lat_weight, lon_weight, inner_values)
    got = exchange(out)
    following, out = pl.pallas_call(
        second_kernel,
        out_shape=(shape(NF * TILE, LAT), shape(n_send, 128)),
        in_specs=[VMEM] * 9,
        out_specs=(VMEM,) * 2,
        scratch_shapes=[pltpu.VMEM((NF * (LV + 2) * BLOCK + 8, LAT), F32)],
        compiler_params=params(),
        name="second",
    )(own, inner, edge, ring, coef, got, place, lat_weight, lon_weight)
    got = exchange(out)
    result = pl.pallas_call(
        last_kernel,
        out_shape=shape(NF * TILE, LAT),
        in_specs=[VMEM] * 3,
        out_specs=pl.BlockSpec(memory_space=pl.ANY),
        scratch_shapes=[pltpu.VMEM((NF * TILE, LAT), F32), pltpu.SemaphoreType.DMA((NF,))],
        compiler_params=params(),
        name="last",
    )(following, got, place)
    return result.reshape(state.shape)


def solution(mesh):
    return jax.shard_map(
        body,
        mesh=mesh,
        in_specs=(P("panel", None, "rad", "ang", None), P(None, "rad"), P("rad"), P(), P(), P()),
        out_specs=P("panel", None, "rad", "ang", None),
        check_vma=False,
    )
```

time: 577 us -> 66.6 us (0.12)
  the two profiles are of different devices: /device:TPU:64 before, /device:TPU:193 now
where the time goes in v2:
time: 66.6 us; the launch traced here: 66.2 us
  blocking collectives  36.8 us (55%)
  starting transfers between devices  12.8 us (19%)
  Pallas kernels  7.87 us (12%)
  waiting for transfers between devices  5.4 us (8%)
  local copies, waits for them, and re-layouts  3.12 us (5%)
    all_to_all x2, blocking collectives, exchange(): lax.all_to_all(values.reshape(n, 2, 128), ('panel', 'ang'), 0, 0, tiled=T...  36.8 us
    ppermute x4, starting transfers between devices, shift(): return lax.ppermute(value, axis, pairs)  12.8 us
    ppermute x4, waiting for transfers between devices, shift(): return lax.ppermute(value, axis, pairs)  5.4 us
    pallas_call x1, Pallas kernels, body(): pl.pallas_call(second_kernel, out_shape=(shape(NF * TILE, LAT), shape(n_s...  2.6 us
    slice x1, local copies, waits for them, and re-layouts, body(): above = shift(jnp.stack([state[0, :, :, 0], state[0, :, :, 1]]), 'ang', -1)  1.7 us
    pallas_call x1, Pallas kernels, body(): pl.pallas_call(first_a_kernel, out_shape=(shape(NF * TILE, LAT), shape(NF...  1.65 us
    pallas_call x1, Pallas kernels, body(): pl.pallas_call(last_kernel, out_shape=shape(NF * TILE, LAT), in_specs=[VM...  1.61 us
  transfers between devices with their start and end apart: 4, of which 2 were waited for; matrix products, arithmetic and copies ran while one was open for 0% of the time, Pallas kernels for 4%

profile of v2, /device:TPU:193, one launch (start us, length us, event | category | flops | bytes accessed | tf_op | source)
XLA Modules:
  0.0 66.2 jit_solution(9526655233880550725)
XLA Ops:
  0.0 0.0 copy-start
  0.0 1.7 %fusion = (f32[1,7,16,1,128]{4,3,2,1,0:T(1,128)S(1)}, f32[1,7,16,1,128]{4,3,2,1,0:T(1,128)S(1)}, f32[1,7,16,1,128]{4,3,2,1,0:T(1,128)S(1)}, f32[1,7,16,1,128]{4,3,2,1,0:T(1,128)S(1)}) fusion(f32[1,7,16,16,128]{4,3,2,1,0:T(8,128)} %param.6), kind=kLoop, calls=%fused_computation.3 | loop fusion | bytes 458752 | tf_op jit(solution)/shard_map/slice | solution.py:349
  1.7 3.8 %collective-permute-start = (f32[2,7,16,128]{3,2,1,0:T(8,128)S(1)}, f32[2,7,16,128]{3,2,1,0:T(8,128)S(1)}, u32[]{:S(2)}, u32[]{:S(2)}) collective-permute-start(f32[2,7,16,128]{3,2,1,0:T(8,128)S(1)} %pad_maximum_fusion), channel_id=1, source_target_pairs={{0,1},{1,2},{2,3},{3,4},{4,5},{5,6},{6,7},{7,8},{8,9},{9,10},{10,1... | collective-permute-start | bytes 344072 | tf_op jit(solution)/shard_map/ppermute | solution.py:334
  5.5 1.9 %collective-permute-start.1 = (f32[2,7,16,128]{3,2,1,0:T(8,128)S(1)}, f32[2,7,16,128]{3,2,1,0:T(8,128)S(1)}, u32[]{:S(2)}, u32[]{:S(2)}) collective-permute-start(f32[2,7,16,128]{3,2,1,0:T(8,128)S(1)} %pad_maximum_fusion.1), channel_id=1, source_target_pairs={{1,0},{2,1},{3,2},{4,3},{5,4},{6,5},{7,6},{8,7},{9,8},{10,9},{11,1... | collective-permute-start | bytes 344072 | tf_op jit(solution)/shard_map/ppermute | solution.py:334
  7.5 0.0 copy-start.1
  7.5 0.0 copy-start.2
  7.5 0.0 copy-start.3
  7.5 0.1 stack.23.where_ref
  7.6 0.6 copy-done.1
  8.2 0.0 copy-done.2
  8.2 0.0 copy-done.3
  8.2 0.0 copy-start.4
  8.2 0.9 %tables.1 = (f32[128,128]{1,0:T(8,128)S(1)}, f32[16,128]{1,0:T(8,128)S(1)}, f32[128,128]{1,0:T(8,128)S(1)}) custom-call(s32[5]{0:T(128)S(1)} %stack.23.where_ref, s32[2,512]{1,0:T(2,128)S(1)} %copy-done.2, s32[2,512]{1,0:T(2,128)S(1)} %copy-done.3, f32[2,2,512]{2,1,0:T(2,128)S(1)} %copy-done.1), custom_call_target="tpu_custom_call" | custom-call | flops 4000000 | bytes 2000000 | tf_op jit(solution)/shard_map/tables/pallas_call | solution.py:354
  9.1 0.0 copy-start.5
  9.1 0.0 copy-done.4
  9.1 0.6 copy-done.5
  9.8 0.1 broadcast_in_dim.10.coef_ref
  9.8 0.0 collective-permute-done.below_ref
  9.8 1.9 %collective-permute-done.1.above_ref = f32[2,7,16,128]{3,2,1,0:T(8,128)S(1)} collective-permute-done((f32[2,7,16,128]{3,2,1,0:T(8,128)S(1)}, f32[2,7,16,128]{3,2,1,0:T(8,128)S(1)}, u32[]{:S(2)}, u32[]{:S(2)}) %collective-permute-start.1) | collective-permute-done | bytes 114720 | tf_op jit(solution)/shard_map/ppermute | solution.py:334
  11.8 0.0 copy-done
  11.8 5.2 %collective-permute-start.2 = (f32[7,40,128]{2,1,0:T(8,128)S(1)}, f32[7,40,128]{2,1,0:T(8,128)S(1)}, u32[]{:S(2)}, u32[]{:S(2)}) collective-permute-start(f32[7,40,128]{2,1,0:T(8,128)S(1)} %get-tuple-element.24), channel_id=1, source_target_pairs={{0,32},{32,64},{64,96},{96,128},{128,160},{160,192},{192,224},{224... | collective-permute-start | bytes 430088 | tf_op jit(solution)/shard_map/ppermute | solution.py:334
  17.0 1.9 %collective-permute-start.3 = (f32[7,40,128]{2,1,0:T(8,128)S(1)}, f32[7,40,128]{2,1,0:T(8,128)S(1)}, u32[]{:S(2)}, u32[]{:S(2)}) collective-permute-start(f32[7,40,128]{2,1,0:T(8,128)S(1)} %get-tuple-element.25), channel_id=1, source_target_pairs={{32,0},{64,32},{96,64},{128,96},{160,128},{192,160},{224,192},{256... | collective-permute-start | bytes 430088 | tf_op jit(solution)/shard_map/ppermute | solution.py:334
  19.0 1.6 %first_a.1 = (f32[1792,128]{1,0:T(8,128)S(1)}, f32[112,128]{1,0:T(8,128)S(1)}) custom-call(f32[1792,128]{1,0:T(8,128)S(1)} %bitcast.23, f32[2,7,16,128]{3,2,1,0:T(8,128)S(1)} %collective-permute-done.below_ref, f32[2,7,16,128]{3,2,1,0:T(8,128)S(1)} %collective-permute-done.1.above_ref, f32[8,16,128]{2,1,0:T(8,128)S(1)} %broadcast_in_dim.10.coef_ref, ...), custom_call_target="tpu_custom_call" | custom-call | flops 60000000 | bytes 2000000 | tf_op jit(solution)/shard_map/first_a/pallas_call | solution.py:376
  20.6 0.0 collective-permute-done.2.rad_below_ref
  20.6 3.5 %collective-permute-done.3.rad_above_ref = f32[7,40,128]{2,1,0:T(8,128)S(1)} collective-permute-done((f32[7,40,128]{2,1,0:T(8,128)S(1)}, f32[7,40,128]{2,1,0:T(8,128)S(1)}, u32[]{:S(2)}, u32[]{:S(2)}) %collective-permute-start.3) | collective-permute-done | bytes 143392 | tf_op jit(solution)/shard_map/ppermute | solution.py:334
  24.1 1.1 %first_b.1 = (f32[512,128]{1,0:T(8,128)S(1)}, f32[2,7,16,128]{3,2,1,0:T(8,128)S(1)}, f32[128,128]{1,0:T(8,128)S(1)}) custom-call(s32[5]{0:T(128)S(1)} %stack.23.where_ref, f32[1792,128]{1,0:T(8,128)S(1)} %bitcast.24, f32[2,7,16,128]{3,2,1,0:T(8,128)S(1)} %collective-permute-done.below_ref, f32[2,7,16,128]{3,2,1,0:T(8,128)S(1)} %collective-permute-done.1.above_ref, ...), custom_call_target="tpu_custom_call" | custom-call | tf_op jit(solution)/shard_map/first_b/pallas_call | solution.py:386
  25.2 22.9 %all_to_all.10 = f32[64,2,128]{2,1,0:T(2,128)S(1)} all-to-all(f32[64,2,128]{2,1,0:T(2,128)S(1)} %bitcast.28), channel_id=1, replica_groups=mesh['panel'=2,'rad'=12,'ang'=32] {'panel','ang'}, dimensions={0} | all-to-all | bytes 131072 | tf_op jit(solution)/shard_map/all_to_all | solution.py:339
  48.1 2.6 %second.1 = (f32[1792,128]{1,0:T(8,128)S(1)}, f32[128,128]{1,0:T(8,128)S(1)}) custom-call(f32[1792,128]{1,0:T(8,128)S(1)} %bitcast.25, f32[1792,128]{1,0:T(8,128)S(1)} %get-tuple-element.23.inner_ref, f32[512,128]{1,0:T(8,128)S(1)} %get-tuple-element.27.edge_ref, f32[2,7,16,128]{3,2,1,0:T(8,128)S(1)} %get-tuple-element.28.ring_ref, ...), custom_call_target="tpu_custom_call" | custom-call | tf_op jit(solution)/shard_map/second/pallas_call | solution.py:399
  50.7 14.0 %all_to_all.11 = f32[64,2,128]{2,1,0:T(2,128)S(1)} all-to-all(f32[64,2,128]{2,1,0:T(2,128)S(1)} %bitcast.29), channel_id=1, replica_groups=mesh['panel'=2,'rad'=12,'ang'=32] {'panel','ang'}, dimensions={0} | all-to-all | bytes 131072 | tf_op jit(solution)/shard_map/all_to_all | solution.py:339
  64.6 1.6 %last.1 = f32[1792,128]{1,0:T(8,128)} custom-call(f32[1792,128]{1,0:T(8,128)S(1)} %get-tuple-element.31.next_ref, f32[128,128]{1,0:T(8,128)S(1)} %bitcast.27, f32[128,128]{1,0:T(8,128)S(1)} %get-tuple-element.30.place_ref), custom_call_target="tpu_custom_call" | custom-call | tf_op jit(solution)/shard_map/last/pallas_call | solution.py:409
  (4 shorter events, 0.1 us)
Async XLA Ops:
  0.0 11.8 %copy-start = (f32[1,7,16,16,128]{4,3,2,1,0:T(8,128)S(1)}, f32[1,7,16,16,128]{4,3,2,1,0:T(8,128)}, u32[]{:S(2)}) copy-start(f32[1,7,16,16,128]{4,3,2,1,0:T(8,128)} %param.6) | copy-start | bytes 2752516
  1.7 8.1 %collective-permute-start = (f32[2,7,16,128]{3,2,1,0:T(8,128)S(1)}, f32[2,7,16,128]{3,2,1,0:T(8,128)S(1)}, u32[]{:S(2)}, u32[]{:S(2)}) collective-permute-start(f32[2,7,16,128]{3,2,1,0:T(8,128)S(1)} %pad_maximum_fusion), channel_id=1, source_target_pairs={{0,1},{1,2},{2,3},{3,4},{4,5},{5,6},{6,7},{7,8},{8,9},{9,10},{10,1... | collective-permute-start | bytes 344072 | tf_op jit(solution)/shard_map/ppermute | solution.py:334
  5.5 6.3 %collective-permute-start.1 = (f32[2,7,16,128]{3,2,1,0:T(8,128)S(1)}, f32[2,7,16,128]{3,2,1,0:T(8,128)S(1)}, u32[]{:S(2)}, u32[]{:S(2)}) collective-permute-start(f32[2,7,16,128]{3,2,1,0:T(8,128)S(1)} %pad_maximum_fusion.1), channel_id=1, source_target_pairs={{1,0},{2,1},{3,2},{4,3},{5,4},{6,5},{7,6},{8,7},{9,8},{10,9},{11,1... | collective-permute-start | bytes 344072 | tf_op jit(solution)/shard_map/ppermute | solution.py:334
  7.5 0.7 %copy-start.1 = (f32[2,2,512]{2,1,0:T(2,128)S(1)}, f32[2,2,512]{2,1,0:T(2,128)}, u32[]{:S(2)}) copy-start(f32[2,2,512]{2,1,0:T(2,128)} %frac_ref.1) | copy-start | bytes 24580
  7.5 0.7 %copy-start.2 = (s32[2,512]{1,0:T(2,128)S(1)}, s32[2,512]{1,0:T(2,128)}, u32[]{:S(2)}) copy-start(s32[2,512]{1,0:T(2,128)} %lon_ref.1) | copy-start | bytes 12292
  7.5 0.7 %copy-start.3 = (s32[2,512]{1,0:T(2,128)S(1)}, s32[2,512]{1,0:T(2,128)}, u32[]{:S(2)}) copy-start(s32[2,512]{1,0:T(2,128)} %lat_ref.1) | copy-start | bytes 12292
  8.2 0.9 %copy-start.4 = (f32[7,16]{1,0:T(8,128)S(1)}, f32[7,16]{1,0:T(8,128)}, u32[]{:S(2)}) copy-start(f32[7,16]{1,0:T(8,128)} %param.7) | copy-start | bytes 1348
  9.1 0.7 copy-start.5
  11.8 8.8 %collective-permute-start.2 = (f32[7,40,128]{2,1,0:T(8,128)S(1)}, f32[7,40,128]{2,1,0:T(8,128)S(1)}, u32[]{:S(2)}, u32[]{:S(2)}) collective-permute-start(f32[7,40,128]{2,1,0:T(8,128)S(1)} %get-tuple-element.24), channel_id=1, source_target_pairs={{0,32},{32,64},{64,96},{96,128},{128,160},{160,192},{192,224},{224... | collective-permute-start | bytes 430088 | tf_op jit(solution)/shard_map/ppermute | solution.py:334
  17.0 7.1 %collective-permute-start.3 = (f32[7,40,128]{2,1,0:T(8,128)S(1)}, f32[7,40,128]{2,1,0:T(8,128)S(1)}, u32[]{:S(2)}, u32[]{:S(2)}) collective-permute-start(f32[7,40,128]{2,1,0:T(8,128)S(1)} %get-tuple-element.25), channel_id=1, source_target_pairs={{32,0},{64,32},{96,64},{128,96},{160,128},{192,160},{224,192},{256... | collective-permute-start | bytes 430088 | tf_op jit(solution)/shard_map/ppermute | solution.py:334

commit v3 on v2

--- a/solution.py
+++ b/solution.py
@@ -112,14 +112,31 @@
     return jnp.sum(along.reshape(n, CP, along.shape[1]) * lon_weight_ref[...][None], axis=1)
 
 
-def pack_kernel(state_ref, below_ref, above_ref, coef_ref, up_ref, down_ref):
+def cut_kernel(where_ref, state_ref, outer_ref, inner_ref):
+    odd = where_ref[2] % 2 == 1
+    for f in range(NF):
+        for i in range(2):
+            low = state_ref[pl.ds(f * TILE + i, LV, CP), :]
+            high = state_ref[pl.ds(f * TILE + CP - 1 - i, LV, CP), :]
+            outer_ref[i, f] = jnp.where(odd, high, low)
+            inner_ref[i, f] = jnp.where(odd, low, high)
+
+
+def pack_kernel(
+    where_ref, state_ref, outer_ref, inner_ref, coef_ref, up_ref, down_ref, below_ref, above_ref
+):
+    odd = where_ref[2] % 2 == 1
+    for i in range(2):
+        for f in range(NF):
+            above_ref[i, f] = jnp.where(odd, outer_ref[i, f], inner_ref[i, f])
+            below_ref[i, f] = jnp.where(odd, inner_ref[i, f], outer_ref[i, f])
     for ref, near, far in ((up_ref, LV - 1, LV - 2), (down_ref, 0, 1)):
         for f in range(NF):
             start = f * TILE
             ref[f, 0:CP, :] = state_ref[start + near * CP : start + (near + 1) * CP, :]
             ref[f, CP : 2 * CP, :] = state_ref[start + far * CP : start + (far + 1) * CP, :]
             ref[f, 32:33, :] = above_ref[0, f, near : near + 1, :]
-            ref[f, 33:34, :] = below_ref[1, f, near : near + 1, :]
+            ref[f, 33:34, :] = below_ref[0, f, near : near + 1, :]
             ref[f, 34:35, :] = coef_ref[f, near : near + 1, :]
             ref[f, 35:36, :] = coef_ref[NF, near : near + 1, :]
             ref[f, 36:40, :] = jnp.zeros((4, LAT), F32)
@@ -132,7 +149,7 @@
         for r in range(LV):
             base = (f * LV + r) * BLOCK + 8
             line_ref[base : base + CP, :] = state_ref[f * TILE + r * CP : f * TILE + (r + 1) * CP, :]
-        line_ref[pl.ds(f * LV * BLOCK + 7, LV, BLOCK), :] = below_ref[1, f]
+        line_ref[pl.ds(f * LV * BLOCK + 7, LV, BLOCK), :] = below_ref[0, f]
         line_ref[pl.ds(f * LV * BLOCK + 24, LV, BLOCK), :] = above_ref[0, f]
         for r in (0, LV - 1):
             inner_ref[f * TILE + r * CP : f * TILE + (r + 1) * CP, :] = jnp.zeros((CP, LAT), F32)
@@ -173,14 +190,14 @@
         for e, r in ((1, 0), (2, LV - 1)):
             base = (e * NF + f) * BLOCK + 8
             line_ref[base : base + CP, :] = state_ref[f * TILE + r * CP : f * TILE + (r + 1) * CP, :]
-            line_ref[base - 1 : base, :] = below_ref[1, f, r : r + 1, :]
+            line_ref[base - 1 : base, :] = below_ref[0, f, r : r + 1, :]
             line_ref[base + CP : base + CP + 1, :] = above_ref[0, f, r : r + 1, :]
         for e, ref in ((0, rad_below_ref), (3, rad_above_ref)):
             base = (e * NF + f) * BLOCK + 8
             line_ref[base : base + CP, :] = ref[f, 0:CP, :]
             line_ref[base - 1 : base, :] = ref[f, 33:34, :]
             line_ref[base + CP : base + CP + 1, :] = ref[f, 32:33, :]
-        for side, ref in ((0, below_ref.at[1]), (1, above_ref.at[0])):
+        for side, ref in ((0, below_ref.at[0]), (1, above_ref.at[0])):
             base = (side * NF + f) * BLOCK + 8
             column_ref[base : base + LV, :] = ref[f]
             column_ref[base - 1 : base, :] = rad_below_ref[f, 33 - side : 34 - side, :]
@@ -230,12 +247,12 @@
                 column = (side * NF + f) * BLOCK + 8 + 8 * t
                 near = state_ref[pl.ds(f * TILE + 8 * t * CP + side * (CP - 1), 8, CP), :]
                 if side == 0:
-                    east, west = near, below_ref[0, f, part, :]
+                    east, west = near, below_ref[1, f, part, :]
                 else:
                     east, west = above_ref[1, f, part, :], near
                 return column_ref[column + 1 : column + 9, :], column_ref[column - 1 : column + 7, :], east, west
 
-            center = [(below_ref[1, f, part, :] if side == 0 else above_ref[0, f, part, :]) for f in range(NF)]
+            center = [(below_ref[0, f, part, :] if side == 0 else above_ref[0, f, part, :]) for f in range(NF)]
             rates = increments(center, neighbours, lambda f: coef_ref[f, part, :], coef_ref[NF, part, :], step_size)
             for f in range(NF):
                 ring_ref[side, f, part, :] = keep_ang[side] * (center[f] + rates[f])
@@ -334,6 +351,12 @@
     return lax.ppermute(value, axis, pairs)
 
 
+def swap(value, axis, first):
+    count = lax.axis_size(axis)
+    low = range(first, count - 1, 2)
+    return lax.ppermute(value, axis, [(i, i + 1) for i in low] + [(i + 1, i) for i in low])
+
+
 def exchange(values):
     n = values.shape[0] // 2
     got = lax.all_to_all(values.reshape(n, 2, 128), ("panel", "ang"), 0, 0, tiled=True)
@@ -345,9 +368,17 @@
         [lax.axis_index(a) for a in ("panel", "rad", "ang")] + [lax.axis_size(a) for a in ("rad", "ang")]
     ).astype(jnp.int32)
 
-    below = shift(jnp.stack([state[0, :, :, CP - 2], state[0, :, :, CP - 1]]), "ang", 1)
-    above = shift(jnp.stack([state[0, :, :, 0], state[0, :, :, 1]]), "ang", -1)
     own = state.reshape(NF * TILE, LAT)
+    outer, inner = pl.pallas_call(
+        cut_kernel,
+        out_shape=(shape(2, NF, LV, LAT),) * 2,
+        in_specs=[SMEM, VMEM],
+        out_specs=(VMEM,) * 2,
+        compiler_params=params(),
+        name="cut",
+    )(where, own)
+    outer = swap(outer, "ang", 1)
+    inner = swap(inner, "ang", 0)
 
     coef = jnp.broadcast_to(jnp.concatenate([kappa, buoyancy[None]])[:, :, None], (NF + 1, LV, LAT))
     n_send = 4 * donor_lon.shape[1] // CP
@@ -362,18 +393,18 @@
     )(where, donor_lon, donor_lat, fractions)
     coef, lat_weight = lax.optimization_barrier((coef, lat_weight))
 
-    up, down = pl.pallas_call(
+    up, down, below, above = pl.pallas_call(
         pack_kernel,
-        out_shape=(shape(NF, MESSAGE, LAT),) * 2,
-        in_specs=[VMEM] * 4,
-        out_specs=(VMEM,) * 2,
+        out_shape=(shape(NF, MESSAGE, LAT),) * 2 + (shape(2, NF, LV, LAT),) * 2,
+        in_specs=[SMEM] + [VMEM] * 4,
+        out_specs=(VMEM,) * 4,
         compiler_params=params(),
         name="pack",
-    )(own, below, above, coef)
+    )(where, own, outer, inner, coef)
     rad_below = shift(up, "rad", 1)
     rad_above = shift(down, "rad", -1)
 
-    inner, inner_values = pl.pallas_call(
+    middle, middle_values = pl.pallas_call(
         first_a_kernel,
         out_shape=(shape(NF * TILE, LAT), shape(NF * LV, n_send)),
         in_specs=[VMEM] * 6,
@@ -394,7 +425,7 @@
         ],
         compiler_params=params(),
         name="first_b",
-    )(where, own, below, above, coef, rad_below, rad_above, lat_weight, lon_weight, inner_values)
+    )(where, own, below, above, coef, rad_below, rad_above, lat_weight, lon_weight, middle_values)
     got = exchange(out)
     following, out = pl.pallas_call(
         second_kernel,
@@ -404,7 +435,7 @@
         scratch_shapes=[pltpu.VMEM((NF * (LV + 2) * BLOCK + 8, LAT), F32)],
         compiler_params=params(),
         name="second",
-    )(own, inner, edge, ring, coef, got, place, lat_weight, lon_weight)
+    )(own, middle, edge, ring, coef, got, place, lat_weight, lon_weight)
     got = exchange(out)
     result = pl.pallas_call(
         last_kernel,

time: 66.6 us -> 65.4 us (0.982)
  waiting for transfers between devices: 5.4 us -> 3.94 us
  Pallas kernels: 7.87 us -> 9.18 us
  local copies, waits for them, and re-layouts: 3.12 us -> 2 us
    ppermute x4 -> x2, starting transfers between devices: 12.8 us -> 7.13 us  [shift(): return lax.ppermute(value, axis, pairs)]
    ppermute x0 -> x2, starting transfers between devices: none -> 5.69 us  [swap(): lax.ppermute(value, axis, [(i, i + 1) for i in low] + [(i + 1, i) for i i...]
    slice x1 -> x0, local copies, waits for them, and re-layouts: 1.7 us -> none  [body(): above = shift(jnp.stack([state[0, :, :, 0], state[0, :, :, 1]]), 'ang', -1)]
    ppermute x4 -> x2, waiting for transfers between devices: 5.4 us -> 3.93 us  [shift(): return lax.ppermute(value, axis, pairs)]
    pallas_call x1 -> x2, Pallas kernels: 0.04 us -> 1.21 us  [the longest x1 0.61 us: body(): pl.pallas_call(cut_kernel, out_shape=(shape(2, NF, LV, LAT),) * 2, in_spe...]
    unnamed x12 -> x14, local copies, waits for them, and re-layouts: 1.26 us -> 1.84 us
  transfers between devices with their start and end apart: 4 -> 4, of which waited for: 2 -> 1; matrix products, arithmetic and copies ran while one was open for 0% -> 0% of each run, Pallas kernels for 4% -> 4%
where the time goes in v3:
time: 65.4 us; the launch traced here: 65.1 us
  blocking collectives  37 us (57%)
  starting transfers between devices  12.8 us (20%)
  Pallas kernels  9.18 us (14%)
  waiting for transfers between devices  3.94 us (6%)
  local copies, waits for them, and re-layouts  2 us (3%)
    all_to_all x2, blocking collectives, exchange(): lax.all_to_all(values.reshape(n, 2, 128), ('panel', 'ang'), 0, 0, tiled=T...  37 us
    ppermute x2, starting transfers between devices, shift(): return lax.ppermute(value, axis, pairs)  7.13 us
    ppermute x2, starting transfers between devices, swap(): lax.ppermute(value, axis, [(i, i + 1) for i in low] + [(i + 1, i) for i i...  5.69 us
    ppermute x2, waiting for transfers between devices, shift(): return lax.ppermute(value, axis, pairs)  3.93 us
    pallas_call x1, Pallas kernels, body(): pl.pallas_call(second_kernel, out_shape=(shape(NF * TILE, LAT), shape(n_s...  2.61 us
    unnamed x14, local copies, waits for them, and re-layouts  1.84 us
    pallas_call x1, Pallas kernels, body(): pl.pallas_call(first_a_kernel, out_shape=(shape(NF * TILE, LAT), shape(NF...  1.73 us
    pallas_call x1, Pallas kernels, body(): pl.pallas_call(last_kernel, out_shape=shape(NF * TILE, LAT), in_specs=[VM...  1.61 us
  transfers between devices with their start and end apart: 4, of which 1 were waited for; matrix products, arithmetic and copies ran while one was open for 0% of the time, Pallas kernels for 4%

profile of v3, /device:TPU:193, one launch (start us, length us, event | category | flops | bytes accessed | tf_op | source)
XLA Modules:
  0.0 65.1 jit_solution(9502935602197925453)
XLA Ops:
  0.0 0.0 copy-start.4
  0.0 0.0 copy-start.2
  0.0 0.1 stack.15.where_ref
  0.1 0.0 copy-start
  0.1 1.2 %copy-done = f32[1,7,16,16,128]{4,3,2,1,0:T(8,128)S(1)} copy-done((f32[1,7,16,16,128]{4,3,2,1,0:T(8,128)S(1)}, f32[1,7,16,16,128]{4,3,2,1,0:T(8,128)}, u32[]{:S(2)}) %copy-start) | copy-done | bytes 917528
  1.3 0.0 copy-start.3
  1.3 0.0 copy-start.1
  1.3 0.6 cut.1
  1.9 3.8 %collective-permute-start = (f32[2,7,16,128]{3,2,1,0:T(8,128)S(1)}, f32[2,7,16,128]{3,2,1,0:T(8,128)S(1)}, u32[]{:S(2)}, u32[]{:S(2)}) collective-permute-start(f32[2,7,16,128]{3,2,1,0:T(8,128)S(1)} %get-tuple-element.23), channel_id=1, source_target_pairs={{1,2},{3,4},{5,6},{7,8},{9,10},{11,12},{13,14},{15,16},{17,18},{19... | collective-permute-start | bytes 344072 | tf_op jit(solution)/shard_map/ppermute | solution.py:357
  5.7 1.9 %collective-permute-start.1 = (f32[2,7,16,128]{3,2,1,0:T(8,128)S(1)}, f32[2,7,16,128]{3,2,1,0:T(8,128)S(1)}, u32[]{:S(2)}, u32[]{:S(2)}) collective-permute-start(f32[2,7,16,128]{3,2,1,0:T(8,128)S(1)} %get-tuple-element.24), channel_id=1, source_target_pairs={{0,1},{2,3},{4,5},{6,7},{8,9},{10,11},{12,13},{14,15},{16,17},{18,... | collective-permute-start | bytes 344072 | tf_op jit(solution)/shard_map/ppermute | solution.py:357
  7.6 0.0 copy-done.4
  7.6 0.0 copy-done.2
  7.6 0.0 copy-done.3
  7.6 0.0 copy-start.5
  7.6 0.9 %tables.1 = (f32[128,128]{1,0:T(8,128)S(1)}, f32[16,128]{1,0:T(8,128)S(1)}, f32[128,128]{1,0:T(8,128)S(1)}) custom-call(s32[5]{0:T(128)S(1)} %stack.15.where_ref, s32[2,512]{1,0:T(2,128)S(1)} %copy-done.3, s32[2,512]{1,0:T(2,128)S(1)} %copy-done.4, f32[2,2,512]{2,1,0:T(2,128)S(1)} %copy-done.2), custom_call_target="tpu_custom_call" | custom-call | flops 4000000 | bytes 2000000 | tf_op jit(solution)/shard_map/tables/pallas_call | solution.py:385
  8.5 0.0 copy-start.6
  8.6 0.0 copy-done.5
  8.6 0.6 copy-done.6
  9.2 0.1 broadcast_in_dim.10.coef_ref
  9.3 0.0 collective-permute-done.outer_ref
  9.3 0.0 collective-permute-done.1.inner_ref
  9.3 0.0 copy-done.1
  9.3 0.6 pack.1
  9.9 5.2 %collective-permute-start.2 = (f32[7,40,128]{2,1,0:T(8,128)S(1)}, f32[7,40,128]{2,1,0:T(8,128)S(1)}, u32[]{:S(2)}, u32[]{:S(2)}) collective-permute-start(f32[7,40,128]{2,1,0:T(8,128)S(1)} %get-tuple-element.32), channel_id=1, source_target_pairs={{0,32},{32,64},{64,96},{96,128},{128,160},{160,192},{192,224},{224... | collective-permute-start | bytes 430088 | tf_op jit(solution)/shard_map/ppermute | solution.py:351
  15.1 1.9 %collective-permute-start.3 = (f32[7,40,128]{2,1,0:T(8,128)S(1)}, f32[7,40,128]{2,1,0:T(8,128)S(1)}, u32[]{:S(2)}, u32[]{:S(2)}) collective-permute-start(f32[7,40,128]{2,1,0:T(8,128)S(1)} %get-tuple-element.33), channel_id=1, source_target_pairs={{32,0},{64,32},{96,64},{128,96},{160,128},{192,160},{224,192},{256... | collective-permute-start | bytes 430088 | tf_op jit(solution)/shard_map/ppermute | solution.py:351
  17.1 1.7 %first_a.1 = (f32[1792,128]{1,0:T(8,128)S(1)}, f32[112,128]{1,0:T(8,128)S(1)}) custom-call(f32[1792,128]{1,0:T(8,128)S(1)} %bitcast.12, f32[2,7,16,128]{3,2,1,0:T(8,128)S(1)} %get-tuple-element.27.below_ref, f32[2,7,16,128]{3,2,1,0:T(8,128)S(1)} %get-tuple-element.28.above_ref, f32[8,16,128]{2,1,0:T(8,128)S(1)} %broadcast_in_dim.10.coef_ref, ...), custom_call_target="tpu_custom_call" | custom-call | flops 60000000 | bytes 2000000 | tf_op jit(solution)/shard_map/first_a/pallas_call | solution.py:407
  18.8 0.0 collective-permute-done.2.rad_below_ref
  18.8 3.9 %collective-permute-done.3.rad_above_ref = f32[7,40,128]{2,1,0:T(8,128)S(1)} collective-permute-done((f32[7,40,128]{2,1,0:T(8,128)S(1)}, f32[7,40,128]{2,1,0:T(8,128)S(1)}, u32[]{:S(2)}, u32[]{:S(2)}) %collective-permute-start.3) | collective-permute-done | bytes 143392 | tf_op jit(solution)/shard_map/ppermute | solution.py:351
  22.8 1.1 %first_b.1 = (f32[512,128]{1,0:T(8,128)S(1)}, f32[2,7,16,128]{3,2,1,0:T(8,128)S(1)}, f32[128,128]{1,0:T(8,128)S(1)}) custom-call(s32[5]{0:T(128)S(1)} %stack.15.where_ref, f32[1792,128]{1,0:T(8,128)S(1)} %bitcast.13, f32[2,7,16,128]{3,2,1,0:T(8,128)S(1)} %get-tuple-element.27.below_ref, f32[2,7,16,128]{3,2,1,0:T(8,128)S(1)} %get-tuple-element.28.above_ref, ...), custom_call_target="tpu_custom_call" | custom-call | tf_op jit(solution)/shard_map/first_b/pallas_call | solution.py:417
  23.9 23.1 %all_to_all.10 = f32[64,2,128]{2,1,0:T(2,128)S(1)} all-to-all(f32[64,2,128]{2,1,0:T(2,128)S(1)} %bitcast.17), channel_id=1, replica_groups=mesh['panel'=2,'rad'=12,'ang'=32] {'panel','ang'}, dimensions={0} | all-to-all | bytes 131072 | tf_op jit(solution)/shard_map/all_to_all | solution.py:362
  46.9 2.6 %second.1 = (f32[1792,128]{1,0:T(8,128)S(1)}, f32[128,128]{1,0:T(8,128)S(1)}) custom-call(f32[1792,128]{1,0:T(8,128)S(1)} %bitcast.14, f32[1792,128]{1,0:T(8,128)S(1)} %get-tuple-element.31.inner_ref, f32[512,128]{1,0:T(8,128)S(1)} %get-tuple-element.35.edge_ref, f32[2,7,16,128]{3,2,1,0:T(8,128)S(1)} %get-tuple-element.36.ring_ref, ...), custom_call_target="tpu_custom_call" | custom-call | tf_op jit(solution)/shard_map/second/pallas_call | solution.py:430
  49.5 14.0 %all_to_all.11 = f32[64,2,128]{2,1,0:T(2,128)S(1)} all-to-all(f32[64,2,128]{2,1,0:T(2,128)S(1)} %bitcast.18), channel_id=1, replica_groups=mesh['panel'=2,'rad'=12,'ang'=32] {'panel','ang'}, dimensions={0} | all-to-all | bytes 131072 | tf_op jit(solution)/shard_map/all_to_all | solution.py:362
  63.5 1.6 %last.1 = f32[1792,128]{1,0:T(8,128)} custom-call(f32[1792,128]{1,0:T(8,128)S(1)} %get-tuple-element.39.next_ref, f32[128,128]{1,0:T(8,128)S(1)} %bitcast.16, f32[128,128]{1,0:T(8,128)S(1)} %get-tuple-element.38.place_ref), custom_call_target="tpu_custom_call" | custom-call | tf_op jit(solution)/shard_map/last/pallas_call | solution.py:440
  (1 shorter events, 0.0 us)
Async XLA Ops:
  0.0 7.6 %copy-start.4 = (s32[2,512]{1,0:T(2,128)S(1)}, s32[2,512]{1,0:T(2,128)}, u32[]{:S(2)}) copy-start(s32[2,512]{1,0:T(2,128)} %lat_ref.1) | copy-start | bytes 12292
  0.0 7.6 %copy-start.2 = (f32[2,2,512]{2,1,0:T(2,128)S(1)}, f32[2,2,512]{2,1,0:T(2,128)}, u32[]{:S(2)}) copy-start(f32[2,2,512]{2,1,0:T(2,128)} %frac_ref.1) | copy-start | bytes 24580
  0.1 1.2 %copy-start = (f32[1,7,16,16,128]{4,3,2,1,0:T(8,128)S(1)}, f32[1,7,16,16,128]{4,3,2,1,0:T(8,128)}, u32[]{:S(2)}) copy-start(f32[1,7,16,16,128]{4,3,2,1,0:T(8,128)} %param.6) | copy-start | bytes 2752516
  1.3 6.3 %copy-start.3 = (s32[2,512]{1,0:T(2,128)S(1)}, s32[2,512]{1,0:T(2,128)}, u32[]{:S(2)}) copy-start(s32[2,512]{1,0:T(2,128)} %lon_ref.1) | copy-start | bytes 12292
  1.3 8.0 %copy-start.1 = (f32[1,7,16,16,128]{4,3,2,1,0:T(8,128)S(1)}, f32[1,7,16,16,128]{4,3,2,1,0:T(8,128)}, u32[]{:S(2)}) copy-start(f32[1,7,16,16,128]{4,3,2,1,0:T(8,128)} %param.6) | copy-start | bytes 2752516
  1.9 7.4 %collective-permute-start = (f32[2,7,16,128]{3,2,1,0:T(8,128)S(1)}, f32[2,7,16,128]{3,2,1,0:T(8,128)S(1)}, u32[]{:S(2)}, u32[]{:S(2)}) collective-permute-start(f32[2,7,16,128]{3,2,1,0:T(8,128)S(1)} %get-tuple-element.23), channel_id=1, source_target_pairs={{1,2},{3,4},{5,6},{7,8},{9,10},{11,12},{13,14},{15,16},{17,18},{19... | collective-permute-start | bytes 344072 | tf_op jit(solution)/shard_map/ppermute | solution.py:357
  5.7 3.6 %collective-permute-start.1 = (f32[2,7,16,128]{3,2,1,0:T(8,128)S(1)}, f32[2,7,16,128]{3,2,1,0:T(8,128)S(1)}, u32[]{:S(2)}, u32[]{:S(2)}) collective-permute-start(f32[2,7,16,128]{3,2,1,0:T(8,128)S(1)} %get-tuple-element.24), channel_id=1, source_target_pairs={{0,1},{2,3},{4,5},{6,7},{8,9},{10,11},{12,13},{14,15},{16,17},{18,... | collective-permute-start | bytes 344072 | tf_op jit(solution)/shard_map/ppermute | solution.py:357
  7.6 0.9 %copy-start.5 = (f32[7,16]{1,0:T(8,128)S(1)}, f32[7,16]{1,0:T(8,128)}, u32[]{:S(2)}) copy-start(f32[7,16]{1,0:T(8,128)} %param.7) | copy-start | bytes 1348
  8.5 0.7 %copy-start.6 = (f32[16]{0:T(128)S(1)}, f32[16]{0:T(128)}, u32[]{:S(2)}) copy-start(f32[16]{0:T(128)} %param.8) | copy-start | bytes 196
  9.9 8.9 %collective-permute-start.2 = (f32[7,40,128]{2,1,0:T(8,128)S(1)}, f32[7,40,128]{2,1,0:T(8,128)S(1)}, u32[]{:S(2)}, u32[]{:S(2)}) collective-permute-start(f32[7,40,128]{2,1,0:T(8,128)S(1)} %get-tuple-element.32), channel_id=1, source_target_pairs={{0,32},{32,64},{64,96},{96,128},{128,160},{160,192},{192,224},{224... | collective-permute-start | bytes 430088 | tf_op jit(solution)/shard_map/ppermute | solution.py:351
  15.1 7.6 %collective-permute-start.3 = (f32[7,40,128]{2,1,0:T(8,128)S(1)}, f32[7,40,128]{2,1,0:T(8,128)S(1)}, u32[]{:S(2)}, u32[]{:S(2)}) collective-permute-start(f32[7,40,128]{2,1,0:T(8,128)S(1)} %get-tuple-element.33), channel_id=1, source_target_pairs={{32,0},{64,32},{96,64},{128,96},{160,128},{192,160},{224,192},{256... | collective-permute-start | bytes 430088 | tf_op jit(solution)/shard_map/ppermute | solution.py:351

commit v4 on v3

--- a/solution.py
+++ b/solution.py
@@ -8,7 +8,6 @@
 step_size = 0.1
 HIGHEST = lax.Precision.HIGHEST
 VMEM = pl.BlockSpec(memory_space=pltpu.VMEM)
-SMEM = pl.BlockSpec(memory_space=pltpu.SMEM)
 F32 = jnp.float32
 
 NF = 7
@@ -17,7 +16,7 @@
 LAT = 128
 TILE = LV * CP
 BLOCK = 24
-MESSAGE = 40
+LATE = 24
 
 
 def params():
@@ -40,12 +39,12 @@
     return jnp.where(slot == 0, low_or_none, high_or_none)
 
 
-def tables_kernel(where_ref, lon_ref, lat_ref, frac_ref, lat_weight_ref, lon_weight_ref, place_ref):
+def tables_kernel(lon_ref, lat_ref, frac_ref, lat_weight_ref, lon_weight_ref, place_ref):
     nlon = lon_ref.shape[1]
     half = 2 * nlon // CP
     points = 2 * nlon
-    panel = where_ref[0]
-    tile = where_ref[2]
+    panel = lax.axis_index("panel")
+    tile = lax.axis_index("ang")
 
     def flat(low, high):
         return jnp.concatenate([low, high], axis=1)
@@ -112,20 +111,20 @@
     return jnp.sum(along.reshape(n, CP, along.shape[1]) * lon_weight_ref[...][None], axis=1)
 
 
-def cut_kernel(where_ref, state_ref, outer_ref, inner_ref):
-    odd = where_ref[2] % 2 == 1
+def cut_kernel(state_ref, outer_ref, inner_ref, up_ref, down_ref):
+    odd = lax.axis_index("ang") % 2 == 1
     for f in range(NF):
         for i in range(2):
             low = state_ref[pl.ds(f * TILE + i, LV, CP), :]
             high = state_ref[pl.ds(f * TILE + CP - 1 - i, LV, CP), :]
             outer_ref[i, f] = jnp.where(odd, high, low)
             inner_ref[i, f] = jnp.where(odd, low, high)
-
-
-def pack_kernel(
-    where_ref, state_ref, outer_ref, inner_ref, coef_ref, up_ref, down_ref, below_ref, above_ref
-):
-    odd = where_ref[2] % 2 == 1
+        up_ref[f] = state_ref[(f + 1) * TILE - CP : (f + 1) * TILE, :]
+        down_ref[f] = state_ref[f * TILE : f * TILE + CP, :]
+
+
+def pack_kernel(state_ref, outer_ref, inner_ref, coef_ref, up_ref, down_ref, below_ref, above_ref):
+    odd = lax.axis_index("ang") % 2 == 1
     for i in range(2):
         for f in range(NF):
             above_ref[i, f] = jnp.where(odd, outer_ref[i, f], inner_ref[i, f])
@@ -133,13 +132,12 @@
     for ref, near, far in ((up_ref, LV - 1, LV - 2), (down_ref, 0, 1)):
         for f in range(NF):
             start = f * TILE
-            ref[f, 0:CP, :] = state_ref[start + near * CP : start + (near + 1) * CP, :]
-            ref[f, CP : 2 * CP, :] = state_ref[start + far * CP : start + (far + 1) * CP, :]
-            ref[f, 32:33, :] = above_ref[0, f, near : near + 1, :]
-            ref[f, 33:34, :] = below_ref[0, f, near : near + 1, :]
-            ref[f, 34:35, :] = coef_ref[f, near : near + 1, :]
-            ref[f, 35:36, :] = coef_ref[NF, near : near + 1, :]
-            ref[f, 36:40, :] = jnp.zeros((4, LAT), F32)
+            ref[f, 0:CP, :] = state_ref[start + far * CP : start + (far + 1) * CP, :]
+            ref[f, 16:17, :] = above_ref[0, f, near : near + 1, :]
+            ref[f, 17:18, :] = below_ref[0, f, near : near + 1, :]
+            ref[f, 18:19, :] = coef_ref[f, near : near + 1, :]
+            ref[f, 19:20, :] = coef_ref[NF, near : near + 1, :]
+            ref[f, 20:24, :] = jnp.zeros((4, LAT), F32)
 
 
 def first_a_kernel(
@@ -178,87 +176,95 @@
 
 
 def first_b_kernel(
-    where_ref, state_ref, below_ref, above_ref, coef_ref, rad_below_ref, rad_above_ref, lat_weight_ref,
-    lon_weight_ref, values_ref, edge_ref, ring_ref, send_ref, line_ref, column_ref,
+    state_ref, below_ref, above_ref, coef_ref, near_below_ref, near_above_ref, lat_weight_ref, lon_weight_ref,
+    values_ref, edge_ref, send_ref, line_ref,
 ):
-    rad, ang, n_rad, n_ang = where_ref[1], where_ref[2], where_ref[3], where_ref[4]
-    keep_rad = [jnp.where(rad == 0, 0.0, 1.0), jnp.where(rad == n_rad - 1, 0.0, 1.0)]
-    keep_ang = [jnp.where(ang == 0, 0.0, 1.0), jnp.where(ang == n_ang - 1, 0.0, 1.0)]
-    radial = (rad_below_ref, rad_above_ref)
-
-    for f in range(NF):
-        for e, r in ((1, 0), (2, LV - 1)):
+    for e, r in enumerate((0, LV - 1)):
+        for f in range(NF):
             base = (e * NF + f) * BLOCK + 8
             line_ref[base : base + CP, :] = state_ref[f * TILE + r * CP : f * TILE + (r + 1) * CP, :]
             line_ref[base - 1 : base, :] = below_ref[0, f, r : r + 1, :]
             line_ref[base + CP : base + CP + 1, :] = above_ref[0, f, r : r + 1, :]
-        for e, ref in ((0, rad_below_ref), (3, rad_above_ref)):
-            base = (e * NF + f) * BLOCK + 8
-            line_ref[base : base + CP, :] = ref[f, 0:CP, :]
-            line_ref[base - 1 : base, :] = ref[f, 33:34, :]
-            line_ref[base + CP : base + CP + 1, :] = ref[f, 32:33, :]
-        for side, ref in ((0, below_ref.at[0]), (1, above_ref.at[0])):
-            base = (side * NF + f) * BLOCK + 8
-            column_ref[base : base + LV, :] = ref[f]
-            column_ref[base - 1 : base, :] = rad_below_ref[f, 33 - side : 34 - side, :]
-            column_ref[base + LV : base + LV + 1, :] = rad_above_ref[f, 33 - side : 34 - side, :]
-
-    for e in range(4):
+    for e, r in enumerate((0, LV - 1)):
         for t in range(2):
-            part = slice(8 * t, 8 * t + 8)
-
-            def own(f, r):
-                return state_ref[f * TILE + r * CP + 8 * t : f * TILE + r * CP + 8 * t + 8, :]
+
+            def own(f, level):
+                return state_ref[f * TILE + level * CP + 8 * t : f * TILE + level * CP + 8 * t + 8, :]
 
             def neighbours(f):
                 line = (e * NF + f) * BLOCK + 8 + 8 * t
                 if e == 0:
-                    up, down = own(f, 0), rad_below_ref[f, CP + 8 * t : CP + 8 * t + 8, :]
-                elif e == 1:
-                    up, down = own(f, 1), rad_below_ref[f, part, :]
-                elif e == 2:
-                    up, down = rad_above_ref[f, part, :], own(f, LV - 2)
+                    up, down = own(f, 1), near_below_ref[f, 8 * t : 8 * t + 8, :]
                 else:
-                    up, down = rad_above_ref[f, CP + 8 * t : CP + 8 * t + 8, :], own(f, LV - 1)
+                    up, down = near_above_ref[f, 8 * t : 8 * t + 8, :], own(f, LV - 2)
                 return up, down, line_ref[line + 1 : line + 9, :], line_ref[line - 1 : line + 7, :]
 
-            center = [line_ref[(e * NF + f) * BLOCK + 8 + 8 * t : (e * NF + f) * BLOCK + 16 + 8 * t, :] for f in range(NF)]
-            if e in (0, 3):
-                source = radial[e // 3]
-                rates = increments(center, neighbours, lambda f: source[f, 34:35, :], source[0, 35:36, :], step_size)
-            else:
-                r = (e - 1) * (LV - 1)
-                rates = increments(
-                    center, neighbours, lambda f: coef_ref[f, r : r + 1, :], coef_ref[NF, r : r + 1, :], step_size
-                )
+            center = [own(f, r) for f in range(NF)]
+            rates = increments(
+                center, neighbours, lambda f: coef_ref[f, r : r + 1, :], coef_ref[NF, r : r + 1, :], step_size
+            )
             for f in range(NF):
-                value = center[f] + rates[f]
-                if e in (0, 3):
-                    value = keep_rad[e // 3] * value
                 base = (e * 8 + f) * CP + 8 * t
-                edge_ref[base : base + 8, :] = value
+                edge_ref[base : base + 8, :] = center[f] + rates[f]
         edge_ref[(e * 8 + NF) * CP : (e * 8 + 8) * CP, :] = jnp.zeros((CP, LAT), F32)
-
-    for side in range(2):
+    edges = interpolate(edge_ref[...], lat_weight_ref, lon_weight_ref)
+    send_ref[...] = jnp.transpose(jnp.concatenate([values_ref[...], edges], axis=0))
+
+
+def surround(
+    state_ref, below_ref, above_ref, coef_ref, near_refs, late_refs, work_ref, column_ref, line_ref
+):
+    rad, ang = lax.axis_index("rad"), lax.axis_index("ang")
+    keep_rad = [jnp.where(rad == 0, 0.0, 1.0), jnp.where(rad == lax.axis_size("rad") - 1, 0.0, 1.0)]
+    keep_ang = [jnp.where(ang == 0, 0.0, 1.0), jnp.where(ang == lax.axis_size("ang") - 1, 0.0, 1.0)]
+    for e in range(2):
+        late = late_refs[e]
+        for f in range(NF):
+            base = (e * NF + f) * BLOCK + 8
+            work_ref[base : base + CP, :] = near_refs[e][f]
+            work_ref[base - 1 : base, :] = late[f, 17:18, :]
+            work_ref[base + CP : base + CP + 1, :] = late[f, 16:17, :]
+    for side, ref in ((0, below_ref), (1, above_ref)):
+        for f in range(NF):
+            base = (side * NF + f) * BLOCK + 8
+            column_ref[base : base + LV, :] = ref[0, f]
+            column_ref[base - 1 : base, :] = late_refs[0][f, 17 - side : 18 - side, :]
+            column_ref[base + LV : base + LV + 1, :] = late_refs[1][f, 17 - side : 18 - side, :]
+
+    for e in range(2):
+        late = late_refs[e]
         for t in range(2):
             part = slice(8 * t, 8 * t + 8)
 
             def neighbours(f):
+                line = (e * NF + f) * BLOCK + 8 + 8 * t
+                start = f * TILE + e * (LV - 1) * CP + 8 * t
+                inside, outside = state_ref[start : start + 8, :], late[f, part, :]
+                up, down = (inside, outside) if e == 0 else (outside, inside)
+                return up, down, work_ref[line + 1 : line + 9, :], work_ref[line - 1 : line + 7, :]
+
+            center = [near_refs[e][f, part, :] for f in range(NF)]
+            rates = increments(center, neighbours, lambda f: late[f, 18:19, :], late[0, 19:20, :], step_size)
+            for f in range(NF):
+                base = (f * (LV + 2) + e * (LV + 1)) * BLOCK + 8 + 8 * t
+                line_ref[base : base + 8, :] = keep_rad[e] * (center[f] + rates[f])
+
+    for side, ref in ((0, below_ref), (1, above_ref)):
+        for t in range(2):
+            part = slice(8 * t, 8 * t + 8)
+
+            def neighbours(f):
                 column = (side * NF + f) * BLOCK + 8 + 8 * t
-                near = state_ref[pl.ds(f * TILE + 8 * t * CP + side * (CP - 1), 8, CP), :]
-                if side == 0:
-                    east, west = near, below_ref[1, f, part, :]
-                else:
-                    east, west = above_ref[1, f, part, :], near
+                inside = state_ref[pl.ds(f * TILE + 8 * t * CP + side * (CP - 1), 8, CP), :]
+                outside = ref[1, f, part, :]
+                east, west = (inside, outside) if side == 0 else (outside, inside)
                 return column_ref[column + 1 : column + 9, :], column_ref[column - 1 : column + 7, :], east, west
 
-            center = [(below_ref[0, f, part, :] if side == 0 else above_ref[0, f, part, :]) for f in range(NF)]
+            center = [ref[0, f, part, :] for f in range(NF)]
             rates = increments(center, neighbours, lambda f: coef_ref[f, part, :], coef_ref[NF, part, :], step_size)
             for f in range(NF):
-                ring_ref[side, f, part, :] = keep_ang[side] * (center[f] + rates[f])
-
-    edges = interpolate(edge_ref[8 * CP : 24 * CP, :], lat_weight_ref, lon_weight_ref)
-    send_ref[...] = jnp.transpose(jnp.concatenate([values_ref[...], edges], axis=0))
+                start = (f * (LV + 2) + 1 + 8 * t) * BLOCK + (7 if side == 0 else 24)
+                line_ref[pl.ds(start, 8, BLOCK), :] = keep_ang[side] * (center[f] + rates[f])
 
 
 def received(place_ref, recv_ref):
@@ -283,27 +289,27 @@
 
 
 def second_kernel(
-    state_ref, inner_ref, edge_ref, ring_ref, coef_ref, recv_ref, place_ref, lat_weight_ref, lon_weight_ref,
-    next_ref, send_ref, line_ref,
+    state_ref, below_ref, above_ref, coef_ref, near_below_ref, near_above_ref, late_below_ref, late_above_ref,
+    inner_ref, edge_ref, recv_ref, place_ref, lat_weight_ref, lon_weight_ref, next_ref, send_ref,
+    line_ref, work_ref, column_ref,
 ):
     values = received(place_ref, recv_ref)
     ends = ends_of()
     for f in range(NF):
-        for r in range(-1, LV + 1):
+        for r in range(LV):
             base = (f * (LV + 2) + r + 1) * BLOCK + 8
             if 1 <= r <= LV - 2:
                 own = inner_ref[f * TILE + r * CP : f * TILE + (r + 1) * CP, :]
                 point = f * LV + r
             else:
-                e = {-1: 0, 0: 1, LV - 1: 2, LV: 3}[r]
+                e = r // (LV - 1)
                 own = edge_ref[(e * 8 + f) * CP : (e * 8 + f + 1) * CP, :]
-                point = NF * LV + (e - 1) * 8 + f
-            if 0 <= r <= LV - 1:
-                own = with_rows(own, values, point, ends)
-            line_ref[base : base + CP, :] = own
-        start = (f * (LV + 2) + 1) * BLOCK
-        line_ref[pl.ds(start + 7, LV, BLOCK), :] = ring_ref[0, f]
-        line_ref[pl.ds(start + 24, LV, BLOCK), :] = ring_ref[1, f]
+                point = NF * LV + e * 8 + f
+            line_ref[base : base + CP, :] = with_rows(own, values, point, ends)
+    surround(
+        state_ref, below_ref, above_ref, coef_ref, (near_below_ref, near_above_ref), (late_below_ref, late_above_ref),
+        work_ref, column_ref, line_ref,
+    )
 
     for r in range(LV):
         for t in range(2):
@@ -363,86 +369,68 @@
     return got.reshape(2 * n, 128)
 
 
+def call(kernel, name, outs, scratch, flops, *operands):
+    return pl.pallas_call(
+        kernel,
+        out_shape=outs,
+        in_specs=[VMEM] * len(operands),
+        out_specs=(VMEM,) * len(outs),
+        scratch_shapes=scratch,
+        compiler_params=params(),
+        cost_estimate=cost(flops),
+        name=name,
+    )(*operands)
+
+
+def rows(count):
+    return pltpu.VMEM((count, LAT), F32)
+
+
 def body(state, kappa, buoyancy, donor_lon, donor_lat, fractions):
-    where = jnp.stack(
-        [lax.axis_index(a) for a in ("panel", "rad", "ang")] + [lax.axis_size(a) for a in ("rad", "ang")]
-    ).astype(jnp.int32)
-
+    n_send = 4 * donor_lon.shape[1] // CP
     own = state.reshape(NF * TILE, LAT)
-    outer, inner = pl.pallas_call(
-        cut_kernel,
-        out_shape=(shape(2, NF, LV, LAT),) * 2,
-        in_specs=[SMEM, VMEM],
-        out_specs=(VMEM,) * 2,
-        compiler_params=params(),
-        name="cut",
-    )(where, own)
+    halo, level, late = shape(2, NF, LV, LAT), shape(NF, CP, LAT), shape(NF, LATE, LAT)
+
+    outer, inner, up, down = call(cut_kernel, "cut", (halo, halo, level, level), [], 100_000, own)
     outer = swap(outer, "ang", 1)
     inner = swap(inner, "ang", 0)
+    near_below = shift(up, "rad", 1)
+    near_above = shift(down, "rad", -1)
 
     coef = jnp.broadcast_to(jnp.concatenate([kappa, buoyancy[None]])[:, :, None], (NF + 1, LV, LAT))
-    n_send = 4 * donor_lon.shape[1] // CP
-    lat_weight, lon_weight, place = pl.pallas_call(
-        tables_kernel,
-        out_shape=(shape(LAT, n_send), shape(CP, n_send), shape(n_send, 128)),
-        in_specs=[SMEM] + [VMEM] * 3,
-        out_specs=(VMEM,) * 3,
-        compiler_params=params(),
-        cost_estimate=cost(4_000_000),
-        name="tables",
-    )(where, donor_lon, donor_lat, fractions)
+    lat_weight, lon_weight, place = call(
+        tables_kernel, "tables", (shape(LAT, n_send), shape(CP, n_send), shape(n_send, 128)), [], 4_000_000,
+        donor_lon, donor_lat, fractions,
+    )
     coef, lat_weight = lax.optimization_barrier((coef, lat_weight))
 
-    up, down, below, above = pl.pallas_call(
-        pack_kernel,
-        out_shape=(shape(NF, MESSAGE, LAT),) * 2 + (shape(2, NF, LV, LAT),) * 2,
-        in_specs=[SMEM] + [VMEM] * 4,
-        out_specs=(VMEM,) * 4,
-        compiler_params=params(),
-        name="pack",
-    )(where, own, outer, inner, coef)
-    rad_below = shift(up, "rad", 1)
-    rad_above = shift(down, "rad", -1)
-
-    middle, middle_values = pl.pallas_call(
-        first_a_kernel,
-        out_shape=(shape(NF * TILE, LAT), shape(NF * LV, n_send)),
-        in_specs=[VMEM] * 6,
-        out_specs=(VMEM,) * 2,
-        scratch_shapes=[pltpu.VMEM((NF * LV * BLOCK + 8, LAT), F32)],
-        compiler_params=params(),
-        cost_estimate=cost(60_000_000),
-        name="first_a",
-    )(own, below, above, coef, lat_weight, lon_weight)
-    edge, ring, out = pl.pallas_call(
-        first_b_kernel,
-        out_shape=(shape(4 * 8 * CP, LAT), shape(2, NF, LV, LAT), shape(n_send, 128)),
-        in_specs=[SMEM] + [VMEM] * 9,
-        out_specs=(VMEM,) * 3,
-        scratch_shapes=[
-            pltpu.VMEM((4 * NF * BLOCK + 8, LAT), F32),
-            pltpu.VMEM((2 * NF * BLOCK + 8, LAT), F32),
-        ],
-        compiler_params=params(),
-        name="first_b",
-    )(where, own, below, above, coef, rad_below, rad_above, lat_weight, lon_weight, middle_values)
+    up, down, below, above = call(
+        pack_kernel, "pack", (late, late, halo, halo), [], 100_000, own, outer, inner, coef
+    )
+    late_below = shift(up, "rad", 1)
+    late_above = shift(down, "rad", -1)
+    middle, values = call(
+        first_a_kernel, "first_a", (shape(NF * TILE, LAT), shape(NF * LV, n_send)), [rows(NF * LV * BLOCK + 8)],
+        60_000_000, own, below, above, coef, lat_weight, lon_weight,
+    )
+    edge, out = call(
+        first_b_kernel, "first_b", (shape(2 * 8 * CP, LAT), shape(n_send, 128)), [rows(2 * NF * BLOCK + 8)],
+        10_000_000, own, below, above, coef, near_below, near_above, lat_weight, lon_weight, values,
+    )
     got = exchange(out)
-    following, out = pl.pallas_call(
-        second_kernel,
-        out_shape=(shape(NF * TILE, LAT), shape(n_send, 128)),
-        in_specs=[VMEM] * 9,
-        out_specs=(VMEM,) * 2,
-        scratch_shapes=[pltpu.VMEM((NF * (LV + 2) * BLOCK + 8, LAT), F32)],
-        compiler_params=params(),
-        name="second",
-    )(own, middle, edge, ring, coef, got, place, lat_weight, lon_weight)
+    following, out = call(
+        second_kernel, "second", (shape(NF * TILE, LAT), shape(n_send, 128)),
+        [rows(NF * (LV + 2) * BLOCK + 8), rows(2 * NF * BLOCK + 8), rows(2 * NF * BLOCK + 8)], 60_000_000,
+        own, below, above, coef, near_below, near_above, late_below, late_above, middle, edge, got, place,
+        lat_weight, lon_weight,
+    )
     got = exchange(out)
     result = pl.pallas_call(
         last_kernel,
         out_shape=shape(NF * TILE, LAT),
         in_specs=[VMEM] * 3,
         out_specs=pl.BlockSpec(memory_space=pl.ANY),
-        scratch_shapes=[pltpu.VMEM((NF * TILE, LAT), F32), pltpu.SemaphoreType.DMA((NF,))],
+        scratch_shapes=[rows(NF * TILE), pltpu.SemaphoreType.DMA((NF,))],
         compiler_params=params(),
         name="last",
     )(following, got, place)

time: 65.4 us -> 67.4 us (1.031)
  the two profiles are of different devices: /device:TPU:193 before, /device:TPU:65 now
where the time goes in v4:
time: 67.4 us; the launch traced here: 67 us
  starting transfers between devices  30.9 us (46%)
  blocking collectives  21.3 us (32%)
  Pallas kernels  7.47 us (11%)
  waiting for transfers between devices  5.11 us (8%)
  local copies, waits for them, and re-layouts  1.28 us (2%)
  other arithmetic  0.7 us (1%)
    all_to_all x1, blocking collectives, exchange(): lax.all_to_all(values.reshape(n, 2, 128), ('panel', 'ang'), 0, 0, tiled=T...  21.3 us
    ppermute x4, starting transfers between devices, shift(): return lax.ppermute(value, axis, pairs)  16.3 us
    all_to_all x1, starting transfers between devices, exchange(): lax.all_to_all(values.reshape(n, 2, 128), ('panel', 'ang'), 0, 0, tiled=T...  8.84 us
    pallas_call x6, Pallas kernels, call(): pl.pallas_call(kernel, out_shape=outs, in_specs=[VMEM] * len(operands), o...  5.86 us
    ppermute x2, starting transfers between devices, swap(): lax.ppermute(value, axis, [(i, i + 1) for i in low] + [(i + 1, i) for i i...  5.82 us
    ppermute x4, waiting for transfers between devices, shift(): return lax.ppermute(value, axis, pairs)  5.1 us
    pallas_call x1, Pallas kernels, body(): pl.pallas_call(last_kernel, out_shape=shape(NF * TILE, LAT), in_specs=[VM...  1.61 us
  transfers between devices with their start and end apart: 7, of which 1 were waited for; matrix products, arithmetic and copies ran while one was open for 1% of the time, Pallas kernels for 3%

profile of v4, /device:TPU:65, one launch (start us, length us, event | category | flops | bytes accessed | tf_op | source)
XLA Modules:
  0.0 67.0 jit_solution(1089273366772386549)
XLA Ops:
  0.0 0.0 copy-start
  0.0 1.2 %copy-done = f32[1,7,16,16,128]{4,3,2,1,0:T(8,128)S(1)} copy-done((f32[1,7,16,16,128]{4,3,2,1,0:T(8,128)S(1)}, f32[1,7,16,16,128]{4,3,2,1,0:T(8,128)}, u32[]{:S(2)}) %copy-start) | copy-done | bytes 917528
  1.2 0.0 copy-start.5
  1.2 0.0 copy-start.1
  1.2 0.1 cut.1
  1.3 0.0 copy-start.2
  1.3 3.9 %collective-permute-start = (f32[2,7,16,128]{3,2,1,0:T(8,128)S(1)}, f32[2,7,16,128]{3,2,1,0:T(8,128)S(1)}, u32[]{:S(2)}, u32[]{:S(2)}) collective-permute-start(f32[2,7,16,128]{3,2,1,0:T(8,128)S(1)} %get-tuple-element.24), channel_id=1, source_target_pairs={{1,2},{3,4},{5,6},{7,8},{9,10},{11,12},{13,14},{15,16},{17,18},{19... | collective-permute-start | bytes 344072 | tf_op jit(solution)/shard_map/ppermute | solution.py:363
  5.2 1.9 %collective-permute-start.1 = (f32[2,7,16,128]{3,2,1,0:T(8,128)S(1)}, f32[2,7,16,128]{3,2,1,0:T(8,128)S(1)}, u32[]{:S(2)}, u32[]{:S(2)}) collective-permute-start(f32[2,7,16,128]{3,2,1,0:T(8,128)S(1)} %get-tuple-element.25), channel_id=1, source_target_pairs={{0,1},{2,3},{4,5},{6,7},{8,9},{10,11},{12,13},{14,15},{16,17},{18,... | collective-permute-start | bytes 344072 | tf_op jit(solution)/shard_map/ppermute | solution.py:363
  7.1 4.0 %collective-permute-start.2 = (f32[7,16,128]{2,1,0:T(8,128)S(1)}, f32[7,16,128]{2,1,0:T(8,128)S(1)}, u32[]{:S(2)}, u32[]{:S(2)}) collective-permute-start(f32[7,16,128]{2,1,0:T(8,128)S(1)} %get-tuple-element.30), channel_id=1, source_target_pairs={{0,32},{32,64},{64,96},{96,128},{128,160},{160,192},{192,224},{224... | collective-permute-start | bytes 172040 | tf_op jit(solution)/shard_map/ppermute | solution.py:357
  11.1 5.2 %collective-permute-start.3 = (f32[7,16,128]{2,1,0:T(8,128)S(1)}, f32[7,16,128]{2,1,0:T(8,128)S(1)}, u32[]{:S(2)}, u32[]{:S(2)}) collective-permute-start(f32[7,16,128]{2,1,0:T(8,128)S(1)} %get-tuple-element.31), channel_id=1, source_target_pairs={{32,0},{64,32},{96,64},{128,96},{160,128},{192,160},{224,192},{256... | collective-permute-start | bytes 172040 | tf_op jit(solution)/shard_map/ppermute | solution.py:357
  16.3 0.0 copy-done.5
  16.3 0.0 copy-start.3
  16.3 0.0 copy-start.4
  16.3 0.7 %pad_maximum_fusion = f32[8,16]{1,0:T(8,128)S(1)} fusion(f32[1,16]{1,0:T(1,128)S(1)} %bitcast.15, f32[7,16]{1,0:T(8,128)} %param.7), kind=kLoop, calls=%fused_computation | loop fusion | flops 128 | bytes 1024 | tf_op jit(solution)/shard_map/concatenate | solution.py:400
  17.0 0.0 copy-done.2
  17.0 0.0 copy-done.3
  17.0 0.0 copy-done.4
  17.0 0.4 tables.1
  17.4 0.1 broadcast_in_dim.10.coef_ref
  17.5 0.0 collective-permute-done.outer_ref
  17.5 0.0 collective-permute-done.1.inner_ref
  17.5 0.0 copy-done.1
  17.6 1.6 %first_a.1 = (f32[1792,128]{1,0:T(8,128)S(1)}, f32[112,128]{1,0:T(8,128)S(1)}) custom-call(f32[1792,128]{1,0:T(8,128)S(1)} %bitcast.9, f32[2,7,16,128]{3,2,1,0:T(8,128)S(1)} %get-tuple-element.28.below_ref, f32[2,7,16,128]{3,2,1,0:T(8,128)S(1)} %get-tuple-element.29.above_ref, f32[8,16,128]{2,1,0:T(8,128)S(1)} %broadcast_in_dim.10.coef_ref, ...), custom_call_target="tpu_custom_call" | custom-call | flops 60000000 | bytes 2000000 | tf_op jit(solution)/shard_map/first_a/pallas_call | solution.py:373
  19.2 0.0 collective-permute-done.2.near_below_ref
  19.2 0.0 collective-permute-done.3.near_above_ref
  19.2 1.1 %first_b.1 = (f32[256,128]{1,0:T(8,128)S(1)}, f32[128,128]{1,0:T(8,128)}) custom-call(f32[1792,128]{1,0:T(8,128)S(1)} %bitcast.10, f32[2,7,16,128]{3,2,1,0:T(8,128)S(1)} %get-tuple-element.28.below_ref, f32[2,7,16,128]{3,2,1,0:T(8,128)S(1)} %get-tuple-element.29.above_ref, f32[8,16,128]{2,1,0:T(8,128)S(1)} %broadcast_in_dim.10.coef_ref, ...), custom_call_target="tpu_custom_call" | custom-call | flops 10000000 | bytes 2000000 | tf_op jit(solution)/shard_map/first_b/pallas_call | solution.py:373
  20.3 8.8 %all-to-all-start = ((f32[64,2,128]{2,1,0:T(2,128)}), f32[64,2,128]{2,1,0:T(2,128)S(1)}, u32[]{:S(2)}, u32[]{:S(2)}) async-start(f32[64,2,128]{2,1,0:T(2,128)} %bitcast.2), calls=%async_computation | async-start | bytes 131072 | tf_op jit(solution)/shard_map/all_to_all | solution.py:368
  29.1 5.2 %collective-permute-start.4 = (f32[7,24,128]{2,1,0:T(8,128)S(1)}, f32[7,24,128]{2,1,0:T(8,128)S(1)}, u32[]{:S(2)}, u32[]{:S(2)}) collective-permute-start(f32[7,24,128]{2,1,0:T(8,128)S(1)} %get-tuple-element.32), channel_id=1, source_target_pairs={{0,32},{32,64},{64,96},{96,128},{128,160},{160,192},{192,224},{224... | collective-permute-start | bytes 258056 | tf_op jit(solution)/shard_map/ppermute | solution.py:357
  34.4 1.9 %collective-permute-start.5 = (f32[7,24,128]{2,1,0:T(8,128)S(1)}, f32[7,24,128]{2,1,0:T(8,128)S(1)}, u32[]{:S(2)}, u32[]{:S(2)}) collective-permute-start(f32[7,24,128]{2,1,0:T(8,128)S(1)} %get-tuple-element.33), channel_id=1, source_target_pairs={{32,0},{64,32},{96,64},{128,96},{160,128},{192,160},{224,192},{256... | collective-permute-start | bytes 258056 | tf_op jit(solution)/shard_map/ppermute | solution.py:357
  36.3 0.0 collective-permute-done.4.late_below_ref
  36.3 5.1 %collective-permute-done.5.late_above_ref = f32[7,24,128]{2,1,0:T(8,128)S(1)} collective-permute-done((f32[7,24,128]{2,1,0:T(8,128)S(1)}, f32[7,24,128]{2,1,0:T(8,128)S(1)}, u32[]{:S(2)}, u32[]{:S(2)}) %collective-permute-start.5) | collective-permute-done | bytes 86048 | tf_op jit(solution)/shard_map/ppermute | solution.py:357
  41.4 0.0 all-to-all-done
  41.4 2.7 %second.1 = (f32[1792,128]{1,0:T(8,128)S(1)}, f32[128,128]{1,0:T(8,128)S(1)}) custom-call(f32[1792,128]{1,0:T(8,128)S(1)} %bitcast.11, f32[2,7,16,128]{3,2,1,0:T(8,128)S(1)} %get-tuple-element.28.below_ref, f32[2,7,16,128]{3,2,1,0:T(8,128)S(1)} %get-tuple-element.29.above_ref, f32[8,16,128]{2,1,0:T(8,128)S(1)} %broadcast_in_dim.10.coef_ref, ...), custom_call_target="tpu_custom_call" | custom-call | flops 60000000 | bytes 2000000 | tf_op jit(solution)/shard_map/second/pallas_call | solution.py:373
  44.1 21.3 %all_to_all.10 = f32[64,2,128]{2,1,0:T(2,128)S(1)} all-to-all(f32[64,2,128]{2,1,0:T(2,128)S(1)} %bitcast.14), channel_id=1, replica_groups=mesh['panel'=2,'rad'=12,'ang'=32] {'panel','ang'}, dimensions={0} | all-to-all | bytes 131072 | tf_op jit(solution)/shard_map/all_to_all | solution.py:368
  65.4 1.6 %last.1 = f32[1792,128]{1,0:T(8,128)} custom-call(f32[1792,128]{1,0:T(8,128)S(1)} %get-tuple-element.41.next_ref, f32[128,128]{1,0:T(8,128)S(1)} %bitcast.13, f32[128,128]{1,0:T(8,128)S(1)} %get-tuple-element.40.place_ref), custom_call_target="tpu_custom_call" | custom-call | tf_op jit(solution)/shard_map/last/pallas_call | solution.py:428
  (1 shorter events, 0.0 us)
Async XLA Ops:
  0.0 1.2 %copy-start = (f32[1,7,16,16,128]{4,3,2,1,0:T(8,128)S(1)}, f32[1,7,16,16,128]{4,3,2,1,0:T(8,128)}, u32[]{:S(2)}) copy-start(f32[1,7,16,16,128]{4,3,2,1,0:T(8,128)} %param.6) | copy-start | bytes 2752516
  1.2 15.1 %copy-start.5 = (f32[16]{0:T(128)S(1)}, f32[16]{0:T(128)}, u32[]{:S(2)}) copy-start(f32[16]{0:T(128)} %param.8) | copy-start | bytes 196
  1.2 16.3 %copy-start.1 = (f32[1,7,16,16,128]{4,3,2,1,0:T(8,128)S(1)}, f32[1,7,16,16,128]{4,3,2,1,0:T(8,128)}, u32[]{:S(2)}) copy-start(f32[1,7,16,16,128]{4,3,2,1,0:T(8,128)} %param.6) | copy-start | bytes 2752516
  1.3 15.8 %copy-start.2 = (f32[2,2,512]{2,1,0:T(2,128)S(1)}, f32[2,2,512]{2,1,0:T(2,128)}, u32[]{:S(2)}) copy-start(f32[2,2,512]{2,1,0:T(2,128)} %frac_ref.1) | copy-start | bytes 24580
  1.3 16.2 %collective-permute-start = (f32[2,7,16,128]{3,2,1,0:T(8,128)S(1)}, f32[2,7,16,128]{3,2,1,0:T(8,128)S(1)}, u32[]{:S(2)}, u32[]{:S(2)}) collective-permute-start(f32[2,7,16,128]{3,2,1,0:T(8,128)S(1)} %get-tuple-element.24), channel_id=1, source_target_pairs={{1,2},{3,4},{5,6},{7,8},{9,10},{11,12},{13,14},{15,16},{17,18},{19... | collective-permute-start | bytes 344072 | tf_op jit(solution)/shard_map/ppermute | solution.py:363
  5.2 12.3 %collective-permute-start.1 = (f32[2,7,16,128]{3,2,1,0:T(8,128)S(1)}, f32[2,7,16,128]{3,2,1,0:T(8,128)S(1)}, u32[]{:S(2)}, u32[]{:S(2)}) collective-permute-start(f32[2,7,16,128]{3,2,1,0:T(8,128)S(1)} %get-tuple-element.25), channel_id=1, source_target_pairs={{0,1},{2,3},{4,5},{6,7},{8,9},{10,11},{12,13},{14,15},{16,17},{18,... | collective-permute-start | bytes 344072 | tf_op jit(solution)/shard_map/ppermute | solution.py:363
  7.1 12.1 %collective-permute-start.2 = (f32[7,16,128]{2,1,0:T(8,128)S(1)}, f32[7,16,128]{2,1,0:T(8,128)S(1)}, u32[]{:S(2)}, u32[]{:S(2)}) collective-permute-start(f32[7,16,128]{2,1,0:T(8,128)S(1)} %get-tuple-element.30), channel_id=1, source_target_pairs={{0,32},{32,64},{64,96},{96,128},{128,160},{160,192},{192,224},{224... | collective-permute-start | bytes 172040 | tf_op jit(solution)/shard_map/ppermute | solution.py:357
  11.1 8.1 %collective-permute-start.3 = (f32[7,16,128]{2,1,0:T(8,128)S(1)}, f32[7,16,128]{2,1,0:T(8,128)S(1)}, u32[]{:S(2)}, u32[]{:S(2)}) collective-permute-start(f32[7,16,128]{2,1,0:T(8,128)S(1)} %get-tuple-element.31), channel_id=1, source_target_pairs={{32,0},{64,32},{96,64},{128,96},{160,128},{192,160},{224,192},{256... | collective-permute-start | bytes 172040 | tf_op jit(solution)/shard_map/ppermute | solution.py:357
  16.3 0.7 %copy-start.3 = (s32[2,512]{1,0:T(2,128)S(1)}, s32[2,512]{1,0:T(2,128)}, u32[]{:S(2)}) copy-start(s32[2,512]{1,0:T(2,128)} %lon_ref.1) | copy-start | bytes 12292
  16.3 0.7 %copy-start.4 = (s32[2,512]{1,0:T(2,128)S(1)}, s32[2,512]{1,0:T(2,128)}, u32[]{:S(2)}) copy-start(s32[2,512]{1,0:T(2,128)} %lat_ref.1) | copy-start | bytes 12292
  20.3 21.1 %all-to-all-start = ((f32[64,2,128]{2,1,0:T(2,128)}), f32[64,2,128]{2,1,0:T(2,128)S(1)}, u32[]{:S(2)}, u32[]{:S(2)}) async-start(f32[64,2,128]{2,1,0:T(2,128)} %bitcast.2), calls=%async_computation | async-start | bytes 131072 | tf_op jit(solution)/shard_map/all_to_all | solution.py:368
  29.1 7.2 %collective-permute-start.4 = (f32[7,24,128]{2,1,0:T(8,128)S(1)}, f32[7,24,128]{2,1,0:T(8,128)S(1)}, u32[]{:S(2)}, u32[]{:S(2)}) collective-permute-start(f32[7,24,128]{2,1,0:T(8,128)S(1)} %get-tuple-element.32), channel_id=1, source_target_pairs={{0,32},{32,64},{64,96},{96,128},{128,160},{160,192},{192,224},{224... | collective-permute-start | bytes 258056 | tf_op jit(solution)/shard_map/ppermute | solution.py:357
  34.4 7.0 %collective-permute-start.5 = (f32[7,24,128]{2,1,0:T(8,128)S(1)}, f32[7,24,128]{2,1,0:T(8,128)S(1)}, u32[]{:S(2)}, u32[]{:S(2)}) collective-permute-start(f32[7,24,128]{2,1,0:T(8,128)S(1)} %get-tuple-element.33), channel_id=1, source_target_pairs={{32,0},{64,32},{96,64},{128,96},{160,128},{192,160},{224,192},{256... | collective-permute-start | bytes 258056 | tf_op jit(solution)/shard_map/ppermute | solution.py:357

commit v5 on v4

--- a/solution.py
+++ b/solution.py
@@ -16,7 +16,7 @@
 LAT = 128
 TILE = LV * CP
 BLOCK = 24
-LATE = 24
+MESSAGE = 40
 
 
 def params():
@@ -83,8 +83,8 @@
     target = jnp.where(pick >= 0, target, -1)
     lane = lax.broadcasted_iota(jnp.int32, (half, 128), 1)
     place = jnp.where(lane == target, 1.0, 0.0)
-    place_ref[0:half, :] = place * panel.astype(F32)
-    place_ref[half : 2 * half, :] = place * (1 - panel).astype(F32)
+    place = jnp.concatenate([place * panel.astype(F32), place * (1 - panel).astype(F32)], axis=0)
+    place_ref[...] = jnp.transpose(place)[0 : 2 * CP]
 
 
 def increments(center, neighbours, kappa, buoyancy, scale):
@@ -111,7 +111,7 @@
     return jnp.sum(along.reshape(n, CP, along.shape[1]) * lon_weight_ref[...][None], axis=1)
 
 
-def cut_kernel(state_ref, outer_ref, inner_ref, up_ref, down_ref):
+def cut_kernel(state_ref, outer_ref, inner_ref):
     odd = lax.axis_index("ang") % 2 == 1
     for f in range(NF):
         for i in range(2):
@@ -119,8 +119,6 @@
             high = state_ref[pl.ds(f * TILE + CP - 1 - i, LV, CP), :]
             outer_ref[i, f] = jnp.where(odd, high, low)
             inner_ref[i, f] = jnp.where(odd, low, high)
-        up_ref[f] = state_ref[(f + 1) * TILE - CP : (f + 1) * TILE, :]
-        down_ref[f] = state_ref[f * TILE : f * TILE + CP, :]
 
 
 def pack_kernel(state_ref, outer_ref, inner_ref, coef_ref, up_ref, down_ref, below_ref, above_ref):
@@ -132,12 +130,13 @@
     for ref, near, far in ((up_ref, LV - 1, LV - 2), (down_ref, 0, 1)):
         for f in range(NF):
             start = f * TILE
-            ref[f, 0:CP, :] = state_ref[start + far * CP : start + (far + 1) * CP, :]
-            ref[f, 16:17, :] = above_ref[0, f, near : near + 1, :]
-            ref[f, 17:18, :] = below_ref[0, f, near : near + 1, :]
-            ref[f, 18:19, :] = coef_ref[f, near : near + 1, :]
-            ref[f, 19:20, :] = coef_ref[NF, near : near + 1, :]
-            ref[f, 20:24, :] = jnp.zeros((4, LAT), F32)
+            ref[f, 0:CP, :] = state_ref[start + near * CP : start + (near + 1) * CP, :]
+            ref[f, CP : 2 * CP, :] = state_ref[start + far * CP : start + (far + 1) * CP, :]
+            ref[f, 32:33, :] = above_ref[0, f, near : near + 1, :]
+            ref[f, 33:34, :] = below_ref[0, f, near : near + 1, :]
+            ref[f, 34:35, :] = coef_ref[f, near : near + 1, :]
+            ref[f, 35:36, :] = coef_ref[NF, near : near + 1, :]
+            ref[f, 36:40, :] = jnp.zeros((4, LAT), F32)
 
 
 def first_a_kernel(
@@ -176,7 +175,7 @@
 
 
 def first_b_kernel(
-    state_ref, below_ref, above_ref, coef_ref, near_below_ref, near_above_ref, lat_weight_ref, lon_weight_ref,
+    state_ref, below_ref, above_ref, coef_ref, rad_below_ref, rad_above_ref, lat_weight_ref, lon_weight_ref,
     values_ref, edge_ref, send_ref, line_ref,
 ):
     for e, r in enumerate((0, LV - 1)):
@@ -194,9 +193,9 @@
             def neighbours(f):
                 line = (e * NF + f) * BLOCK + 8 + 8 * t
                 if e == 0:
-                    up, down = own(f, 1), near_below_ref[f, 8 * t : 8 * t + 8, :]
+                    up, down = own(f, 1), rad_below_ref[f, 8 * t : 8 * t + 8, :]
                 else:
-                    up, down = near_above_ref[f, 8 * t : 8 * t + 8, :], own(f, LV - 2)
+                    up, down = rad_above_ref[f, 8 * t : 8 * t + 8, :], own(f, LV - 2)
                 return up, down, line_ref[line + 1 : line + 9, :], line_ref[line - 1 : line + 7, :]
 
             center = [own(f, r) for f in range(NF)]
@@ -212,39 +211,39 @@
 
 
 def surround(
-    state_ref, below_ref, above_ref, coef_ref, near_refs, late_refs, work_ref, column_ref, line_ref
+    state_ref, below_ref, above_ref, coef_ref, rad_refs, work_ref, column_ref, line_ref
 ):
     rad, ang = lax.axis_index("rad"), lax.axis_index("ang")
     keep_rad = [jnp.where(rad == 0, 0.0, 1.0), jnp.where(rad == lax.axis_size("rad") - 1, 0.0, 1.0)]
     keep_ang = [jnp.where(ang == 0, 0.0, 1.0), jnp.where(ang == lax.axis_size("ang") - 1, 0.0, 1.0)]
     for e in range(2):
-        late = late_refs[e]
+        source = rad_refs[e]
         for f in range(NF):
             base = (e * NF + f) * BLOCK + 8
-            work_ref[base : base + CP, :] = near_refs[e][f]
-            work_ref[base - 1 : base, :] = late[f, 17:18, :]
-            work_ref[base + CP : base + CP + 1, :] = late[f, 16:17, :]
+            work_ref[base : base + CP, :] = source[f, 0:CP, :]
+            work_ref[base - 1 : base, :] = source[f, 33:34, :]
+            work_ref[base + CP : base + CP + 1, :] = source[f, 32:33, :]
     for side, ref in ((0, below_ref), (1, above_ref)):
         for f in range(NF):
             base = (side * NF + f) * BLOCK + 8
             column_ref[base : base + LV, :] = ref[0, f]
-            column_ref[base - 1 : base, :] = late_refs[0][f, 17 - side : 18 - side, :]
-            column_ref[base + LV : base + LV + 1, :] = late_refs[1][f, 17 - side : 18 - side, :]
+            column_ref[base - 1 : base, :] = rad_refs[0][f, 33 - side : 34 - side, :]
+            column_ref[base + LV : base + LV + 1, :] = rad_refs[1][f, 33 - side : 34 - side, :]
 
     for e in range(2):
-        late = late_refs[e]
+        source = rad_refs[e]
         for t in range(2):
             part = slice(8 * t, 8 * t + 8)
 
             def neighbours(f):
                 line = (e * NF + f) * BLOCK + 8 + 8 * t
                 start = f * TILE + e * (LV - 1) * CP + 8 * t
-                inside, outside = state_ref[start : start + 8, :], late[f, part, :]
+                inside, outside = state_ref[start : start + 8, :], source[f, CP + 8 * t : CP + 8 * t + 8, :]
                 up, down = (inside, outside) if e == 0 else (outside, inside)
                 return up, down, work_ref[line + 1 : line + 9, :], work_ref[line - 1 : line + 7, :]
 
-            center = [near_refs[e][f, part, :] for f in range(NF)]
-            rates = increments(center, neighbours, lambda f: late[f, 18:19, :], late[0, 19:20, :], step_size)
+            center = [source[f, part, :] for f in range(NF)]
+            rates = increments(center, neighbours, lambda f: source[f, 34:35, :], source[0, 35:36, :], step_size)
             for f in range(NF):
                 base = (f * (LV + 2) + e * (LV + 1)) * BLOCK + 8 + 8 * t
                 line_ref[base : base + 8, :] = keep_rad[e] * (center[f] + rates[f])
@@ -267,13 +266,13 @@
                 line_ref[pl.ds(start, 8, BLOCK), :] = keep_ang[side] * (center[f] + rates[f])
 
 
-def received(place_ref, recv_ref):
-    values = lax.dot_general(
-        place_ref[...], recv_ref[...], (((0,), (0,)), ((), ())), precision=HIGHEST, preferred_element_type=F32
-    )
-    low, high = values[0:CP], pltpu.roll(values[CP : 2 * CP], LAT - 1, 1)
-    even = (lax.broadcasted_iota(jnp.int32, (CP, LAT), 1) & 1) == 0
-    return jnp.where(even, low, high), jnp.where(even, high, low)
+def received(place_ref, recv_ref, edge):
+    values = jnp.dot(place_ref[...], recv_ref[...], precision=HIGHEST, preferred_element_type=F32)
+    low, high = values[0:CP], pltpu.roll(values[CP : 2 * CP], LAT - 1 - edge, 1)
+    if edge:
+        low = pltpu.roll(low, edge, 1)
+    first = (lax.broadcasted_iota(jnp.int32, (CP, LAT), 1) & 1) == edge & 1
+    return jnp.where(first, low, high), jnp.where(first, high, low)
 
 
 def with_rows(own, values, point, ends):
@@ -283,32 +282,29 @@
     return jnp.where(ends, rows, own)
 
 
-def ends_of():
+def ends_of(edge):
     lane = lax.broadcasted_iota(jnp.int32, (CP, LAT), 1)
-    return (lane == 0) | (lane == LAT - 1)
-
-
-def second_kernel(
-    state_ref, below_ref, above_ref, coef_ref, near_below_ref, near_above_ref, late_below_ref, late_above_ref,
-    inner_ref, edge_ref, recv_ref, place_ref, lat_weight_ref, lon_weight_ref, next_ref, send_ref,
+    return (lane == edge) | (lane == LAT - 1 - edge)
+
+
+def first_at(inner_ref, edge_ref, f, r):
+    if 1 <= r <= LV - 2:
+        return inner_ref[f * TILE + r * CP : f * TILE + (r + 1) * CP, :], f * LV + r
+    e = r // (LV - 1)
+    return edge_ref[(e * 8 + f) * CP : (e * 8 + f + 1) * CP, :], NF * LV + e * 8 + f
+
+
+def second_a_kernel(
+    state_ref, below_ref, above_ref, coef_ref, rad_below_ref, rad_above_ref, inner_ref, edge_ref, next_ref,
     line_ref, work_ref, column_ref,
 ):
-    values = received(place_ref, recv_ref)
-    ends = ends_of()
+    ends = ends_of(0)
     for f in range(NF):
         for r in range(LV):
             base = (f * (LV + 2) + r + 1) * BLOCK + 8
-            if 1 <= r <= LV - 2:
-                own = inner_ref[f * TILE + r * CP : f * TILE + (r + 1) * CP, :]
-                point = f * LV + r
-            else:
-                e = r // (LV - 1)
-                own = edge_ref[(e * 8 + f) * CP : (e * 8 + f + 1) * CP, :]
-                point = NF * LV + e * 8 + f
-            line_ref[base : base + CP, :] = with_rows(own, values, point, ends)
+            line_ref[base : base + CP, :] = jnp.where(ends, 0.0, first_at(inner_ref, edge_ref, f, r)[0])
     surround(
-        state_ref, below_ref, above_ref, coef_ref, (near_below_ref, near_above_ref), (late_below_ref, late_above_ref),
-        work_ref, column_ref, line_ref,
+        state_ref, below_ref, above_ref, coef_ref, (rad_below_ref, rad_above_ref), work_ref, column_ref, line_ref
     )
 
     for r in range(LV):
@@ -332,13 +328,36 @@
             for f in range(NF):
                 row = f * TILE + r * CP + 8 * t
                 next_ref[row : row + 8, :] = 0.5 * (state_ref[row : row + 8, :] + center[f]) + rates[f]
+
+
+def second_b_kernel(
+    before_ref, inner_ref, edge_ref, coef_ref, recv_ref, place_ref, lat_weight_ref, lon_weight_ref,
+    next_ref, send_ref,
+):
+    values = received(place_ref, recv_ref, 1)
+    beside = ends_of(1)
+    lane = lax.broadcasted_iota(jnp.int32, (CP, LAT), 1)
+    quarter = jnp.where(lane == 1, 0.25 * step_size, -0.25 * step_size)
+    for r in range(LV):
+        u = quarter * first_at(inner_ref, edge_ref, 2, r)[0]
+        b = quarter * first_at(inner_ref, edge_ref, 5, r)[0]
+        rows = [
+            with_rows(jnp.zeros((CP, LAT), F32), values, first_at(inner_ref, edge_ref, f, r)[1], beside)
+            for f in range(NF)
+        ]
+        for f in range(NF):
+            gain = ((0.5 * step_size) * coef_ref[f, r : r + 1, :] + u) * rows[f]
+            if f < 6:
+                gain = gain - b * rows[(f + 3) % 6]
+            row = f * TILE + r * CP
+            next_ref[row : row + CP, :] = before_ref[row : row + CP, :] + gain
     donors = interpolate(next_ref[...], lat_weight_ref, lon_weight_ref)
     send_ref[...] = jnp.transpose(jnp.concatenate([donors, jnp.zeros((128 - NF * LV, 128), F32)], axis=0))
 
 
 def last_kernel(next_ref, recv_ref, place_ref, out_ref, done_ref, sems):
-    values = received(place_ref, recv_ref)
-    ends = ends_of()
+    values = received(place_ref, recv_ref, 0)
+    ends = ends_of(0)
     copies = []
     for f in range(NF):
         for r in range(LV):
@@ -389,40 +408,41 @@
 def body(state, kappa, buoyancy, donor_lon, donor_lat, fractions):
     n_send = 4 * donor_lon.shape[1] // CP
     own = state.reshape(NF * TILE, LAT)
-    halo, level, late = shape(2, NF, LV, LAT), shape(NF, CP, LAT), shape(NF, LATE, LAT)
-
-    outer, inner, up, down = call(cut_kernel, "cut", (halo, halo, level, level), [], 100_000, own)
+    halo, message = shape(2, NF, LV, LAT), shape(NF, MESSAGE, LAT)
+
+    outer, inner = call(cut_kernel, "cut", (halo, halo), [], 100_000, own)
     outer = swap(outer, "ang", 1)
     inner = swap(inner, "ang", 0)
-    near_below = shift(up, "rad", 1)
-    near_above = shift(down, "rad", -1)
 
     coef = jnp.broadcast_to(jnp.concatenate([kappa, buoyancy[None]])[:, :, None], (NF + 1, LV, LAT))
     lat_weight, lon_weight, place = call(
-        tables_kernel, "tables", (shape(LAT, n_send), shape(CP, n_send), shape(n_send, 128)), [], 4_000_000,
+        tables_kernel, "tables", (shape(LAT, n_send), shape(CP, n_send), shape(2 * CP, n_send)), [], 4_000_000,
         donor_lon, donor_lat, fractions,
     )
     coef, lat_weight = lax.optimization_barrier((coef, lat_weight))
 
     up, down, below, above = call(
-        pack_kernel, "pack", (late, late, halo, halo), [], 100_000, own, outer, inner, coef
-    )
-    late_below = shift(up, "rad", 1)
-    late_above = shift(down, "rad", -1)
+        pack_kernel, "pack", (message, message, halo, halo), [], 100_000, own, outer, inner, coef
+    )
+    rad_below = shift(up, "rad", 1)
+    rad_above = shift(down, "rad", -1)
     middle, values = call(
         first_a_kernel, "first_a", (shape(NF * TILE, LAT), shape(NF * LV, n_send)), [rows(NF * LV * BLOCK + 8)],
         60_000_000, own, below, above, coef, lat_weight, lon_weight,
     )
     edge, out = call(
         first_b_kernel, "first_b", (shape(2 * 8 * CP, LAT), shape(n_send, 128)), [rows(2 * NF * BLOCK + 8)],
-        10_000_000, own, below, above, coef, near_below, near_above, lat_weight, lon_weight, values,
+        10_000_000, own, below, above, coef, rad_below, rad_above, lat_weight, lon_weight, values,
     )
     got = exchange(out)
+    (before,) = call(
+        second_a_kernel, "second_a", (shape(NF * TILE, LAT),),
+        [rows(NF * (LV + 2) * BLOCK + 8), rows(2 * NF * BLOCK + 8), rows(2 * NF * BLOCK + 8)], 60_000_000,
+        own, below, above, coef, rad_below, rad_above, middle, edge,
+    )
     following, out = call(
-        second_kernel, "second", (shape(NF * TILE, LAT), shape(n_send, 128)),
-        [rows(NF * (LV + 2) * BLOCK + 8), rows(2 * NF * BLOCK + 8), rows(2 * NF * BLOCK + 8)], 60_000_000,
-        own, below, above, coef, near_below, near_above, late_below, late_above, middle, edge, got, place,
-        lat_weight, lon_weight,
+        second_b_kernel, "second_b", (shape(NF * TILE, LAT), shape(n_send, 128)), [], 30_000_000,
+        before, middle, edge, coef, got, place, lat_weight, lon_weight,
     )
     got = exchange(out)
     result = pl.pallas_call(

time: 67.4 us -> 64.4 us (0.955)
  the two profiles are of different devices: /device:TPU:65 before, /device:TPU:193 now
where the time goes in v5:
time: 64.4 us; the launch traced here: 63.9 us
  starting transfers between devices  24.6 us (38%)
  blocking collectives  14 us (22%)
  waiting for transfers between devices  12.9 us (20%)
  Pallas kernels  8.35 us (13%)
  local copies, waits for them, and re-layouts  3.98 us (6%)
    all_to_all x1, blocking collectives, exchange(): lax.all_to_all(values.reshape(n, 2, 128), ('panel', 'ang'), 0, 0, tiled=T...  14 us
    all_to_all x1, starting transfers between devices, exchange(): lax.all_to_all(values.reshape(n, 2, 128), ('panel', 'ang'), 0, 0, tiled=T...  11.7 us
    all_to_all x1, waiting for transfers between devices, exchange(): lax.all_to_all(values.reshape(n, 2, 128), ('panel', 'ang'), 0, 0, tiled=T...  8.84 us
    ppermute x2, starting transfers between devices, shift(): return lax.ppermute(value, axis, pairs)  7.13 us
    pallas_call x7, Pallas kernels, call(): pl.pallas_call(kernel, out_shape=outs, in_specs=[VMEM] * len(operands), o...  6.84 us
    ppermute x2, starting transfers between devices, swap(): lax.ppermute(value, axis, [(i, i + 1) for i in low] + [(i + 1, i) for i i...  5.82 us
    ppermute x2, waiting for transfers between devices, shift(): return lax.ppermute(value, axis, pairs)  4.05 us
    unnamed x14, local copies, waits for them, and re-layouts  3.9 us
  transfers between devices with their start and end apart: 5, of which 2 were waited for; matrix products, arithmetic and copies ran while one was open for 0% of the time, Pallas kernels for 5%

profile of v5, /device:TPU:193, one launch (start us, length us, event | category | flops | bytes accessed | tf_op | source)
XLA Modules:
  0.0 63.9 jit_solution(7884879090127325164)
XLA Ops:
  0.0 0.0 copy-start
  0.0 1.2 %copy-done = f32[1,7,16,16,128]{4,3,2,1,0:T(8,128)S(1)} copy-done((f32[1,7,16,16,128]{4,3,2,1,0:T(8,128)S(1)}, f32[1,7,16,16,128]{4,3,2,1,0:T(8,128)}, u32[]{:S(2)}) %copy-start) | copy-done | bytes 917528
  1.2 0.0 copy-start.1
  1.2 0.1 cut.1
  1.3 3.9 %collective-permute-start = (f32[2,7,16,128]{3,2,1,0:T(8,128)S(1)}, f32[2,7,16,128]{3,2,1,0:T(8,128)S(1)}, u32[]{:S(2)}, u32[]{:S(2)}) collective-permute-start(f32[2,7,16,128]{3,2,1,0:T(8,128)S(1)} %get-tuple-element.22), channel_id=1, source_target_pairs={{1,2},{3,4},{5,6},{7,8},{9,10},{11,12},{13,14},{15,16},{17,18},{19... | collective-permute-start | bytes 344072 | tf_op jit(solution)/shard_map/ppermute | solution.py:382
  5.2 1.9 %collective-permute-start.1 = (f32[2,7,16,128]{3,2,1,0:T(8,128)S(1)}, f32[2,7,16,128]{3,2,1,0:T(8,128)S(1)}, u32[]{:S(2)}, u32[]{:S(2)}) collective-permute-start(f32[2,7,16,128]{3,2,1,0:T(8,128)S(1)} %get-tuple-element.23), channel_id=1, source_target_pairs={{0,1},{2,3},{4,5},{6,7},{8,9},{10,11},{12,13},{14,15},{16,17},{18,... | collective-permute-start | bytes 344072 | tf_op jit(solution)/shard_map/ppermute | solution.py:382
  7.1 0.0 copy-start.2
  7.1 0.7 %copy-done.2 = f32[2,2,512]{2,1,0:T(2,128)S(1)} copy-done((f32[2,2,512]{2,1,0:T(2,128)S(1)}, f32[2,2,512]{2,1,0:T(2,128)}, u32[]{:S(2)}) %copy-start.2) | copy-done | bytes 8216
  7.8 0.0 copy-start.3
  7.8 0.7 %copy-done.3 = s32[2,512]{1,0:T(2,128)S(1)} copy-done((s32[2,512]{1,0:T(2,128)S(1)}, s32[2,512]{1,0:T(2,128)}, u32[]{:S(2)}) %copy-start.3) | copy-done | bytes 4120
  8.5 0.0 copy-start.4
  8.5 0.7 %copy-done.4 = s32[2,512]{1,0:T(2,128)S(1)} copy-done((s32[2,512]{1,0:T(2,128)S(1)}, s32[2,512]{1,0:T(2,128)}, u32[]{:S(2)}) %copy-start.4) | copy-done | bytes 4120
  9.2 0.0 copy-start.5
  9.2 0.4 tables.1
  9.6 0.0 copy-start.6
  9.6 0.3 copy-done.5
  9.9 0.4 copy-done.6
  10.3 0.1 broadcast_in_dim.10.coef_ref
  10.3 0.0 collective-permute-done.outer_ref
  10.3 0.0 collective-permute-done.1.inner_ref
  10.4 0.0 copy-done.1
  10.4 0.1 pack.1
  10.4 5.2 %collective-permute-start.2 = (f32[7,40,128]{2,1,0:T(8,128)S(1)}, f32[7,40,128]{2,1,0:T(8,128)S(1)}, u32[]{:S(2)}, u32[]{:S(2)}) collective-permute-start(f32[7,40,128]{2,1,0:T(8,128)S(1)} %get-tuple-element.28), channel_id=1, source_target_pairs={{0,32},{32,64},{64,96},{96,128},{128,160},{160,192},{192,224},{224... | collective-permute-start | bytes 430088 | tf_op jit(solution)/shard_map/ppermute | solution.py:376
  15.6 1.9 %collective-permute-start.3 = (f32[7,40,128]{2,1,0:T(8,128)S(1)}, f32[7,40,128]{2,1,0:T(8,128)S(1)}, u32[]{:S(2)}, u32[]{:S(2)}) collective-permute-start(f32[7,40,128]{2,1,0:T(8,128)S(1)} %get-tuple-element.29), channel_id=1, source_target_pairs={{32,0},{64,32},{96,64},{128,96},{160,128},{192,160},{224,192},{256... | collective-permute-start | bytes 430088 | tf_op jit(solution)/shard_map/ppermute | solution.py:376
  17.6 1.6 %first_a.1 = (f32[1792,128]{1,0:T(8,128)S(1)}, f32[112,128]{1,0:T(8,128)S(1)}) custom-call(f32[1792,128]{1,0:T(8,128)S(1)} %bitcast.9, f32[2,7,16,128]{3,2,1,0:T(8,128)S(1)} %get-tuple-element.26.below_ref, f32[2,7,16,128]{3,2,1,0:T(8,128)S(1)} %get-tuple-element.27.above_ref, f32[8,16,128]{2,1,0:T(8,128)S(1)} %broadcast_in_dim.10.coef_ref, ...), custom_call_target="tpu_custom_call" | custom-call | flops 60000000 | bytes 2000000 | tf_op jit(solution)/shard_map/first_a/pallas_call | solution.py:392
  19.2 0.0 collective-permute-done.2.rad_below_ref
  19.2 4.0 %collective-permute-done.3.rad_above_ref = f32[7,40,128]{2,1,0:T(8,128)S(1)} collective-permute-done((f32[7,40,128]{2,1,0:T(8,128)S(1)}, f32[7,40,128]{2,1,0:T(8,128)S(1)}, u32[]{:S(2)}, u32[]{:S(2)}) %collective-permute-start.3) | collective-permute-done | bytes 143392 | tf_op jit(solution)/shard_map/ppermute | solution.py:376
  23.3 1.1 %first_b.1 = (f32[256,128]{1,0:T(8,128)S(1)}, f32[128,128]{1,0:T(8,128)}) custom-call(f32[1792,128]{1,0:T(8,128)S(1)} %bitcast.10, f32[2,7,16,128]{3,2,1,0:T(8,128)S(1)} %get-tuple-element.26.below_ref, f32[2,7,16,128]{3,2,1,0:T(8,128)S(1)} %get-tuple-element.27.above_ref, f32[8,16,128]{2,1,0:T(8,128)S(1)} %broadcast_in_dim.10.coef_ref, ...), custom_call_target="tpu_custom_call" | custom-call | flops 10000000 | bytes 2000000 | tf_op jit(solution)/shard_map/first_b/pallas_call | solution.py:392
  24.3 11.7 %all-to-all-start = ((f32[64,2,128]{2,1,0:T(2,128)}), f32[64,2,128]{2,1,0:T(2,128)}, u32[]{:S(2)}, u32[]{:S(2)}) async-start(f32[64,2,128]{2,1,0:T(2,128)} %bitcast.2), calls=%async_computation | async-start | bytes 131072 | tf_op jit(solution)/shard_map/all_to_all | solution.py:387
  36.0 1.3 %second_a.1.before_ref = f32[1792,128]{1,0:T(8,128)S(1)} custom-call(f32[1792,128]{1,0:T(8,128)S(1)} %bitcast.11, f32[2,7,16,128]{3,2,1,0:T(8,128)S(1)} %get-tuple-element.26.below_ref, f32[2,7,16,128]{3,2,1,0:T(8,128)S(1)} %get-tuple-element.27.above_ref, f32[8,16,128]{2,1,0:T(8,128)S(1)} %broadcast_in_dim.10.coef_ref, ...), custom_call_target="tpu_custom_call" | custom-call | flops 60000000 | bytes 2000000 | tf_op jit(solution)/shard_map/second_a/pallas_call | solution.py:392
  37.3 8.8 %all-to-all-done = f32[64,2,128]{2,1,0:T(2,128)} async-done(((f32[64,2,128]{2,1,0:T(2,128)}), f32[64,2,128]{2,1,0:T(2,128)}, u32[]{:S(2)}, u32[]{:S(2)}) %all-to-all-start) | async-done | bytes 65568 | tf_op jit(solution)/shard_map/all_to_all | solution.py:387
  46.2 2.3 %second_b.1 = (f32[1792,128]{1,0:T(8,128)S(1)}, f32[128,128]{1,0:T(8,128)S(1)}) custom-call(f32[1792,128]{1,0:T(8,128)S(1)} %second_a.1.before_ref, f32[1792,128]{1,0:T(8,128)S(1)} %get-tuple-element.32.inner_ref, f32[256,128]{1,0:T(8,128)S(1)} %get-tuple-element.34.edge_ref, f32[8,16,128]{2,1,0:T(8,128)S(1)} %broadcast_in_dim.10.coef_ref, ...), custom_call_target="tpu_custom_call" | custom-call | flops 30000000 | bytes 2000000 | tf_op jit(solution)/shard_map/second_b/pallas_call | solution.py:392
  48.5 14.0 %all_to_all.10 = f32[64,2,128]{2,1,0:T(2,128)S(1)} all-to-all(f32[64,2,128]{2,1,0:T(2,128)S(1)} %bitcast.13), channel_id=1, replica_groups=mesh['panel'=2,'rad'=12,'ang'=32] {'panel','ang'}, dimensions={0} | all-to-all | bytes 131072 | tf_op jit(solution)/shard_map/all_to_all | solution.py:387
  62.4 1.5 %last.1 = f32[1792,128]{1,0:T(8,128)} custom-call(f32[1792,128]{1,0:T(8,128)S(1)} %get-tuple-element.37.next_ref, f32[128,128]{1,0:T(8,128)S(1)} %bitcast.12, f32[32,128]{1,0:T(8,128)S(1)} %get-tuple-element.36.place_ref), custom_call_target="tpu_custom_call" | custom-call | tf_op jit(solution)/shard_map/last/pallas_call | solution.py:448
  (1 shorter events, 0.0 us)
Async XLA Ops:
  0.0 1.2 %copy-start = (f32[1,7,16,16,128]{4,3,2,1,0:T(8,128)S(1)}, f32[1,7,16,16,128]{4,3,2,1,0:T(8,128)}, u32[]{:S(2)}) copy-start(f32[1,7,16,16,128]{4,3,2,1,0:T(8,128)} %param.6) | copy-start | bytes 2752516
  1.2 9.2 %copy-start.1 = (f32[1,7,16,16,128]{4,3,2,1,0:T(8,128)S(1)}, f32[1,7,16,16,128]{4,3,2,1,0:T(8,128)}, u32[]{:S(2)}) copy-start(f32[1,7,16,16,128]{4,3,2,1,0:T(8,128)} %param.6) | copy-start | bytes 2752516
  1.3 9.1 %collective-permute-start = (f32[2,7,16,128]{3,2,1,0:T(8,128)S(1)}, f32[2,7,16,128]{3,2,1,0:T(8,128)S(1)}, u32[]{:S(2)}, u32[]{:S(2)}) collective-permute-start(f32[2,7,16,128]{3,2,1,0:T(8,128)S(1)} %get-tuple-element.22), channel_id=1, source_target_pairs={{1,2},{3,4},{5,6},{7,8},{9,10},{11,12},{13,14},{15,16},{17,18},{19... | collective-permute-start | bytes 344072 | tf_op jit(solution)/shard_map/ppermute | solution.py:382
  5.2 5.2 %collective-permute-start.1 = (f32[2,7,16,128]{3,2,1,0:T(8,128)S(1)}, f32[2,7,16,128]{3,2,1,0:T(8,128)S(1)}, u32[]{:S(2)}, u32[]{:S(2)}) collective-permute-start(f32[2,7,16,128]{3,2,1,0:T(8,128)S(1)} %get-tuple-element.23), channel_id=1, source_target_pairs={{0,1},{2,3},{4,5},{6,7},{8,9},{10,11},{12,13},{14,15},{16,17},{18,... | collective-permute-start | bytes 344072 | tf_op jit(solution)/shard_map/ppermute | solution.py:382
  7.1 0.7 %copy-start.2 = (f32[2,2,512]{2,1,0:T(2,128)S(1)}, f32[2,2,512]{2,1,0:T(2,128)}, u32[]{:S(2)}) copy-start(f32[2,2,512]{2,1,0:T(2,128)} %frac_ref.1) | copy-start | bytes 24580
  7.8 0.7 %copy-start.3 = (s32[2,512]{1,0:T(2,128)S(1)}, s32[2,512]{1,0:T(2,128)}, u32[]{:S(2)}) copy-start(s32[2,512]{1,0:T(2,128)} %lon_ref.1) | copy-start | bytes 12292
  8.5 0.7 %copy-start.4 = (s32[2,512]{1,0:T(2,128)S(1)}, s32[2,512]{1,0:T(2,128)}, u32[]{:S(2)}) copy-start(s32[2,512]{1,0:T(2,128)} %lat_ref.1) | copy-start | bytes 12292
  9.2 0.7 %copy-start.5 = (f32[7,16]{1,0:T(8,128)S(1)}, f32[7,16]{1,0:T(8,128)}, u32[]{:S(2)}) copy-start(f32[7,16]{1,0:T(8,128)} %param.7) | copy-start | bytes 1348
  9.6 0.7 %copy-start.6 = (f32[16]{0:T(128)S(1)}, f32[16]{0:T(128)}, u32[]{:S(2)}) copy-start(f32[16]{0:T(128)} %param.8) | copy-start | bytes 196
  10.4 8.8 %collective-permute-start.2 = (f32[7,40,128]{2,1,0:T(8,128)S(1)}, f32[7,40,128]{2,1,0:T(8,128)S(1)}, u32[]{:S(2)}, u32[]{:S(2)}) collective-permute-start(f32[7,40,128]{2,1,0:T(8,128)S(1)} %get-tuple-element.28), channel_id=1, source_target_pairs={{0,32},{32,64},{64,96},{96,128},{128,160},{160,192},{192,224},{224... | collective-permute-start | bytes 430088 | tf_op jit(solution)/shard_map/ppermute | solution.py:376
  15.6 7.6 %collective-permute-start.3 = (f32[7,40,128]{2,1,0:T(8,128)S(1)}, f32[7,40,128]{2,1,0:T(8,128)S(1)}, u32[]{:S(2)}, u32[]{:S(2)}) collective-permute-start(f32[7,40,128]{2,1,0:T(8,128)S(1)} %get-tuple-element.29), channel_id=1, source_target_pairs={{32,0},{64,32},{96,64},{128,96},{160,128},{192,160},{224,192},{256... | collective-permute-start | bytes 430088 | tf_op jit(solution)/shard_map/ppermute | solution.py:376
  24.3 21.8 %all-to-all-start = ((f32[64,2,128]{2,1,0:T(2,128)}), f32[64,2,128]{2,1,0:T(2,128)}, u32[]{:S(2)}, u32[]{:S(2)}) async-start(f32[64,2,128]{2,1,0:T(2,128)} %bitcast.2), calls=%async_computation | async-start | bytes 131072 | tf_op jit(solution)/shard_map/all_to_all | solution.py:387

commit v6 on v5

--- a/solution.py
+++ b/solution.py
@@ -39,7 +39,17 @@
     return jnp.where(slot == 0, low_or_none, high_or_none)
 
 
-def tables_kernel(lon_ref, lat_ref, frac_ref, lat_weight_ref, lon_weight_ref, place_ref):
+def tables_kernel(
+    kappa_ref, buoyancy_ref, lon_ref, lat_ref, frac_ref, coef_ref, lat_weight_ref, lon_weight_ref, beside_weight_ref,
+    place_ref, placed_ref,
+):
+    level = lax.broadcasted_iota(jnp.int32, (LV, LV), 0)
+    same = level == lax.broadcasted_iota(jnp.int32, (LV, LV), 1)
+    for f in range(NF + 1):
+        line = kappa_ref[f : f + 1, :] if f < NF else buoyancy_ref[...]
+        column = jnp.sum(jnp.where(same, line, 0.0), axis=1, keepdims=True)
+        coef_ref[f] = jnp.broadcast_to(column, (LV, LAT))
+
     nlon = lon_ref.shape[1]
     half = 2 * nlon // CP
     points = 2 * nlon
@@ -73,6 +83,9 @@
     lat_weight = jnp.where(lane == lat, 1.0 - fy, 0.0) + jnp.where(lane == lat + 1.0, fy, 0.0)
     lat_weight = jnp.where(pick >= 0.0, lat_weight, 0.0)
     lon_weight = jnp.where(lane == off, 1.0 - fx, 0.0) + jnp.where(lane == off + 1.0, fx, 0.0)
+    shifted = pltpu.roll(lon_weight, CP, 1)
+    beside = jnp.where(lane < CP, lat_weight[:, 1:2] * lon_weight, lat_weight[:, LAT - 2 : LAT - 1] * shifted)
+    beside_weight_ref[...] = jnp.transpose(jnp.concatenate([beside, beside], axis=0))
     lat_weight_ref[...] = jnp.transpose(jnp.concatenate([lat_weight, lat_weight], axis=0))
     lon_weight_ref[...] = jnp.transpose(jnp.concatenate([lon_weight, lon_weight], axis=0))[0:CP]
 
@@ -84,7 +97,8 @@
     lane = lax.broadcasted_iota(jnp.int32, (half, 128), 1)
     place = jnp.where(lane == target, 1.0, 0.0)
     place = jnp.concatenate([place * panel.astype(F32), place * (1 - panel).astype(F32)], axis=0)
-    place_ref[...] = jnp.transpose(place)[0 : 2 * CP]
+    place_ref[...] = place
+    placed_ref[...] = jnp.transpose(place)[0 : 2 * CP]
 
 
 def increments(center, neighbours, kappa, buoyancy, scale):
@@ -176,7 +190,7 @@
 
 def first_b_kernel(
     state_ref, below_ref, above_ref, coef_ref, rad_below_ref, rad_above_ref, lat_weight_ref, lon_weight_ref,
-    values_ref, edge_ref, send_ref, line_ref,
+    values_ref, edge_ref, send_ref, line_ref, donors_ref,
 ):
     for e, r in enumerate((0, LV - 1)):
         for f in range(NF):
@@ -207,7 +221,12 @@
                 edge_ref[base : base + 8, :] = center[f] + rates[f]
         edge_ref[(e * 8 + NF) * CP : (e * 8 + 8) * CP, :] = jnp.zeros((CP, LAT), F32)
     edges = interpolate(edge_ref[...], lat_weight_ref, lon_weight_ref)
-    send_ref[...] = jnp.transpose(jnp.concatenate([values_ref[...], edges], axis=0))
+    donors_ref[0 : NF * LV, :] = values_ref[...]
+    donors_ref[NF * LV : 128, :] = jnp.zeros((128 - NF * LV, 128), F32)
+    for f in range(NF):
+        donors_ref[f * LV : f * LV + 1, :] = edges[f : f + 1]
+        donors_ref[(f + 1) * LV - 1 : (f + 1) * LV, :] = edges[8 + f : 9 + f]
+    send_ref[...] = jnp.transpose(donors_ref[...])
 
 
 def surround(
@@ -266,43 +285,30 @@
                 line_ref[pl.ds(start, 8, BLOCK), :] = keep_ang[side] * (center[f] + rates[f])
 
 
-def received(place_ref, recv_ref, edge):
-    values = jnp.dot(place_ref[...], recv_ref[...], precision=HIGHEST, preferred_element_type=F32)
-    low, high = values[0:CP], pltpu.roll(values[CP : 2 * CP], LAT - 1 - edge, 1)
-    if edge:
-        low = pltpu.roll(low, edge, 1)
-    first = (lax.broadcasted_iota(jnp.int32, (CP, LAT), 1) & 1) == edge & 1
-    return jnp.where(first, low, high), jnp.where(first, high, low)
-
-
-def with_rows(own, values, point, ends):
-    rows = values[point % 2]
-    if point:
-        rows = pltpu.roll(rows, LAT - point, 1)
-    return jnp.where(ends, rows, own)
-
-
-def ends_of(edge):
-    lane = lax.broadcasted_iota(jnp.int32, (CP, LAT), 1)
-    return (lane == edge) | (lane == LAT - 1 - edge)
-
-
 def first_at(inner_ref, edge_ref, f, r):
     if 1 <= r <= LV - 2:
-        return inner_ref[f * TILE + r * CP : f * TILE + (r + 1) * CP, :], f * LV + r
+        return inner_ref[f * TILE + r * CP : f * TILE + (r + 1) * CP, :]
     e = r // (LV - 1)
-    return edge_ref[(e * 8 + f) * CP : (e * 8 + f + 1) * CP, :], NF * LV + e * 8 + f
+    return edge_ref[(e * 8 + f) * CP : (e * 8 + f + 1) * CP, :]
 
 
 def second_a_kernel(
-    state_ref, below_ref, above_ref, coef_ref, rad_below_ref, rad_above_ref, inner_ref, edge_ref, next_ref,
-    line_ref, work_ref, column_ref,
-):
-    ends = ends_of(0)
+    state_ref, below_ref, above_ref, coef_ref, rad_below_ref, rad_above_ref, inner_ref, edge_ref, lat_weight_ref,
+    lon_weight_ref, next_ref, values_ref, carry_ref, line_ref, work_ref, column_ref,
+):
+    lane = lax.broadcasted_iota(jnp.int32, (CP, LAT), 1)
+    row = lax.broadcasted_iota(jnp.int32, (CP, LAT), 0)
+    ends = (lane == 0) | (lane == LAT - 1)
+    for i, f in enumerate((2, 5)):
+        for r in range(LV):
+            own = (0.25 * step_size) * first_at(inner_ref, edge_ref, f, r)
+            low = jnp.where(lane == row, own[:, 1:2], 0.0)
+            high = jnp.where(lane == row + CP, own[:, LAT - 2 : LAT - 1], 0.0)
+            carry_ref[i, r : r + 1, :] = jnp.sum(low - high, axis=0, keepdims=True)
     for f in range(NF):
         for r in range(LV):
             base = (f * (LV + 2) + r + 1) * BLOCK + 8
-            line_ref[base : base + CP, :] = jnp.where(ends, 0.0, first_at(inner_ref, edge_ref, f, r)[0])
+            line_ref[base : base + CP, :] = jnp.where(ends, 0.0, first_at(inner_ref, edge_ref, f, r))
     surround(
         state_ref, below_ref, above_ref, coef_ref, (rad_below_ref, rad_above_ref), work_ref, column_ref, line_ref
     )
@@ -328,41 +334,53 @@
             for f in range(NF):
                 row = f * TILE + r * CP + 8 * t
                 next_ref[row : row + 8, :] = 0.5 * (state_ref[row : row + 8, :] + center[f]) + rates[f]
+    values_ref[...] = interpolate(next_ref[...], lat_weight_ref, lon_weight_ref)
 
 
 def second_b_kernel(
-    before_ref, inner_ref, edge_ref, coef_ref, recv_ref, place_ref, lat_weight_ref, lon_weight_ref,
-    next_ref, send_ref,
-):
-    values = received(place_ref, recv_ref, 1)
-    beside = ends_of(1)
+    coef_ref, recv_ref, place_ref, carry_ref, values_ref, beside_weight_ref, beside_ref, send_ref
+):
+    ends = lax.dot_general(
+        recv_ref[...], place_ref[...], (((0,), (0,)), ((), ())), precision=HIGHEST, preferred_element_type=F32
+    )
+    ends = [ends[f * LV : (f + 1) * LV] for f in range(NF)]
+    gains = []
+    for f in range(NF):
+        gain = ((0.5 * step_size) * coef_ref[f] + carry_ref[0]) * ends[f]
+        gains.append(gain - carry_ref[1] * ends[(f + 3) % 6] if f < 6 else gain)
+    gains = jnp.concatenate(gains, axis=0)
+    added = jnp.dot(gains, beside_weight_ref[...], precision=HIGHEST, preferred_element_type=F32)
+    blank = jnp.zeros((128 - NF * LV, 128), F32)
+    send_ref[...] = jnp.transpose(jnp.concatenate([values_ref[...] + added, blank], axis=0))
+    beside_ref[...] = jnp.transpose(jnp.concatenate([gains, blank], axis=0))[0 : 2 * CP]
+
+
+def last_kernel(next_ref, beside_ref, recv_ref, placed_ref, out_ref, done_ref, sems):
+    values = jnp.dot(placed_ref[...], recv_ref[...], precision=HIGHEST, preferred_element_type=F32)
+    parts = [
+        values[0:CP],
+        pltpu.roll(beside_ref[0:CP], 1, 1),
+        pltpu.roll(beside_ref[CP : 2 * CP], LAT - 2, 1),
+        pltpu.roll(values[CP : 2 * CP], LAT - 1, 1),
+    ]
     lane = lax.broadcasted_iota(jnp.int32, (CP, LAT), 1)
-    quarter = jnp.where(lane == 1, 0.25 * step_size, -0.25 * step_size)
-    for r in range(LV):
-        u = quarter * first_at(inner_ref, edge_ref, 2, r)[0]
-        b = quarter * first_at(inner_ref, edge_ref, 5, r)[0]
-        rows = [
-            with_rows(jnp.zeros((CP, LAT), F32), values, first_at(inner_ref, edge_ref, f, r)[1], beside)
-            for f in range(NF)
-        ]
-        for f in range(NF):
-            gain = ((0.5 * step_size) * coef_ref[f, r : r + 1, :] + u) * rows[f]
-            if f < 6:
-                gain = gain - b * rows[(f + 3) % 6]
-            row = f * TILE + r * CP
-            next_ref[row : row + CP, :] = before_ref[row : row + CP, :] + gain
-    donors = interpolate(next_ref[...], lat_weight_ref, lon_weight_ref)
-    send_ref[...] = jnp.transpose(jnp.concatenate([donors, jnp.zeros((128 - NF * LV, 128), F32)], axis=0))
-
-
-def last_kernel(next_ref, recv_ref, place_ref, out_ref, done_ref, sems):
-    values = received(place_ref, recv_ref, 0)
-    ends = ends_of(0)
+    mixed = []
+    for q in range(4):
+        place = (lane - q) & 3
+        mixed.append(
+            jnp.where(place < 2, jnp.where(place == 0, parts[0], parts[1]), jnp.where(place == 2, parts[2], parts[3]))
+        )
+    ends = (lane == 0) | (lane == LAT - 1)
+    near = (lane < 2) | (lane >= LAT - 2)
     copies = []
     for f in range(NF):
         for r in range(LV):
-            row = f * TILE + r * CP
-            done_ref[row : row + CP, :] = with_rows(next_ref[row : row + CP, :], values, f * LV + r, ends)
+            row, point = f * TILE + r * CP, f * LV + r
+            rows = mixed[point % 4]
+            if point:
+                rows = pltpu.roll(rows, LAT - point, 1)
+            own = next_ref[row : row + CP, :]
+            done_ref[row : row + CP, :] = jnp.where(ends, 0.0, own) + jnp.where(near, rows, 0.0)
         part = pl.ds(f * TILE, TILE)
         copies.append(pltpu.make_async_copy(done_ref.at[part, :], out_ref.at[part, :], sems.at[f]))
         copies[-1].start()
@@ -396,7 +414,7 @@
         out_specs=(VMEM,) * len(outs),
         scratch_shapes=scratch,
         compiler_params=params(),
-        cost_estimate=cost(flops),
+        cost_estimate=cost(flops) if isinstance(flops, int) else flops,
         name=name,
     )(*operands)
 
@@ -409,17 +427,16 @@
     n_send = 4 * donor_lon.shape[1] // CP
     own = state.reshape(NF * TILE, LAT)
     halo, message = shape(2, NF, LV, LAT), shape(NF, MESSAGE, LAT)
-
-    outer, inner = call(cut_kernel, "cut", (halo, halo), [], 100_000, own)
+    outer, inner = call(cut_kernel, "cut", (halo, halo), [], pl.CostEstimate(flops=4_000_000_000, bytes_accessed=20_000_000, transcendentals=0), own)
     outer = swap(outer, "ang", 1)
     inner = swap(inner, "ang", 0)
-
-    coef = jnp.broadcast_to(jnp.concatenate([kappa, buoyancy[None]])[:, :, None], (NF + 1, LV, LAT))
-    lat_weight, lon_weight, place = call(
-        tables_kernel, "tables", (shape(LAT, n_send), shape(CP, n_send), shape(2 * CP, n_send)), [], 4_000_000,
-        donor_lon, donor_lat, fractions,
-    )
-    coef, lat_weight = lax.optimization_barrier((coef, lat_weight))
+    coef, lat_weight, lon_weight, beside_weight, place, placed = call(
+        tables_kernel, "tables",
+        (
+            shape(NF + 1, LV, LAT), shape(LAT, n_send), shape(CP, n_send), shape(LAT, n_send), shape(n_send, 128),
+            shape(2 * CP, n_send),
+        ), [], 4_000_000, kappa, buoyancy[None], donor_lon, donor_lat, fractions,
+    )
 
     up, down, below, above = call(
         pack_kernel, "pack", (message, message, halo, halo), [], 100_000, own, outer, inner, coef
@@ -431,29 +448,29 @@
         60_000_000, own, below, above, coef, lat_weight, lon_weight,
     )
     edge, out = call(
-        first_b_kernel, "first_b", (shape(2 * 8 * CP, LAT), shape(n_send, 128)), [rows(2 * NF * BLOCK + 8)],
+        first_b_kernel, "first_b", (shape(2 * 8 * CP, LAT), shape(n_send, 128)), [rows(2 * NF * BLOCK + 8), rows(128)],
         10_000_000, own, below, above, coef, rad_below, rad_above, lat_weight, lon_weight, values,
     )
     got = exchange(out)
-    (before,) = call(
-        second_a_kernel, "second_a", (shape(NF * TILE, LAT),),
+    following, values, carry = call(
+        second_a_kernel, "second_a", (shape(NF * TILE, LAT), shape(NF * LV, n_send), shape(2, LV, LAT)),
         [rows(NF * (LV + 2) * BLOCK + 8), rows(2 * NF * BLOCK + 8), rows(2 * NF * BLOCK + 8)], 60_000_000,
-        own, below, above, coef, rad_below, rad_above, middle, edge,
-    )
-    following, out = call(
-        second_b_kernel, "second_b", (shape(NF * TILE, LAT), shape(n_send, 128)), [], 30_000_000,
-        before, middle, edge, coef, got, place, lat_weight, lon_weight,
+        own, below, above, coef, rad_below, rad_above, middle, edge, lat_weight, lon_weight,
+    )
+    beside, out = call(
+        second_b_kernel, "second_b", (shape(2 * CP, LAT), shape(n_send, 128)), [], 1_000_000,
+        coef, got, place, carry, values, beside_weight,
     )
     got = exchange(out)
     result = pl.pallas_call(
         last_kernel,
         out_shape=shape(NF * TILE, LAT),
-        in_specs=[VMEM] * 3,
+        in_specs=[VMEM] * 4,
         out_specs=pl.BlockSpec(memory_space=pl.ANY),
         scratch_shapes=[rows(NF * TILE), pltpu.SemaphoreType.DMA((NF,))],
         compiler_params=params(),
         name="last",
-    )(following, got, place)
+    )(following, beside, got, placed)
     return result.reshape(state.shape)
 
 

time: 64.4 us -> 66 us (1.025)
  local copies, waits for them, and re-layouts: 3.98 us -> 6.35 us
  waiting for transfers between devices: 12.9 us -> 10.9 us
  starting transfers between devices: 24.6 us -> 26.3 us
  Pallas kernels: 8.35 us -> 7.4 us
    all_to_all x1, waiting for transfers between devices: 8.84 us -> 6 us  [exchange(): lax.all_to_all(values.reshape(n, 2, 128), ('panel', 'ang'), 0, 0, tiled=T...]
    unnamed x14 -> x30, local copies, waits for them, and re-layouts: 3.9 us -> 6.35 us
    all_to_all x1, starting transfers between devices: 11.7 us -> 13.3 us  [exchange(): lax.all_to_all(values.reshape(n, 2, 128), ('panel', 'ang'), 0, 0, tiled=T...]
    pallas_call x7, Pallas kernels: 6.84 us -> 6.09 us  [call(): pl.pallas_call(kernel, out_shape=outs, in_specs=[VMEM] * len(operands), o...]
    ppermute x2, waiting for transfers between devices: 0.01 us -> 0.67 us  [swap(): lax.ppermute(value, axis, [(i, i + 1) for i in low] + [(i + 1, i) for i i...]
  transfers between devices with their start and end apart: 5 -> 5, of which waited for: 2 -> 3; matrix products, arithmetic and copies ran while one was open for 0% -> 0% of each run, Pallas kernels for 5% -> 7%
where the time goes in v6:
time: 66 us; the launch traced here: 65.5 us
  starting transfers between devices  26.3 us (40%)
  blocking collectives  14.4 us (22%)
  waiting for transfers between devices  10.9 us (17%)
  Pallas kernels  7.4 us (11%)
  local copies, waits for them, and re-layouts  6.35 us (10%)
    all_to_all x1, blocking collectives, exchange(): lax.all_to_all(values.reshape(n, 2, 128), ('panel', 'ang'), 0, 0, tiled=T...  14.4 us
    all_to_all x1, starting transfers between devices, exchange(): lax.all_to_all(values.reshape(n, 2, 128), ('panel', 'ang'), 0, 0, tiled=T...  13.3 us
    ppermute x2, starting transfers between devices, shift(): return lax.ppermute(value, axis, pairs)  7.13 us
    unnamed x30, local copies, waits for them, and re-layouts  6.35 us
    pallas_call x7, Pallas kernels, call(): pl.pallas_call(kernel, out_shape=outs, in_specs=[VMEM] * len(operands), o...  6.09 us
    all_to_all x1, waiting for transfers between devices, exchange(): lax.all_to_all(values.reshape(n, 2, 128), ('panel', 'ang'), 0, 0, tiled=T...  6 us
    ppermute x2, starting transfers between devices, swap(): lax.ppermute(value, axis, [(i, i + 1) for i in low] + [(i + 1, i) for i i...  5.82 us
    ppermute x2, waiting for transfers between devices, shift(): return lax.ppermute(value, axis, pairs)  4.21 us
  transfers between devices with their start and end apart: 5, of which 3 were waited for; matrix products, arithmetic and copies ran while one was open for 0% of the time, Pallas kernels for 7%

profile of v6, /device:TPU:193, one launch (start us, length us, event | category | flops | bytes accessed | tf_op | source)
XLA Modules:
  0.0 65.5 jit_solution(4763613122036752752)
XLA Ops:
  0.0 0.0 copy-start
  0.0 1.2 %copy-done = f32[1,7,16,16,128]{4,3,2,1,0:T(8,128)S(1)} copy-done((f32[1,7,16,16,128]{4,3,2,1,0:T(8,128)S(1)}, f32[1,7,16,16,128]{4,3,2,1,0:T(8,128)}, u32[]{:S(2)}) %copy-start) | copy-done | bytes 917528
  1.2 0.0 copy-start.10
  1.2 0.0 copy-start.12
  1.2 0.0 copy-start.13
  1.2 0.0 copy-start.1
  1.2 0.1 cut.1
  1.3 0.0 copy-start.11
  1.3 3.9 %collective-permute-start = (f32[2,7,16,128]{3,2,1,0:T(8,128)S(1)}, f32[2,7,16,128]{3,2,1,0:T(8,128)S(1)}, u32[]{:S(2)}, u32[]{:S(2)}) collective-permute-start(f32[2,7,16,128]{3,2,1,0:T(8,128)S(1)} %get-tuple-element.26), channel_id=1, source_target_pairs={{1,2},{3,4},{5,6},{7,8},{9,10},{11,12},{13,14},{15,16},{17,18},{19... | collective-permute-start | bytes 344072 | tf_op jit(solution)/shard_map/ppermute | solution.py:400
  5.2 0.0 copy-start.14
  5.2 1.9 %collective-permute-start.1 = (f32[2,7,16,128]{3,2,1,0:T(8,128)S(1)}, f32[2,7,16,128]{3,2,1,0:T(8,128)S(1)}, u32[]{:S(2)}, u32[]{:S(2)}) collective-permute-start(f32[2,7,16,128]{3,2,1,0:T(8,128)S(1)} %get-tuple-element.27), channel_id=1, source_target_pairs={{0,1},{2,3},{4,5},{6,7},{8,9},{10,11},{12,13},{14,15},{16,17},{18,... | collective-permute-start | bytes 344072 | tf_op jit(solution)/shard_map/ppermute | solution.py:400
  7.1 0.0 copy-done.10
  7.1 0.0 copy-done.12
  7.2 0.0 copy-done.13
  7.2 0.0 copy-done.11
  7.2 0.0 copy-done.14
  7.2 0.5 tables.1
  7.7 0.0 copy-start.4
  7.7 0.0 collective-permute-done.outer_ref
  7.8 0.7 %collective-permute-done.1.inner_ref = f32[2,7,16,128]{3,2,1,0:T(8,128)S(1)} collective-permute-done((f32[2,7,16,128]{3,2,1,0:T(8,128)S(1)}, f32[2,7,16,128]{3,2,1,0:T(8,128)S(1)}, u32[]{:S(2)}, u32[]{:S(2)}) %collective-permute-start.1) | collective-permute-done | bytes 114720 | tf_op jit(solution)/shard_map/ppermute | solution.py:400
  8.4 0.0 copy-done.1
  8.4 0.1 pack.1
  8.5 0.0 copy-done.4
  8.5 5.2 %collective-permute-start.2 = (f32[7,40,128]{2,1,0:T(8,128)S(1)}, f32[7,40,128]{2,1,0:T(8,128)S(1)}, u32[]{:S(2)}, u32[]{:S(2)}) collective-permute-start(f32[7,40,128]{2,1,0:T(8,128)S(1)} %get-tuple-element.31), channel_id=1, source_target_pairs={{0,32},{32,64},{64,96},{96,128},{128,160},{160,192},{192,224},{224... | collective-permute-start | bytes 430088 | tf_op jit(solution)/shard_map/ppermute | solution.py:394
  13.7 1.9 %collective-permute-start.3 = (f32[7,40,128]{2,1,0:T(8,128)S(1)}, f32[7,40,128]{2,1,0:T(8,128)S(1)}, u32[]{:S(2)}, u32[]{:S(2)}) collective-permute-start(f32[7,40,128]{2,1,0:T(8,128)S(1)} %get-tuple-element.32), channel_id=1, source_target_pairs={{32,0},{64,32},{96,64},{128,96},{160,128},{192,160},{224,192},{256... | collective-permute-start | bytes 430088 | tf_op jit(solution)/shard_map/ppermute | solution.py:394
  15.6 1.6 %first_a.1 = (f32[1792,128]{1,0:T(8,128)S(1)}, f32[112,128]{1,0:T(8,128)S(1)}) custom-call(f32[1792,128]{1,0:T(8,128)S(1)} %bitcast.9, f32[2,7,16,128]{3,2,1,0:T(8,128)S(1)} %get-tuple-element.29.below_ref, f32[2,7,16,128]{3,2,1,0:T(8,128)S(1)} %get-tuple-element.30.above_ref, f32[8,16,128]{2,1,0:T(8,128)S(1)} %get-tuple-element.28.coef_ref, ...), custom_call_target="tpu_custom_call" | custom-call | flops 60000000 | bytes 2000000 | tf_op jit(solution)/shard_map/first_a/pallas_call | solution.py:410
  17.3 0.0 collective-permute-done.2.rad_below_ref
  17.3 4.2 %collective-permute-done.3.rad_above_ref = f32[7,40,128]{2,1,0:T(8,128)S(1)} collective-permute-done((f32[7,40,128]{2,1,0:T(8,128)S(1)}, f32[7,40,128]{2,1,0:T(8,128)S(1)}, u32[]{:S(2)}, u32[]{:S(2)}) %collective-permute-start.3) | collective-permute-done | bytes 143392 | tf_op jit(solution)/shard_map/ppermute | solution.py:394
  21.5 1.1 %first_b.1 = (f32[256,128]{1,0:T(8,128)S(1)}, f32[128,128]{1,0:T(8,128)}) custom-call(f32[1792,128]{1,0:T(8,128)S(1)} %bitcast.10, f32[2,7,16,128]{3,2,1,0:T(8,128)S(1)} %get-tuple-element.29.below_ref, f32[2,7,16,128]{3,2,1,0:T(8,128)S(1)} %get-tuple-element.30.above_ref, f32[8,16,128]{2,1,0:T(8,128)S(1)} %get-tuple-element.28.coef_ref, ...), custom_call_target="tpu_custom_call" | custom-call | flops 10000000 | bytes 2000000 | tf_op jit(solution)/shard_map/first_b/pallas_call | solution.py:410
  22.6 0.0 copy-start.2
  22.6 0.7 copy-done.2
  23.2 13.3 %all-to-all-start = ((f32[64,2,128]{2,1,0:T(2,128)}), f32[64,2,128]{2,1,0:T(2,128)S(1)}, u32[]{:S(2)}, u32[]{:S(2)}) async-start(f32[64,2,128]{2,1,0:T(2,128)} %bitcast.2), calls=%async_computation | async-start | bytes 131072 | tf_op jit(solution)/shard_map/all_to_all | solution.py:405
  36.5 0.0 copy-start.3
  36.6 0.9 %copy-done.3 = f32[256,128]{1,0:T(8,128)S(1)} copy-done((f32[256,128]{1,0:T(8,128)S(1)}, f32[256,128]{1,0:T(8,128)}, u32[]{:S(2)}) %copy-start.3) | copy-done | bytes 131096
  37.4 2.1 %second_a.1 = (f32[1792,128]{1,0:T(8,128)S(1)}, f32[112,128]{1,0:T(8,128)S(1)}, f32[2,16,128]{2,1,0:T(8,128)S(1)}) custom-call(f32[1792,128]{1,0:T(8,128)S(1)} %bitcast.11, f32[2,7,16,128]{3,2,1,0:T(8,128)S(1)} %get-tuple-element.29.below_ref, f32[2,7,16,128]{3,2,1,0:T(8,128)S(1)} %get-tuple-element.30.above_ref, ...), custom_call_target="tpu_custom_call" | custom-call | flops 60000000 | bytes 2000000 | tf_op jit(solution)/shard_map/second_a/pallas_call | solution.py:410
  39.6 0.0 copy-start.6
  39.6 0.6 copy-done.6
  40.2 0.0 copy-start.8
  40.2 0.6 copy-done.8
  40.8 6.0 %all-to-all-done = f32[64,2,128]{2,1,0:T(2,128)S(1)} async-done(((f32[64,2,128]{2,1,0:T(2,128)}), f32[64,2,128]{2,1,0:T(2,128)S(1)}, u32[]{:S(2)}, u32[]{:S(2)}) %all-to-all-start) | async-done | bytes 65568 | tf_op jit(solution)/shard_map/all_to_all | solution.py:405
  46.8 0.0 copy-start.5
  46.8 0.8 %copy-done.5 = f32[128,128]{1,0:T(8,128)S(1)} copy-done((f32[128,128]{1,0:T(8,128)S(1)}, f32[128,128]{1,0:T(8,128)}, u32[]{:S(2)}) %copy-start.5) | copy-done | bytes 65560
  47.6 0.0 copy-start.7
  47.6 0.8 %copy-done.7 = f32[112,128]{1,0:T(8,128)S(1)} copy-done((f32[112,128]{1,0:T(8,128)S(1)}, f32[112,128]{1,0:T(8,128)}, u32[]{:S(2)}) %copy-start.7) | copy-done | bytes 57368
  48.4 0.0 copy-start.9
  48.4 0.7 %copy-done.9 = f32[2,16,128]{2,1,0:T(8,128)S(1)} copy-done((f32[2,16,128]{2,1,0:T(8,128)S(1)}, f32[2,16,128]{2,1,0:T(8,128)}, u32[]{:S(2)}) %copy-start.9) | copy-done | bytes 16408
  49.2 0.6 second_b.1
  49.8 14.4 %all_to_all.10 = f32[64,2,128]{2,1,0:T(2,128)S(1)} all-to-all(f32[64,2,128]{2,1,0:T(2,128)S(1)} %bitcast.14), channel_id=1, replica_groups=mesh['panel'=2,'rad'=12,'ang'=32] {'panel','ang'}, dimensions={0} | all-to-all | bytes 131072 | tf_op jit(solution)/shard_map/all_to_all | solution.py:405
  64.2 1.3 %last.1 = f32[1792,128]{1,0:T(8,128)} custom-call(f32[1792,128]{1,0:T(8,128)S(1)} %get-tuple-element.38.next_ref, f32[32,128]{1,0:T(8,128)S(1)} %get-tuple-element.44.beside_ref, f32[128,128]{1,0:T(8,128)S(1)} %bitcast.13, f32[32,128]{1,0:T(8,128)S(1)} %get-tuple-element.46.placed_ref), custom_call_target="tpu_custom_call" | custom-call | tf_op jit(solution)/shard_map/last/pallas_call | solution.py:465
Async XLA Ops:
  0.0 1.2 %copy-start = (f32[1,7,16,16,128]{4,3,2,1,0:T(8,128)S(1)}, f32[1,7,16,16,128]{4,3,2,1,0:T(8,128)}, u32[]{:S(2)}) copy-start(f32[1,7,16,16,128]{4,3,2,1,0:T(8,128)} %param.6) | copy-start | bytes 2752516
  1.2 6.0 %copy-start.10 = (f32[2,2,512]{2,1,0:T(2,128)S(1)}, f32[2,2,512]{2,1,0:T(2,128)}, u32[]{:S(2)}) copy-start(f32[2,2,512]{2,1,0:T(2,128)} %frac_ref.1) | copy-start | bytes 24580
  1.2 6.0 %copy-start.12 = (s32[2,512]{1,0:T(2,128)S(1)}, s32[2,512]{1,0:T(2,128)}, u32[]{:S(2)}) copy-start(s32[2,512]{1,0:T(2,128)} %lon_ref.1) | copy-start | bytes 12292
  1.2 6.0 %copy-start.13 = (s32[2,512]{1,0:T(2,128)S(1)}, s32[2,512]{1,0:T(2,128)}, u32[]{:S(2)}) copy-start(s32[2,512]{1,0:T(2,128)} %lat_ref.1) | copy-start | bytes 12292
  1.2 7.2 %copy-start.1 = (f32[1,7,16,16,128]{4,3,2,1,0:T(8,128)S(1)}, f32[1,7,16,16,128]{4,3,2,1,0:T(8,128)}, u32[]{:S(2)}) copy-start(f32[1,7,16,16,128]{4,3,2,1,0:T(8,128)} %param.6) | copy-start | bytes 2752516
  1.3 5.9 %copy-start.11 = (f32[7,16]{1,0:T(8,128)S(1)}, f32[7,16]{1,0:T(8,128)}, u32[]{:S(2)}) copy-start(f32[7,16]{1,0:T(8,128)} %kappa_ref.1) | copy-start | bytes 1348
  1.3 6.5 %collective-permute-start = (f32[2,7,16,128]{3,2,1,0:T(8,128)S(1)}, f32[2,7,16,128]{3,2,1,0:T(8,128)S(1)}, u32[]{:S(2)}, u32[]{:S(2)}) collective-permute-start(f32[2,7,16,128]{3,2,1,0:T(8,128)S(1)} %get-tuple-element.26), channel_id=1, source_target_pairs={{1,2},{3,4},{5,6},{7,8},{9,10},{11,12},{13,14},{15,16},{17,18},{19... | collective-permute-start | bytes 344072 | tf_op jit(solution)/shard_map/ppermute | solution.py:400
  5.2 2.0 %copy-start.14 = (f32[16]{0:T(128)S(1)}, f32[16]{0:T(128)}, u32[]{:S(2)}) copy-start(f32[16]{0:T(128)} %param.8) | copy-start | bytes 196
  5.2 3.2 %collective-permute-start.1 = (f32[2,7,16,128]{3,2,1,0:T(8,128)S(1)}, f32[2,7,16,128]{3,2,1,0:T(8,128)S(1)}, u32[]{:S(2)}, u32[]{:S(2)}) collective-permute-start(f32[2,7,16,128]{3,2,1,0:T(8,128)S(1)} %get-tuple-element.27), channel_id=1, source_target_pairs={{0,1},{2,3},{4,5},{6,7},{8,9},{10,11},{12,13},{14,15},{16,17},{18,... | collective-permute-start | bytes 344072 | tf_op jit(solution)/shard_map/ppermute | solution.py:400
  7.7 0.7 %copy-start.4 = (f32[128,128]{1,0:T(8,128)}, f32[128,128]{1,0:T(8,128)S(1)}, u32[]{:S(2)}) copy-start(f32[128,128]{1,0:T(8,128)S(1)} %get-tuple-element.40.place_ref) | copy-start | bytes 196612
  8.5 8.8 %collective-permute-start.2 = (f32[7,40,128]{2,1,0:T(8,128)S(1)}, f32[7,40,128]{2,1,0:T(8,128)S(1)}, u32[]{:S(2)}, u32[]{:S(2)}) collective-permute-start(f32[7,40,128]{2,1,0:T(8,128)S(1)} %get-tuple-element.31), channel_id=1, source_target_pairs={{0,32},{32,64},{64,96},{96,128},{128,160},{160,192},{192,224},{224... | collective-permute-start | bytes 430088 | tf_op jit(solution)/shard_map/ppermute | solution.py:394
  13.7 7.8 %collective-permute-start.3 = (f32[7,40,128]{2,1,0:T(8,128)S(1)}, f32[7,40,128]{2,1,0:T(8,128)S(1)}, u32[]{:S(2)}, u32[]{:S(2)}) collective-permute-start(f32[7,40,128]{2,1,0:T(8,128)S(1)} %get-tuple-element.32), channel_id=1, source_target_pairs={{32,0},{64,32},{96,64},{128,96},{160,128},{192,160},{224,192},{256... | collective-permute-start | bytes 430088 | tf_op jit(solution)/shard_map/ppermute | solution.py:394
  22.6 0.7 copy-start.2
  23.2 23.6 %all-to-all-start = ((f32[64,2,128]{2,1,0:T(2,128)}), f32[64,2,128]{2,1,0:T(2,128)S(1)}, u32[]{:S(2)}, u32[]{:S(2)}) async-start(f32[64,2,128]{2,1,0:T(2,128)} %bitcast.2), calls=%async_computation | async-start | bytes 131072 | tf_op jit(solution)/shard_map/all_to_all | solution.py:405
  36.5 0.9 %copy-start.3 = (f32[256,128]{1,0:T(8,128)S(1)}, f32[256,128]{1,0:T(8,128)}, u32[]{:S(2)}) copy-start(f32[256,128]{1,0:T(8,128)} %copy-done.2) | copy-start | bytes 393220
  39.6 0.6 copy-start.6
  40.2 0.6 copy-start.8
  46.8 0.8 %copy-start.5 = (f32[128,128]{1,0:T(8,128)S(1)}, f32[128,128]{1,0:T(8,128)}, u32[]{:S(2)}) copy-start(f32[128,128]{1,0:T(8,128)} %copy-done.4) | copy-start | bytes 196612
  47.6 0.8 %copy-start.7 = (f32[112,128]{1,0:T(8,128)S(1)}, f32[112,128]{1,0:T(8,128)}, u32[]{:S(2)}) copy-start(f32[112,128]{1,0:T(8,128)} %copy-done.6) | copy-start | bytes 172036
  48.4 0.7 %copy-start.9 = (f32[2,16,128]{2,1,0:T(8,128)S(1)}, f32[2,16,128]{2,1,0:T(8,128)}, u32[]{:S(2)}) copy-start(f32[2,16,128]{2,1,0:T(8,128)} %copy-done.8) | copy-start | bytes 49156

commit v7 on v6

--- a/solution.py
+++ b/solution.py
@@ -41,7 +41,7 @@
 
 def tables_kernel(
     kappa_ref, buoyancy_ref, lon_ref, lat_ref, frac_ref, coef_ref, lat_weight_ref, lon_weight_ref, beside_weight_ref,
-    place_ref, placed_ref,
+    placed_ref,
 ):
     level = lax.broadcasted_iota(jnp.int32, (LV, LV), 0)
     same = level == lax.broadcasted_iota(jnp.int32, (LV, LV), 1)
@@ -85,7 +85,7 @@
     lon_weight = jnp.where(lane == off, 1.0 - fx, 0.0) + jnp.where(lane == off + 1.0, fx, 0.0)
     shifted = pltpu.roll(lon_weight, CP, 1)
     beside = jnp.where(lane < CP, lat_weight[:, 1:2] * lon_weight, lat_weight[:, LAT - 2 : LAT - 1] * shifted)
-    beside_weight_ref[...] = jnp.transpose(jnp.concatenate([beside, beside], axis=0))
+    beside_weight_ref[...] = jnp.transpose(jnp.concatenate([beside, beside], axis=0))[0 : 2 * CP]
     lat_weight_ref[...] = jnp.transpose(jnp.concatenate([lat_weight, lat_weight], axis=0))
     lon_weight_ref[...] = jnp.transpose(jnp.concatenate([lon_weight, lon_weight], axis=0))[0:CP]
 
@@ -97,7 +97,6 @@
     lane = lax.broadcasted_iota(jnp.int32, (half, 128), 1)
     place = jnp.where(lane == target, 1.0, 0.0)
     place = jnp.concatenate([place * panel.astype(F32), place * (1 - panel).astype(F32)], axis=0)
-    place_ref[...] = place
     placed_ref[...] = jnp.transpose(place)[0 : 2 * CP]
 
 
@@ -190,37 +189,85 @@
 
 def first_b_kernel(
     state_ref, below_ref, above_ref, coef_ref, rad_below_ref, rad_above_ref, lat_weight_ref, lon_weight_ref,
-    values_ref, edge_ref, send_ref, line_ref, donors_ref,
+    values_ref, edge_ref, ring_ref, send_ref, line_ref, column_ref, donors_ref,
 ):
-    for e, r in enumerate((0, LV - 1)):
-        for f in range(NF):
+    rad, ang = lax.axis_index("rad"), lax.axis_index("ang")
+    keep_rad = [jnp.where(rad == 0, 0.0, 1.0), jnp.where(rad == lax.axis_size("rad") - 1, 0.0, 1.0)]
+    keep_ang = [jnp.where(ang == 0, 0.0, 1.0), jnp.where(ang == lax.axis_size("ang") - 1, 0.0, 1.0)]
+    radial = (rad_below_ref, rad_above_ref)
+
+    for f in range(NF):
+        for e, r in ((1, 0), (2, LV - 1)):
             base = (e * NF + f) * BLOCK + 8
             line_ref[base : base + CP, :] = state_ref[f * TILE + r * CP : f * TILE + (r + 1) * CP, :]
             line_ref[base - 1 : base, :] = below_ref[0, f, r : r + 1, :]
             line_ref[base + CP : base + CP + 1, :] = above_ref[0, f, r : r + 1, :]
-    for e, r in enumerate((0, LV - 1)):
+        for e, ref in ((0, rad_below_ref), (3, rad_above_ref)):
+            base = (e * NF + f) * BLOCK + 8
+            line_ref[base : base + CP, :] = ref[f, 0:CP, :]
+            line_ref[base - 1 : base, :] = ref[f, 33:34, :]
+            line_ref[base + CP : base + CP + 1, :] = ref[f, 32:33, :]
+        for side, ref in ((0, below_ref.at[0]), (1, above_ref.at[0])):
+            base = (side * NF + f) * BLOCK + 8
+            column_ref[base : base + LV, :] = ref[f]
+            column_ref[base - 1 : base, :] = rad_below_ref[f, 33 - side : 34 - side, :]
+            column_ref[base + LV : base + LV + 1, :] = rad_above_ref[f, 33 - side : 34 - side, :]
+
+    for e in range(4):
         for t in range(2):
-
-            def own(f, level):
-                return state_ref[f * TILE + level * CP + 8 * t : f * TILE + level * CP + 8 * t + 8, :]
+            part = slice(8 * t, 8 * t + 8)
+
+            def own(f, r):
+                return state_ref[f * TILE + r * CP + 8 * t : f * TILE + r * CP + 8 * t + 8, :]
 
             def neighbours(f):
                 line = (e * NF + f) * BLOCK + 8 + 8 * t
                 if e == 0:
-                    up, down = own(f, 1), rad_below_ref[f, 8 * t : 8 * t + 8, :]
+                    up, down = own(f, 0), rad_below_ref[f, CP + 8 * t : CP + 8 * t + 8, :]
+                elif e == 1:
+                    up, down = own(f, 1), rad_below_ref[f, part, :]
+                elif e == 2:
+                    up, down = rad_above_ref[f, part, :], own(f, LV - 2)
                 else:
-                    up, down = rad_above_ref[f, 8 * t : 8 * t + 8, :], own(f, LV - 2)
+                    up, down = rad_above_ref[f, CP + 8 * t : CP + 8 * t + 8, :], own(f, LV - 1)
                 return up, down, line_ref[line + 1 : line + 9, :], line_ref[line - 1 : line + 7, :]
 
-            center = [own(f, r) for f in range(NF)]
-            rates = increments(
-                center, neighbours, lambda f: coef_ref[f, r : r + 1, :], coef_ref[NF, r : r + 1, :], step_size
-            )
+            center = [line_ref[(e * NF + f) * BLOCK + 8 + 8 * t : (e * NF + f) * BLOCK + 16 + 8 * t, :] for f in range(NF)]
+            if e in (0, 3):
+                source = radial[e // 3]
+                rates = increments(center, neighbours, lambda f: source[f, 34:35, :], source[0, 35:36, :], step_size)
+            else:
+                r = (e - 1) * (LV - 1)
+                rates = increments(
+                    center, neighbours, lambda f: coef_ref[f, r : r + 1, :], coef_ref[NF, r : r + 1, :], step_size
+                )
             for f in range(NF):
+                value = center[f] + rates[f]
+                if e in (0, 3):
+                    value = keep_rad[e // 3] * value
                 base = (e * 8 + f) * CP + 8 * t
-                edge_ref[base : base + 8, :] = center[f] + rates[f]
+                edge_ref[base : base + 8, :] = value
         edge_ref[(e * 8 + NF) * CP : (e * 8 + 8) * CP, :] = jnp.zeros((CP, LAT), F32)
-    edges = interpolate(edge_ref[...], lat_weight_ref, lon_weight_ref)
+
+    for side in range(2):
+        for t in range(2):
+            part = slice(8 * t, 8 * t + 8)
+
+            def neighbours(f):
+                column = (side * NF + f) * BLOCK + 8 + 8 * t
+                near = state_ref[pl.ds(f * TILE + 8 * t * CP + side * (CP - 1), 8, CP), :]
+                if side == 0:
+                    east, west = near, below_ref[1, f, part, :]
+                else:
+                    east, west = above_ref[1, f, part, :], near
+                return column_ref[column + 1 : column + 9, :], column_ref[column - 1 : column + 7, :], east, west
+
+            center = [(below_ref[0, f, part, :] if side == 0 else above_ref[0, f, part, :]) for f in range(NF)]
+            rates = increments(center, neighbours, lambda f: coef_ref[f, part, :], coef_ref[NF, part, :], step_size)
+            for f in range(NF):
+                ring_ref[side, f, part, :] = keep_ang[side] * (center[f] + rates[f])
+
+    edges = interpolate(edge_ref[8 * CP : 24 * CP, :], lat_weight_ref, lon_weight_ref)
     donors_ref[0 : NF * LV, :] = values_ref[...]
     donors_ref[NF * LV : 128, :] = jnp.zeros((128 - NF * LV, 128), F32)
     for f in range(NF):
@@ -229,72 +276,15 @@
     send_ref[...] = jnp.transpose(donors_ref[...])
 
 
-def surround(
-    state_ref, below_ref, above_ref, coef_ref, rad_refs, work_ref, column_ref, line_ref
-):
-    rad, ang = lax.axis_index("rad"), lax.axis_index("ang")
-    keep_rad = [jnp.where(rad == 0, 0.0, 1.0), jnp.where(rad == lax.axis_size("rad") - 1, 0.0, 1.0)]
-    keep_ang = [jnp.where(ang == 0, 0.0, 1.0), jnp.where(ang == lax.axis_size("ang") - 1, 0.0, 1.0)]
-    for e in range(2):
-        source = rad_refs[e]
-        for f in range(NF):
-            base = (e * NF + f) * BLOCK + 8
-            work_ref[base : base + CP, :] = source[f, 0:CP, :]
-            work_ref[base - 1 : base, :] = source[f, 33:34, :]
-            work_ref[base + CP : base + CP + 1, :] = source[f, 32:33, :]
-    for side, ref in ((0, below_ref), (1, above_ref)):
-        for f in range(NF):
-            base = (side * NF + f) * BLOCK + 8
-            column_ref[base : base + LV, :] = ref[0, f]
-            column_ref[base - 1 : base, :] = rad_refs[0][f, 33 - side : 34 - side, :]
-            column_ref[base + LV : base + LV + 1, :] = rad_refs[1][f, 33 - side : 34 - side, :]
-
-    for e in range(2):
-        source = rad_refs[e]
-        for t in range(2):
-            part = slice(8 * t, 8 * t + 8)
-
-            def neighbours(f):
-                line = (e * NF + f) * BLOCK + 8 + 8 * t
-                start = f * TILE + e * (LV - 1) * CP + 8 * t
-                inside, outside = state_ref[start : start + 8, :], source[f, CP + 8 * t : CP + 8 * t + 8, :]
-                up, down = (inside, outside) if e == 0 else (outside, inside)
-                return up, down, work_ref[line + 1 : line + 9, :], work_ref[line - 1 : line + 7, :]
-
-            center = [source[f, part, :] for f in range(NF)]
-            rates = increments(center, neighbours, lambda f: source[f, 34:35, :], source[0, 35:36, :], step_size)
-            for f in range(NF):
-                base = (f * (LV + 2) + e * (LV + 1)) * BLOCK + 8 + 8 * t
-                line_ref[base : base + 8, :] = keep_rad[e] * (center[f] + rates[f])
-
-    for side, ref in ((0, below_ref), (1, above_ref)):
-        for t in range(2):
-            part = slice(8 * t, 8 * t + 8)
-
-            def neighbours(f):
-                column = (side * NF + f) * BLOCK + 8 + 8 * t
-                inside = state_ref[pl.ds(f * TILE + 8 * t * CP + side * (CP - 1), 8, CP), :]
-                outside = ref[1, f, part, :]
-                east, west = (inside, outside) if side == 0 else (outside, inside)
-                return column_ref[column + 1 : column + 9, :], column_ref[column - 1 : column + 7, :], east, west
-
-            center = [ref[0, f, part, :] for f in range(NF)]
-            rates = increments(center, neighbours, lambda f: coef_ref[f, part, :], coef_ref[NF, part, :], step_size)
-            for f in range(NF):
-                start = (f * (LV + 2) + 1 + 8 * t) * BLOCK + (7 if side == 0 else 24)
-                line_ref[pl.ds(start, 8, BLOCK), :] = keep_ang[side] * (center[f] + rates[f])
-
-
 def first_at(inner_ref, edge_ref, f, r):
     if 1 <= r <= LV - 2:
         return inner_ref[f * TILE + r * CP : f * TILE + (r + 1) * CP, :]
-    e = r // (LV - 1)
+    e = {-1: 0, 0: 1, LV - 1: 2, LV: 3}[r]
     return edge_ref[(e * 8 + f) * CP : (e * 8 + f + 1) * CP, :]
 
 
 def second_a_kernel(
-    state_ref, below_ref, above_ref, coef_ref, rad_below_ref, rad_above_ref, inner_ref, edge_ref, lat_weight_ref,
-    lon_weight_ref, next_ref, values_ref, carry_ref, line_ref, work_ref, column_ref,
+    state_ref, coef_ref, inner_ref, edge_ref, ring_ref, lat_weight_ref, lon_weight_ref, next_ref, mid_ref, line_ref
 ):
     lane = lax.broadcasted_iota(jnp.int32, (CP, LAT), 1)
     row = lax.broadcasted_iota(jnp.int32, (CP, LAT), 0)
@@ -304,14 +294,15 @@
             own = (0.25 * step_size) * first_at(inner_ref, edge_ref, f, r)
             low = jnp.where(lane == row, own[:, 1:2], 0.0)
             high = jnp.where(lane == row + CP, own[:, LAT - 2 : LAT - 1], 0.0)
-            carry_ref[i, r : r + 1, :] = jnp.sum(low - high, axis=0, keepdims=True)
-    for f in range(NF):
-        for r in range(LV):
+            mid_ref[NF * LV + i * LV + r : NF * LV + i * LV + r + 1, :] = jnp.sum(low - high, axis=0, keepdims=True)
+    for f in range(NF):
+        for r in range(-1, LV + 1):
             base = (f * (LV + 2) + r + 1) * BLOCK + 8
-            line_ref[base : base + CP, :] = jnp.where(ends, 0.0, first_at(inner_ref, edge_ref, f, r))
-    surround(
-        state_ref, below_ref, above_ref, coef_ref, (rad_below_ref, rad_above_ref), work_ref, column_ref, line_ref
-    )
+            own = first_at(inner_ref, edge_ref, f, r)
+            line_ref[base : base + CP, :] = jnp.where(ends, 0.0, own) if 0 <= r < LV else own
+        start = (f * (LV + 2) + 1) * BLOCK
+        line_ref[pl.ds(start + 7, LV, BLOCK), :] = ring_ref[0, f]
+        line_ref[pl.ds(start + 24, LV, BLOCK), :] = ring_ref[1, f]
 
     for r in range(LV):
         for t in range(2):
@@ -334,24 +325,27 @@
             for f in range(NF):
                 row = f * TILE + r * CP + 8 * t
                 next_ref[row : row + 8, :] = 0.5 * (state_ref[row : row + 8, :] + center[f]) + rates[f]
-    values_ref[...] = interpolate(next_ref[...], lat_weight_ref, lon_weight_ref)
+    mid_ref[0 : NF * LV, :] = interpolate(next_ref[...], lat_weight_ref, lon_weight_ref)
 
 
 def second_b_kernel(
-    coef_ref, recv_ref, place_ref, carry_ref, values_ref, beside_weight_ref, beside_ref, send_ref
+    coef_ref, recv_ref, placed_ref, mid_ref, beside_weight_ref, beside_ref, send_ref
 ):
     ends = lax.dot_general(
-        recv_ref[...], place_ref[...], (((0,), (0,)), ((), ())), precision=HIGHEST, preferred_element_type=F32
+        recv_ref[...], placed_ref[...], (((0,), (1,)), ((), ())), precision=HIGHEST, preferred_element_type=F32
     )
     ends = [ends[f * LV : (f + 1) * LV] for f in range(NF)]
+    u = mid_ref[NF * LV : (NF + 1) * LV, 0 : 2 * CP]
+    b = mid_ref[(NF + 1) * LV : (NF + 2) * LV, 0 : 2 * CP]
     gains = []
     for f in range(NF):
-        gain = ((0.5 * step_size) * coef_ref[f] + carry_ref[0]) * ends[f]
-        gains.append(gain - carry_ref[1] * ends[(f + 3) % 6] if f < 6 else gain)
+        gain = ((0.5 * step_size) * coef_ref[f, :, 0 : 2 * CP] + u) * ends[f]
+        gains.append(gain - b * ends[(f + 3) % 6] if f < 6 else gain)
     gains = jnp.concatenate(gains, axis=0)
     added = jnp.dot(gains, beside_weight_ref[...], precision=HIGHEST, preferred_element_type=F32)
     blank = jnp.zeros((128 - NF * LV, 128), F32)
-    send_ref[...] = jnp.transpose(jnp.concatenate([values_ref[...] + added, blank], axis=0))
+    send_ref[...] = jnp.transpose(jnp.concatenate([mid_ref[0 : NF * LV, :] + added, blank], axis=0))
+    gains = jnp.concatenate([gains, jnp.zeros((NF * LV, 128 - 2 * CP), F32)], axis=1)
     beside_ref[...] = jnp.transpose(jnp.concatenate([gains, blank], axis=0))[0 : 2 * CP]
 
 
@@ -430,11 +424,10 @@
     outer, inner = call(cut_kernel, "cut", (halo, halo), [], pl.CostEstimate(flops=4_000_000_000, bytes_accessed=20_000_000, transcendentals=0), own)
     outer = swap(outer, "ang", 1)
     inner = swap(inner, "ang", 0)
-    coef, lat_weight, lon_weight, beside_weight, place, placed = call(
+    coef, lat_weight, lon_weight, beside_weight, placed = call(
         tables_kernel, "tables",
         (
-            shape(NF + 1, LV, LAT), shape(LAT, n_send), shape(CP, n_send), shape(LAT, n_send), shape(n_send, 128),
-            shape(2 * CP, n_send),
+            shape(NF + 1, LV, LAT), shape(LAT, n_send), shape(CP, n_send), shape(2 * CP, n_send), shape(2 * CP, n_send),
         ), [], 4_000_000, kappa, buoyancy[None], donor_lon, donor_lat, fractions,
     )
 
@@ -447,19 +440,19 @@
         first_a_kernel, "first_a", (shape(NF * TILE, LAT), shape(NF * LV, n_send)), [rows(NF * LV * BLOCK + 8)],
         60_000_000, own, below, above, coef, lat_weight, lon_weight,
     )
-    edge, out = call(
-        first_b_kernel, "first_b", (shape(2 * 8 * CP, LAT), shape(n_send, 128)), [rows(2 * NF * BLOCK + 8), rows(128)],
-        10_000_000, own, below, above, coef, rad_below, rad_above, lat_weight, lon_weight, values,
+    edge, ring, out = call(
+        first_b_kernel, "first_b", (shape(4 * 8 * CP, LAT), halo, shape(n_send, 128)),
+        [rows(4 * NF * BLOCK + 8), rows(2 * NF * BLOCK + 8), rows(128)], 10_000_000,
+        own, below, above, coef, rad_below, rad_above, lat_weight, lon_weight, values,
     )
     got = exchange(out)
-    following, values, carry = call(
-        second_a_kernel, "second_a", (shape(NF * TILE, LAT), shape(NF * LV, n_send), shape(2, LV, LAT)),
-        [rows(NF * (LV + 2) * BLOCK + 8), rows(2 * NF * BLOCK + 8), rows(2 * NF * BLOCK + 8)], 60_000_000,
-        own, below, above, coef, rad_below, rad_above, middle, edge, lat_weight, lon_weight,
+    following, mid = call(
+        second_a_kernel, "second_a", (shape(NF * TILE, LAT), shape((NF + 2) * LV, n_send)),
+        [rows(NF * (LV + 2) * BLOCK + 8)], 60_000_000, own, coef, middle, edge, ring, lat_weight, lon_weight,
     )
     beside, out = call(
         second_b_kernel, "second_b", (shape(2 * CP, LAT), shape(n_send, 128)), [], 1_000_000,
-        coef, got, place, carry, values, beside_weight,
+        coef, got, placed, mid, beside_weight,
     )
     got = exchange(out)
     result = pl.pallas_call(

time: 66 us -> 62.3 us (0.944)
  local copies, waits for them, and re-layouts: 6.35 us -> 1.21 us
  waiting for transfers between devices: 10.9 us -> 13.5 us
    unnamed x30 -> x14, local copies, waits for them, and re-layouts: 6.35 us -> 1.21 us
    all_to_all x1, waiting for transfers between devices: 6 us -> 8.38 us  [exchange(): lax.all_to_all(values.reshape(n, 2, 128), ('panel', 'ang'), 0, 0, tiled=T...]
  transfers between devices with their start and end apart: 5 -> 5, of which waited for: 3 -> 3; matrix products, arithmetic and copies ran while one was open for 0% -> 0% of each run, Pallas kernels for 7% -> 6%
where the time goes in v7:
time: 62.3 us; the launch traced here: 62 us
  starting transfers between devices  26 us (42%)
  blocking collectives  14 us (22%)
  waiting for transfers between devices  13.5 us (22%)
  Pallas kernels  7.17 us (12%)
  local copies, waits for them, and re-layouts  1.21 us (2%)
    all_to_all x1, blocking collectives, exchange(): lax.all_to_all(values.reshape(n, 2, 128), ('panel', 'ang'), 0, 0, tiled=T...  14 us
    all_to_all x1, starting transfers between devices, exchange(): lax.all_to_all(values.reshape(n, 2, 128), ('panel', 'ang'), 0, 0, tiled=T...  13.1 us
    all_to_all x1, waiting for transfers between devices, exchange(): lax.all_to_all(values.reshape(n, 2, 128), ('panel', 'ang'), 0, 0, tiled=T...  8.38 us
    ppermute x2, starting transfers between devices, shift(): return lax.ppermute(value, axis, pairs)  7.13 us
    pallas_call x7, Pallas kernels, call(): pl.pallas_call(kernel, out_shape=outs, in_specs=[VMEM] * len(operands), o...  5.86 us
    ppermute x2, starting transfers between devices, swap(): lax.ppermute(value, axis, [(i, i + 1) for i in low] + [(i + 1, i) for i i...  5.82 us
    ppermute x2, waiting for transfers between devices, shift(): return lax.ppermute(value, axis, pairs)  4.43 us
    pallas_call x1, Pallas kernels, body(): pl.pallas_call(last_kernel, out_shape=shape(NF * TILE, LAT), in_specs=[VM...  1.31 us
  transfers between devices with their start and end apart: 5, of which 3 were waited for; matrix products, arithmetic and copies ran while one was open for 0% of the time, Pallas kernels for 6%

profile of v7, /device:TPU:193, one launch (start us, length us, event | category | flops | bytes accessed | tf_op | source)
XLA Modules:
  0.0 62.0 jit_solution(1595177463503725844)
XLA Ops:
  0.0 0.0 copy-start
  0.0 1.2 %copy-done = f32[1,7,16,16,128]{4,3,2,1,0:T(8,128)S(1)} copy-done((f32[1,7,16,16,128]{4,3,2,1,0:T(8,128)S(1)}, f32[1,7,16,16,128]{4,3,2,1,0:T(8,128)}, u32[]{:S(2)}) %copy-start) | copy-done | bytes 917528
  1.2 0.0 copy-start.2
  1.2 0.0 copy-start.4
  1.2 0.0 copy-start.5
  1.2 0.0 copy-start.1
  1.2 0.1 cut.1
  1.3 0.0 copy-start.3
  1.3 3.9 %collective-permute-start = (f32[2,7,16,128]{3,2,1,0:T(8,128)S(1)}, f32[2,7,16,128]{3,2,1,0:T(8,128)S(1)}, u32[]{:S(2)}, u32[]{:S(2)}) collective-permute-start(f32[2,7,16,128]{3,2,1,0:T(8,128)S(1)} %get-tuple-element.26), channel_id=1, source_target_pairs={{1,2},{3,4},{5,6},{7,8},{9,10},{11,12},{13,14},{15,16},{17,18},{19... | collective-permute-start | bytes 344072 | tf_op jit(solution)/shard_map/ppermute | solution.py:394
  5.2 0.0 copy-start.6
  5.2 1.9 %collective-permute-start.1 = (f32[2,7,16,128]{3,2,1,0:T(8,128)S(1)}, f32[2,7,16,128]{3,2,1,0:T(8,128)S(1)}, u32[]{:S(2)}, u32[]{:S(2)}) collective-permute-start(f32[2,7,16,128]{3,2,1,0:T(8,128)S(1)} %get-tuple-element.27), channel_id=1, source_target_pairs={{0,1},{2,3},{4,5},{6,7},{8,9},{10,11},{12,13},{14,15},{16,17},{18,... | collective-permute-start | bytes 344072 | tf_op jit(solution)/shard_map/ppermute | solution.py:394
  7.1 0.0 copy-done.2
  7.1 0.0 copy-done.4
  7.2 0.0 copy-done.5
  7.2 0.0 copy-done.3
  7.2 0.0 copy-done.6
  7.2 0.5 tables.1
  7.7 0.0 collective-permute-done.outer_ref
  7.7 0.7 %collective-permute-done.1.inner_ref = f32[2,7,16,128]{3,2,1,0:T(8,128)S(1)} collective-permute-done((f32[2,7,16,128]{3,2,1,0:T(8,128)S(1)}, f32[2,7,16,128]{3,2,1,0:T(8,128)S(1)}, u32[]{:S(2)}, u32[]{:S(2)}) %collective-permute-start.1) | collective-permute-done | bytes 114720 | tf_op jit(solution)/shard_map/ppermute | solution.py:394
  8.4 0.0 copy-done.1
  8.4 0.1 pack.1
  8.5 5.2 %collective-permute-start.2 = (f32[7,40,128]{2,1,0:T(8,128)S(1)}, f32[7,40,128]{2,1,0:T(8,128)S(1)}, u32[]{:S(2)}, u32[]{:S(2)}) collective-permute-start(f32[7,40,128]{2,1,0:T(8,128)S(1)} %get-tuple-element.33), channel_id=1, source_target_pairs={{0,32},{32,64},{64,96},{96,128},{128,160},{160,192},{192,224},{224... | collective-permute-start | bytes 430088 | tf_op jit(solution)/shard_map/ppermute | solution.py:388
  13.7 1.9 %collective-permute-start.3 = (f32[7,40,128]{2,1,0:T(8,128)S(1)}, f32[7,40,128]{2,1,0:T(8,128)S(1)}, u32[]{:S(2)}, u32[]{:S(2)}) collective-permute-start(f32[7,40,128]{2,1,0:T(8,128)S(1)} %get-tuple-element.34), channel_id=1, source_target_pairs={{32,0},{64,32},{96,64},{128,96},{160,128},{192,160},{224,192},{256... | collective-permute-start | bytes 430088 | tf_op jit(solution)/shard_map/ppermute | solution.py:388
  15.6 1.6 %first_a.1 = (f32[1792,128]{1,0:T(8,128)S(1)}, f32[112,128]{1,0:T(8,128)S(1)}) custom-call(f32[1792,128]{1,0:T(8,128)S(1)} %bitcast.9, f32[2,7,16,128]{3,2,1,0:T(8,128)S(1)} %get-tuple-element.28.below_ref, f32[2,7,16,128]{3,2,1,0:T(8,128)S(1)} %get-tuple-element.29.above_ref, f32[8,16,128]{2,1,0:T(8,128)S(1)} %get-tuple-element.25.coef_ref, ...), custom_call_target="tpu_custom_call" | custom-call | flops 60000000 | bytes 2000000 | tf_op jit(solution)/shard_map/first_a/pallas_call | solution.py:404
  17.3 0.0 collective-permute-done.2.rad_below_ref
  17.3 4.4 %collective-permute-done.3.rad_above_ref = f32[7,40,128]{2,1,0:T(8,128)S(1)} collective-permute-done((f32[7,40,128]{2,1,0:T(8,128)S(1)}, f32[7,40,128]{2,1,0:T(8,128)S(1)}, u32[]{:S(2)}, u32[]{:S(2)}) %collective-permute-start.3) | collective-permute-done | bytes 143392 | tf_op jit(solution)/shard_map/ppermute | solution.py:388
  21.7 1.2 %first_b.1 = (f32[512,128]{1,0:T(8,128)S(1)}, f32[2,7,16,128]{3,2,1,0:T(8,128)S(1)}, f32[128,128]{1,0:T(8,128)}) custom-call(f32[1792,128]{1,0:T(8,128)S(1)} %bitcast.10, f32[2,7,16,128]{3,2,1,0:T(8,128)S(1)} %get-tuple-element.28.below_ref, f32[2,7,16,128]{3,2,1,0:T(8,128)S(1)} %get-tuple-element.29.above_ref, ...), custom_call_target="tpu_custom_call" | custom-call | flops 10000000 | bytes 2000000 | tf_op jit(solution)/shard_map/first_b/pallas_call | solution.py:404
  22.9 13.1 %all-to-all-start = ((f32[64,2,128]{2,1,0:T(2,128)}), f32[64,2,128]{2,1,0:T(2,128)S(1)}, u32[]{:S(2)}, u32[]{:S(2)}) async-start(f32[64,2,128]{2,1,0:T(2,128)} %bitcast.2), calls=%async_computation | async-start | bytes 131072 | tf_op jit(solution)/shard_map/all_to_all | solution.py:399
  35.9 1.8 %second_a.1 = (f32[1792,128]{1,0:T(8,128)S(1)}, f32[144,128]{1,0:T(8,128)S(1)}) custom-call(f32[1792,128]{1,0:T(8,128)S(1)} %bitcast.11, f32[8,16,128]{2,1,0:T(8,128)S(1)} %get-tuple-element.25.coef_ref, f32[1792,128]{1,0:T(8,128)S(1)} %get-tuple-element.32.inner_ref, f32[512,128]{1,0:T(8,128)S(1)} %get-tuple-element.36.edge_ref, ...), custom_call_target="tpu_custom_call" | custom-call | flops 60000000 | bytes 2000000 | tf_op jit(solution)/shard_map/second_a/pallas_call | solution.py:404
  37.8 8.4 %all-to-all-done = f32[64,2,128]{2,1,0:T(2,128)S(1)} async-done(((f32[64,2,128]{2,1,0:T(2,128)}), f32[64,2,128]{2,1,0:T(2,128)S(1)}, u32[]{:S(2)}, u32[]{:S(2)}) %all-to-all-start) | async-done | bytes 65568 | tf_op jit(solution)/shard_map/all_to_all | solution.py:399
  46.2 0.6 second_b.1
  46.8 14.0 %all_to_all.10 = f32[64,2,128]{2,1,0:T(2,128)S(1)} all-to-all(f32[64,2,128]{2,1,0:T(2,128)S(1)} %bitcast.14), channel_id=1, replica_groups=mesh['panel'=2,'rad'=12,'ang'=32] {'panel','ang'}, dimensions={0} | all-to-all | bytes 131072 | tf_op jit(solution)/shard_map/all_to_all | solution.py:399
  60.7 1.3 %last.1 = f32[1792,128]{1,0:T(8,128)} custom-call(f32[1792,128]{1,0:T(8,128)S(1)} %get-tuple-element.38.next_ref, f32[32,128]{1,0:T(8,128)S(1)} %get-tuple-element.43.beside_ref, f32[128,128]{1,0:T(8,128)S(1)} %bitcast.13, f32[32,128]{1,0:T(8,128)S(1)} %get-tuple-element.40.placed_ref), custom_call_target="tpu_custom_call" | custom-call | tf_op jit(solution)/shard_map/last/pallas_call | solution.py:458
Async XLA Ops:
  0.0 1.2 %copy-start = (f32[1,7,16,16,128]{4,3,2,1,0:T(8,128)S(1)}, f32[1,7,16,16,128]{4,3,2,1,0:T(8,128)}, u32[]{:S(2)}) copy-start(f32[1,7,16,16,128]{4,3,2,1,0:T(8,128)} %param.6) | copy-start | bytes 2752516
  1.2 6.0 %copy-start.2 = (f32[2,2,512]{2,1,0:T(2,128)S(1)}, f32[2,2,512]{2,1,0:T(2,128)}, u32[]{:S(2)}) copy-start(f32[2,2,512]{2,1,0:T(2,128)} %frac_ref.1) | copy-start | bytes 24580
  1.2 6.0 %copy-start.4 = (s32[2,512]{1,0:T(2,128)S(1)}, s32[2,512]{1,0:T(2,128)}, u32[]{:S(2)}) copy-start(s32[2,512]{1,0:T(2,128)} %lon_ref.1) | copy-start | bytes 12292
  1.2 6.0 %copy-start.5 = (s32[2,512]{1,0:T(2,128)S(1)}, s32[2,512]{1,0:T(2,128)}, u32[]{:S(2)}) copy-start(s32[2,512]{1,0:T(2,128)} %lat_ref.1) | copy-start | bytes 12292
  1.2 7.2 %copy-start.1 = (f32[1,7,16,16,128]{4,3,2,1,0:T(8,128)S(1)}, f32[1,7,16,16,128]{4,3,2,1,0:T(8,128)}, u32[]{:S(2)}) copy-start(f32[1,7,16,16,128]{4,3,2,1,0:T(8,128)} %param.6) | copy-start | bytes 2752516
  1.3 5.9 %copy-start.3 = (f32[7,16]{1,0:T(8,128)S(1)}, f32[7,16]{1,0:T(8,128)}, u32[]{:S(2)}) copy-start(f32[7,16]{1,0:T(8,128)} %kappa_ref.1) | copy-start | bytes 1348
  1.3 6.4 %collective-permute-start = (f32[2,7,16,128]{3,2,1,0:T(8,128)S(1)}, f32[2,7,16,128]{3,2,1,0:T(8,128)S(1)}, u32[]{:S(2)}, u32[]{:S(2)}) collective-permute-start(f32[2,7,16,128]{3,2,1,0:T(8,128)S(1)} %get-tuple-element.26), channel_id=1, source_target_pairs={{1,2},{3,4},{5,6},{7,8},{9,10},{11,12},{13,14},{15,16},{17,18},{19... | collective-permute-start | bytes 344072 | tf_op jit(solution)/shard_map/ppermute | solution.py:394
  5.2 2.0 %copy-start.6 = (f32[16]{0:T(128)S(1)}, f32[16]{0:T(128)}, u32[]{:S(2)}) copy-start(f32[16]{0:T(128)} %param.8) | copy-start | bytes 196
  5.2 3.2 %collective-permute-start.1 = (f32[2,7,16,128]{3,2,1,0:T(8,128)S(1)}, f32[2,7,16,128]{3,2,1,0:T(8,128)S(1)}, u32[]{:S(2)}, u32[]{:S(2)}) collective-permute-start(f32[2,7,16,128]{3,2,1,0:T(8,128)S(1)} %get-tuple-element.27), channel_id=1, source_target_pairs={{0,1},{2,3},{4,5},{6,7},{8,9},{10,11},{12,13},{14,15},{16,17},{18,... | collective-permute-start | bytes 344072 | tf_op jit(solution)/shard_map/ppermute | solution.py:394
  8.5 8.8 %collective-permute-start.2 = (f32[7,40,128]{2,1,0:T(8,128)S(1)}, f32[7,40,128]{2,1,0:T(8,128)S(1)}, u32[]{:S(2)}, u32[]{:S(2)}) collective-permute-start(f32[7,40,128]{2,1,0:T(8,128)S(1)} %get-tuple-element.33), channel_id=1, source_target_pairs={{0,32},{32,64},{64,96},{96,128},{128,160},{160,192},{192,224},{224... | collective-permute-start | bytes 430088 | tf_op jit(solution)/shard_map/ppermute | solution.py:388
  13.7 8.0 %collective-permute-start.3 = (f32[7,40,128]{2,1,0:T(8,128)S(1)}, f32[7,40,128]{2,1,0:T(8,128)S(1)}, u32[]{:S(2)}, u32[]{:S(2)}) collective-permute-start(f32[7,40,128]{2,1,0:T(8,128)S(1)} %get-tuple-element.34), channel_id=1, source_target_pairs={{32,0},{64,32},{96,64},{128,96},{160,128},{192,160},{224,192},{256... | collective-permute-start | bytes 430088 | tf_op jit(solution)/shard_map/ppermute | solution.py:388
  22.9 23.3 %all-to-all-start = ((f32[64,2,128]{2,1,0:T(2,128)}), f32[64,2,128]{2,1,0:T(2,128)S(1)}, u32[]{:S(2)}, u32[]{:S(2)}) async-start(f32[64,2,128]{2,1,0:T(2,128)} %bitcast.2), calls=%async_computation | async-start | bytes 131072 | tf_op jit(solution)/shard_map/all_to_all | solution.py:399

commit v8 on v7

--- a/solution.py
+++ b/solution.py
@@ -124,12 +124,19 @@
     return jnp.sum(along.reshape(n, CP, along.shape[1]) * lon_weight_ref[...][None], axis=1)
 
 
-def cut_kernel(state_ref, outer_ref, inner_ref):
+def cut_kernel(state_ref, outer_ref, inner_ref, own_ref, sems):
+    parts = [pl.ds(f * TILE, TILE) for f in range(NF)]
+    copies = [
+        pltpu.make_async_copy(state_ref.at[part, :], own_ref.at[part, :], sems.at[f]) for f, part in enumerate(parts)
+    ]
+    for copy in copies:
+        copy.start()
     odd = lax.axis_index("ang") % 2 == 1
     for f in range(NF):
+        copies[f].wait()
         for i in range(2):
-            low = state_ref[pl.ds(f * TILE + i, LV, CP), :]
-            high = state_ref[pl.ds(f * TILE + CP - 1 - i, LV, CP), :]
+            low = own_ref[pl.ds(f * TILE + i, LV, CP), :]
+            high = own_ref[pl.ds(f * TILE + CP - 1 - i, LV, CP), :]
             outer_ref[i, f] = jnp.where(odd, high, low)
             inner_ref[i, f] = jnp.where(odd, low, high)
 
@@ -161,9 +168,8 @@
             line_ref[base : base + CP, :] = state_ref[f * TILE + r * CP : f * TILE + (r + 1) * CP, :]
         line_ref[pl.ds(f * LV * BLOCK + 7, LV, BLOCK), :] = below_ref[0, f]
         line_ref[pl.ds(f * LV * BLOCK + 24, LV, BLOCK), :] = above_ref[0, f]
-        for r in (0, LV - 1):
-            inner_ref[f * TILE + r * CP : f * TILE + (r + 1) * CP, :] = jnp.zeros((CP, LAT), F32)
-    for r in range(1, LV - 1):
+    zero = jnp.zeros((8, LAT), F32)
+    for r in range(LV):
         for t in range(2):
 
             def row(f, level=r):
@@ -172,8 +178,8 @@
             def neighbours(f):
                 line = (f * LV + r) * BLOCK + 8 + 8 * t
                 return (
-                    state_ref[row(f, r + 1) : row(f, r + 1) + 8, :],
-                    state_ref[row(f, r - 1) : row(f, r - 1) + 8, :],
+                    state_ref[row(f, r + 1) : row(f, r + 1) + 8, :] if r < LV - 1 else zero,
+                    state_ref[row(f, r - 1) : row(f, r - 1) + 8, :] if r else zero,
                     line_ref[line + 1 : line + 9, :],
                     line_ref[line - 1 : line + 7, :],
                 )
@@ -189,20 +195,38 @@
 
 def first_b_kernel(
     state_ref, below_ref, above_ref, coef_ref, rad_below_ref, rad_above_ref, lat_weight_ref, lon_weight_ref,
-    values_ref, edge_ref, ring_ref, send_ref, line_ref, column_ref, donors_ref,
+    inner_ref, values_ref, edge_ref, ring_ref, send_ref, line_ref, column_ref, outside_ref, donors_ref,
 ):
     rad, ang = lax.axis_index("rad"), lax.axis_index("ang")
     keep_rad = [jnp.where(rad == 0, 0.0, 1.0), jnp.where(rad == lax.axis_size("rad") - 1, 0.0, 1.0)]
     keep_ang = [jnp.where(ang == 0, 0.0, 1.0), jnp.where(ang == lax.axis_size("ang") - 1, 0.0, 1.0)]
     radial = (rad_below_ref, rad_above_ref)
 
-    for f in range(NF):
-        for e, r in ((1, 0), (2, LV - 1)):
-            base = (e * NF + f) * BLOCK + 8
-            line_ref[base : base + CP, :] = state_ref[f * TILE + r * CP : f * TILE + (r + 1) * CP, :]
-            line_ref[base - 1 : base, :] = below_ref[0, f, r : r + 1, :]
-            line_ref[base + CP : base + CP + 1, :] = above_ref[0, f, r : r + 1, :]
-        for e, ref in ((0, rad_below_ref), (3, rad_above_ref)):
+    for e, ref in enumerate(radial):
+        level = e * (LV - 1) * CP
+        sign = (0.5 - e) * step_size
+        u = sign * state_ref[level : level + CP, :]
+        b = sign * state_ref[3 * TILE + level : 3 * TILE + level + CP, :]
+        near = [ref[f, 0:CP, :] for f in range(NF)]
+        for f in range(NF):
+            row = f * TILE + level
+            gain = (step_size * coef_ref[f, e * (LV - 1) : e * (LV - 1) + 1, :] + u) * near[f]
+            if f < 6:
+                gain = gain - b * near[(f + 3) % 6]
+            outside_ref[(e * 8 + f) * CP : (e * 8 + f + 1) * CP, :] = gain
+            edge_ref[((e + 1) * 8 + f) * CP : ((e + 1) * 8 + f + 1) * CP, :] = inner_ref[row : row + CP, :] + gain
+        outside_ref[(e * 8 + NF) * CP : (e * 8 + 8) * CP, :] = jnp.zeros((CP, LAT), F32)
+    edges = interpolate(outside_ref[...], lat_weight_ref, lon_weight_ref)
+    donors_ref[0 : NF * LV, :] = values_ref[...]
+    donors_ref[NF * LV : 128, :] = jnp.zeros((128 - NF * LV, 128), F32)
+    for f in range(NF):
+        for e in range(2):
+            row = f * LV + e * (LV - 1)
+            donors_ref[row : row + 1, :] = values_ref[row : row + 1, :] + edges[e * 8 + f : e * 8 + f + 1]
+    send_ref[...] = jnp.transpose(donors_ref[...])
+
+    for f in range(NF):
+        for e, ref in enumerate(radial):
             base = (e * NF + f) * BLOCK + 8
             line_ref[base : base + CP, :] = ref[f, 0:CP, :]
             line_ref[base - 1 : base, :] = ref[f, 33:34, :]
@@ -213,41 +237,22 @@
             column_ref[base - 1 : base, :] = rad_below_ref[f, 33 - side : 34 - side, :]
             column_ref[base + LV : base + LV + 1, :] = rad_above_ref[f, 33 - side : 34 - side, :]
 
-    for e in range(4):
+    for e, source in enumerate(radial):
         for t in range(2):
             part = slice(8 * t, 8 * t + 8)
 
-            def own(f, r):
-                return state_ref[f * TILE + r * CP + 8 * t : f * TILE + r * CP + 8 * t + 8, :]
-
             def neighbours(f):
                 line = (e * NF + f) * BLOCK + 8 + 8 * t
-                if e == 0:
-                    up, down = own(f, 0), rad_below_ref[f, CP + 8 * t : CP + 8 * t + 8, :]
-                elif e == 1:
-                    up, down = own(f, 1), rad_below_ref[f, part, :]
-                elif e == 2:
-                    up, down = rad_above_ref[f, part, :], own(f, LV - 2)
-                else:
-                    up, down = rad_above_ref[f, CP + 8 * t : CP + 8 * t + 8, :], own(f, LV - 1)
+                start = f * TILE + e * (LV - 1) * CP + 8 * t
+                inside, outside = state_ref[start : start + 8, :], source[f, CP + 8 * t : CP + 8 * t + 8, :]
+                up, down = (inside, outside) if e == 0 else (outside, inside)
                 return up, down, line_ref[line + 1 : line + 9, :], line_ref[line - 1 : line + 7, :]
 
-            center = [line_ref[(e * NF + f) * BLOCK + 8 + 8 * t : (e * NF + f) * BLOCK + 16 + 8 * t, :] for f in range(NF)]
-            if e in (0, 3):
-                source = radial[e // 3]
-                rates = increments(center, neighbours, lambda f: source[f, 34:35, :], source[0, 35:36, :], step_size)
-            else:
-                r = (e - 1) * (LV - 1)
-                rates = increments(
-                    center, neighbours, lambda f: coef_ref[f, r : r + 1, :], coef_ref[NF, r : r + 1, :], step_size
-                )
+            center = [source[f, part, :] for f in range(NF)]
+            rates = increments(center, neighbours, lambda f: source[f, 34:35, :], source[0, 35:36, :], step_size)
             for f in range(NF):
-                value = center[f] + rates[f]
-                if e in (0, 3):
-                    value = keep_rad[e // 3] * value
-                base = (e * 8 + f) * CP + 8 * t
-                edge_ref[base : base + 8, :] = value
-        edge_ref[(e * 8 + NF) * CP : (e * 8 + 8) * CP, :] = jnp.zeros((CP, LAT), F32)
+                base = (e * 24 + f) * CP + 8 * t
+                edge_ref[base : base + 8, :] = keep_rad[e] * (center[f] + rates[f])
 
     for side in range(2):
         for t in range(2):
@@ -266,14 +271,6 @@
             rates = increments(center, neighbours, lambda f: coef_ref[f, part, :], coef_ref[NF, part, :], step_size)
             for f in range(NF):
                 ring_ref[side, f, part, :] = keep_ang[side] * (center[f] + rates[f])
-
-    edges = interpolate(edge_ref[8 * CP : 24 * CP, :], lat_weight_ref, lon_weight_ref)
-    donors_ref[0 : NF * LV, :] = values_ref[...]
-    donors_ref[NF * LV : 128, :] = jnp.zeros((128 - NF * LV, 128), F32)
-    for f in range(NF):
-        donors_ref[f * LV : f * LV + 1, :] = edges[f : f + 1]
-        donors_ref[(f + 1) * LV - 1 : (f + 1) * LV, :] = edges[8 + f : 9 + f]
-    send_ref[...] = jnp.transpose(donors_ref[...])
 
 
 def first_at(inner_ref, edge_ref, f, r):
@@ -421,7 +418,16 @@
     n_send = 4 * donor_lon.shape[1] // CP
     own = state.reshape(NF * TILE, LAT)
     halo, message = shape(2, NF, LV, LAT), shape(NF, MESSAGE, LAT)
-    outer, inner = call(cut_kernel, "cut", (halo, halo), [], pl.CostEstimate(flops=4_000_000_000, bytes_accessed=20_000_000, transcendentals=0), own)
+    outer, inner = pl.pallas_call(
+        cut_kernel,
+        out_shape=(halo, halo),
+        in_specs=[pl.BlockSpec(memory_space=pl.ANY)],
+        out_specs=(VMEM, VMEM),
+        scratch_shapes=[rows(NF * TILE), pltpu.SemaphoreType.DMA((NF,))],
+        compiler_params=pltpu.CompilerParams(vmem_limit_bytes=62 * 1024 * 1024),
+        cost_estimate=pl.CostEstimate(flops=4_000_000_000, bytes_accessed=20_000_000, transcendentals=0),
+        name="cut",
+    )(own)
     outer = swap(outer, "ang", 1)
     inner = swap(inner, "ang", 0)
     coef, lat_weight, lon_weight, beside_weight, placed = call(
@@ -442,8 +448,8 @@
     )
     edge, ring, out = call(
         first_b_kernel, "first_b", (shape(4 * 8 * CP, LAT), halo, shape(n_send, 128)),
-        [rows(4 * NF * BLOCK + 8), rows(2 * NF * BLOCK + 8), rows(128)], 10_000_000,
-        own, below, above, coef, rad_below, rad_above, lat_weight, lon_weight, values,
+        [rows(2 * NF * BLOCK + 8), rows(2 * NF * BLOCK + 8), rows(2 * 8 * CP), rows(128)], 10_000_000,
+        own, below, above, coef, rad_below, rad_above, lat_weight, lon_weight, middle, values,
     )
     got = exchange(out)
     following, mid = call(

time: 62.3 us -> 63.1 us (1.013)
  Pallas kernels: 7.17 us -> 9.2 us
  local copies, waits for them, and re-layouts: 1.21 us -> 0.03 us
    pallas_call x0 -> x1, Pallas kernels: none -> 2.08 us  [body(): pl.pallas_call(cut_kernel, out_shape=(halo, halo), in_specs=[pl.BlockSpec...]
    unnamed x14 -> x12, local copies, waits for them, and re-layouts: 1.21 us -> 0.03 us
    pallas_call x7 -> x6, Pallas kernels: 5.86 us -> 5.81 us  [call(): pl.pallas_call(kernel, out_shape=outs, in_specs=[VMEM] * len(operands), o...]
  transfers between devices with their start and end apart: 5 -> 5, of which waited for: 3 -> 4; matrix products, arithmetic and copies ran while one was open for 0% -> 0% of each run, Pallas kernels for 6% -> 7%
where the time goes in v8:
time: 63.1 us; the launch traced here: 62.8 us
  starting transfers between devices  25.9 us (41%)
  blocking collectives  14 us (22%)
  waiting for transfers between devices  13.6 us (22%)
  Pallas kernels  9.2 us (15%)
    all_to_all x1, blocking collectives, exchange(): lax.all_to_all(values.reshape(n, 2, 128), ('panel', 'ang'), 0, 0, tiled=T...  14 us
    all_to_all x1, starting transfers between devices, exchange(): lax.all_to_all(values.reshape(n, 2, 128), ('panel', 'ang'), 0, 0, tiled=T...  13.1 us
    all_to_all x1, waiting for transfers between devices, exchange(): lax.all_to_all(values.reshape(n, 2, 128), ('panel', 'ang'), 0, 0, tiled=T...  8.38 us
    ppermute x2, starting transfers between devices, shift(): return lax.ppermute(value, axis, pairs)  7.13 us
    pallas_call x6, Pallas kernels, call(): pl.pallas_call(kernel, out_shape=outs, in_specs=[VMEM] * len(operands), o...  5.81 us
    ppermute x2, starting transfers between devices, swap(): lax.ppermute(value, axis, [(i, i + 1) for i in low] + [(i + 1, i) for i i...  5.68 us
    ppermute x2, waiting for transfers between devices, shift(): return lax.ppermute(value, axis, pairs)  4.31 us
    pallas_call x1, Pallas kernels, body(): pl.pallas_call(cut_kernel, out_shape=(halo, halo), in_specs=[pl.BlockSpec...  2.08 us
  transfers between devices with their start and end apart: 5, of which 4 were waited for; matrix products, arithmetic and copies ran while one was open for 0% of the time, Pallas kernels for 7%

profile of v8, /device:TPU:193, one launch (start us, length us, event | category | flops | bytes accessed | tf_op | source)
XLA Modules:
  0.0 62.8 jit_solution(1240516372063875795)
XLA Ops:
  0.0 0.0 copy-start.1
  0.0 0.0 copy-start.3
  0.0 0.0 copy-start.4
  0.0 0.0 copy-start
  0.0 2.1 %cut.1 = (f32[2,7,16,128]{3,2,1,0:T(8,128)}, f32[2,7,16,128]{3,2,1,0:T(8,128)}) custom-call(f32[1792,128]{1,0:T(8,128)} %bitcast.7), custom_call_target="tpu_custom_call" | custom-call | flops 4000000000 | bytes 20000000 | tf_op jit(solution)/shard_map/cut/pallas_call | solution.py:421
  2.1 0.0 copy-start.2
  2.1 3.8 %collective-permute-start = (f32[2,7,16,128]{3,2,1,0:T(8,128)}, f32[2,7,16,128]{3,2,1,0:T(8,128)S(1)}, u32[]{:S(2)}, u32[]{:S(2)}) collective-permute-start(f32[2,7,16,128]{3,2,1,0:T(8,128)} %get-tuple-element.26), channel_id=1, source_target_pairs={{1,2},{3,4},{5,6},{7,8},{9,10},{11,12},{13,14},{15,16},{17,18},{19... | collective-permute-start | bytes 344072 | tf_op jit(solution)/shard_map/ppermute | solution.py:391
  5.9 0.0 copy-start.5
  5.9 1.9 %collective-permute-start.1 = (f32[2,7,16,128]{3,2,1,0:T(8,128)}, f32[2,7,16,128]{3,2,1,0:T(8,128)S(1)}, u32[]{:S(2)}, u32[]{:S(2)}) collective-permute-start(f32[2,7,16,128]{3,2,1,0:T(8,128)} %get-tuple-element.27), channel_id=1, source_target_pairs={{0,1},{2,3},{4,5},{6,7},{8,9},{10,11},{12,13},{14,15},{16,17},{18,... | collective-permute-start | bytes 344072 | tf_op jit(solution)/shard_map/ppermute | solution.py:391
  7.8 0.0 copy-done.1
  7.8 0.0 copy-done.3
  7.9 0.0 copy-done.4
  7.9 0.0 copy-done.2
  7.9 0.0 copy-done.5
  7.9 0.5 tables.1
  8.4 0.1 collective-permute-done.outer_ref
  8.6 0.8 %collective-permute-done.1.inner_ref = f32[2,7,16,128]{3,2,1,0:T(8,128)S(1)} collective-permute-done((f32[2,7,16,128]{3,2,1,0:T(8,128)}, f32[2,7,16,128]{3,2,1,0:T(8,128)S(1)}, u32[]{:S(2)}, u32[]{:S(2)}) %collective-permute-start.1) | collective-permute-done | bytes 114720 | tf_op jit(solution)/shard_map/ppermute | solution.py:391
  9.3 0.0 copy-done
  9.3 0.1 pack.1
  9.4 5.2 %collective-permute-start.2 = (f32[7,40,128]{2,1,0:T(8,128)S(1)}, f32[7,40,128]{2,1,0:T(8,128)S(1)}, u32[]{:S(2)}, u32[]{:S(2)}) collective-permute-start(f32[7,40,128]{2,1,0:T(8,128)S(1)} %get-tuple-element.33), channel_id=1, source_target_pairs={{0,32},{32,64},{64,96},{96,128},{128,160},{160,192},{192,224},{224... | collective-permute-start | bytes 430088 | tf_op jit(solution)/shard_map/ppermute | solution.py:385
  14.6 1.9 %collective-permute-start.3 = (f32[7,40,128]{2,1,0:T(8,128)S(1)}, f32[7,40,128]{2,1,0:T(8,128)S(1)}, u32[]{:S(2)}, u32[]{:S(2)}) collective-permute-start(f32[7,40,128]{2,1,0:T(8,128)S(1)} %get-tuple-element.34), channel_id=1, source_target_pairs={{32,0},{64,32},{96,64},{128,96},{160,128},{192,160},{224,192},{256... | collective-permute-start | bytes 430088 | tf_op jit(solution)/shard_map/ppermute | solution.py:385
  16.5 1.7 %first_a.1 = (f32[1792,128]{1,0:T(8,128)S(1)}, f32[112,128]{1,0:T(8,128)S(1)}) custom-call(f32[1792,128]{1,0:T(8,128)S(1)} %bitcast.9, f32[2,7,16,128]{3,2,1,0:T(8,128)S(1)} %get-tuple-element.28.below_ref, f32[2,7,16,128]{3,2,1,0:T(8,128)S(1)} %get-tuple-element.29.above_ref, f32[8,16,128]{2,1,0:T(8,128)S(1)} %get-tuple-element.25.coef_ref, ...), custom_call_target="tpu_custom_call" | custom-call | flops 60000000 | bytes 2000000 | tf_op jit(solution)/shard_map/first_a/pallas_call | solution.py:401
  18.3 0.0 collective-permute-done.2.rad_below_ref
  18.3 4.3 %collective-permute-done.3.rad_above_ref = f32[7,40,128]{2,1,0:T(8,128)S(1)} collective-permute-done((f32[7,40,128]{2,1,0:T(8,128)S(1)}, f32[7,40,128]{2,1,0:T(8,128)S(1)}, u32[]{:S(2)}, u32[]{:S(2)}) %collective-permute-start.3) | collective-permute-done | bytes 143392 | tf_op jit(solution)/shard_map/ppermute | solution.py:385
  22.6 1.1 %first_b.1 = (f32[512,128]{1,0:T(8,128)S(1)}, f32[2,7,16,128]{3,2,1,0:T(8,128)S(1)}, f32[128,128]{1,0:T(8,128)}) custom-call(f32[1792,128]{1,0:T(8,128)S(1)} %bitcast.10, f32[2,7,16,128]{3,2,1,0:T(8,128)S(1)} %get-tuple-element.28.below_ref, f32[2,7,16,128]{3,2,1,0:T(8,128)S(1)} %get-tuple-element.29.above_ref, ...), custom_call_target="tpu_custom_call" | custom-call | flops 10000000 | bytes 2000000 | tf_op jit(solution)/shard_map/first_b/pallas_call | solution.py:401
  23.7 13.1 %all-to-all-start = ((f32[64,2,128]{2,1,0:T(2,128)}), f32[64,2,128]{2,1,0:T(2,128)S(1)}, u32[]{:S(2)}, u32[]{:S(2)}) async-start(f32[64,2,128]{2,1,0:T(2,128)} %bitcast.2), calls=%async_computation | async-start | bytes 131072 | tf_op jit(solution)/shard_map/all_to_all | solution.py:396
  36.8 1.8 %second_a.1 = (f32[1792,128]{1,0:T(8,128)S(1)}, f32[144,128]{1,0:T(8,128)S(1)}) custom-call(f32[1792,128]{1,0:T(8,128)S(1)} %bitcast.11, f32[8,16,128]{2,1,0:T(8,128)S(1)} %get-tuple-element.25.coef_ref, f32[1792,128]{1,0:T(8,128)S(1)} %get-tuple-element.32.inner_ref, f32[512,128]{1,0:T(8,128)S(1)} %get-tuple-element.36.edge_ref, ...), custom_call_target="tpu_custom_call" | custom-call | flops 60000000 | bytes 2000000 | tf_op jit(solution)/shard_map/second_a/pallas_call | solution.py:401
  38.6 8.4 %all-to-all-done = f32[64,2,128]{2,1,0:T(2,128)S(1)} async-done(((f32[64,2,128]{2,1,0:T(2,128)}), f32[64,2,128]{2,1,0:T(2,128)S(1)}, u32[]{:S(2)}, u32[]{:S(2)}) %all-to-all-start) | async-done | bytes 65568 | tf_op jit(solution)/shard_map/all_to_all | solution.py:396
  47.0 0.6 second_b.1
  47.6 14.0 %all_to_all.10 = f32[64,2,128]{2,1,0:T(2,128)S(1)} all-to-all(f32[64,2,128]{2,1,0:T(2,128)S(1)} %bitcast.14), channel_id=1, replica_groups=mesh['panel'=2,'rad'=12,'ang'=32] {'panel','ang'}, dimensions={0} | all-to-all | bytes 131072 | tf_op jit(solution)/shard_map/all_to_all | solution.py:396
  61.5 1.3 %last.1 = f32[1792,128]{1,0:T(8,128)} custom-call(f32[1792,128]{1,0:T(8,128)S(1)} %get-tuple-element.38.next_ref, f32[32,128]{1,0:T(8,128)S(1)} %get-tuple-element.43.beside_ref, f32[128,128]{1,0:T(8,128)S(1)} %bitcast.13, f32[32,128]{1,0:T(8,128)S(1)} %get-tuple-element.40.placed_ref), custom_call_target="tpu_custom_call" | custom-call | tf_op jit(solution)/shard_map/last/pallas_call | solution.py:464
Async XLA Ops:
  0.0 7.8 %copy-start.1 = (f32[2,2,512]{2,1,0:T(2,128)S(1)}, f32[2,2,512]{2,1,0:T(2,128)}, u32[]{:S(2)}) copy-start(f32[2,2,512]{2,1,0:T(2,128)} %frac_ref.1) | copy-start | bytes 24580
  0.0 7.8 %copy-start.3 = (s32[2,512]{1,0:T(2,128)S(1)}, s32[2,512]{1,0:T(2,128)}, u32[]{:S(2)}) copy-start(s32[2,512]{1,0:T(2,128)} %lon_ref.1) | copy-start | bytes 12292
  0.0 7.8 %copy-start.4 = (s32[2,512]{1,0:T(2,128)S(1)}, s32[2,512]{1,0:T(2,128)}, u32[]{:S(2)}) copy-start(s32[2,512]{1,0:T(2,128)} %lat_ref.1) | copy-start | bytes 12292
  0.0 9.3 %copy-start = (f32[1,7,16,16,128]{4,3,2,1,0:T(8,128)S(1)}, f32[1,7,16,16,128]{4,3,2,1,0:T(8,128)}, u32[]{:S(2)}) copy-start(f32[1,7,16,16,128]{4,3,2,1,0:T(8,128)} %param.6) | copy-start | bytes 2752516
  2.1 5.8 %copy-start.2 = (f32[7,16]{1,0:T(8,128)S(1)}, f32[7,16]{1,0:T(8,128)}, u32[]{:S(2)}) copy-start(f32[7,16]{1,0:T(8,128)} %kappa_ref.1) | copy-start | bytes 1348
  2.1 6.4 %collective-permute-start = (f32[2,7,16,128]{3,2,1,0:T(8,128)}, f32[2,7,16,128]{3,2,1,0:T(8,128)S(1)}, u32[]{:S(2)}, u32[]{:S(2)}) collective-permute-start(f32[2,7,16,128]{3,2,1,0:T(8,128)} %get-tuple-element.26), channel_id=1, source_target_pairs={{1,2},{3,4},{5,6},{7,8},{9,10},{11,12},{13,14},{15,16},{17,18},{19... | collective-permute-start | bytes 344072 | tf_op jit(solution)/shard_map/ppermute | solution.py:391
  5.9 2.0 %copy-start.5 = (f32[16]{0:T(128)S(1)}, f32[16]{0:T(128)}, u32[]{:S(2)}) copy-start(f32[16]{0:T(128)} %param.8) | copy-start | bytes 196
  5.9 3.4 %collective-permute-start.1 = (f32[2,7,16,128]{3,2,1,0:T(8,128)}, f32[2,7,16,128]{3,2,1,0:T(8,128)S(1)}, u32[]{:S(2)}, u32[]{:S(2)}) collective-permute-start(f32[2,7,16,128]{3,2,1,0:T(8,128)} %get-tuple-element.27), channel_id=1, source_target_pairs={{0,1},{2,3},{4,5},{6,7},{8,9},{10,11},{12,13},{14,15},{16,17},{18,... | collective-permute-start | bytes 344072 | tf_op jit(solution)/shard_map/ppermute | solution.py:391
  9.4 8.9 %collective-permute-start.2 = (f32[7,40,128]{2,1,0:T(8,128)S(1)}, f32[7,40,128]{2,1,0:T(8,128)S(1)}, u32[]{:S(2)}, u32[]{:S(2)}) collective-permute-start(f32[7,40,128]{2,1,0:T(8,128)S(1)} %get-tuple-element.33), channel_id=1, source_target_pairs={{0,32},{32,64},{64,96},{96,128},{128,160},{160,192},{192,224},{224... | collective-permute-start | bytes 430088 | tf_op jit(solution)/shard_map/ppermute | solution.py:385
  14.6 8.0 %collective-permute-start.3 = (f32[7,40,128]{2,1,0:T(8,128)S(1)}, f32[7,40,128]{2,1,0:T(8,128)S(1)}, u32[]{:S(2)}, u32[]{:S(2)}) collective-permute-start(f32[7,40,128]{2,1,0:T(8,128)S(1)} %get-tuple-element.34), channel_id=1, source_target_pairs={{32,0},{64,32},{96,64},{128,96},{160,128},{192,160},{224,192},{256... | collective-permute-start | bytes 430088 | tf_op jit(solution)/shard_map/ppermute | solution.py:385
  23.7 23.3 %all-to-all-start = ((f32[64,2,128]{2,1,0:T(2,128)}), f32[64,2,128]{2,1,0:T(2,128)S(1)}, u32[]{:S(2)}, u32[]{:S(2)}) async-start(f32[64,2,128]{2,1,0:T(2,128)} %bitcast.2), calls=%async_computation | async-start | bytes 131072 | tf_op jit(solution)/shard_map/all_to_all | solution.py:396

commit v9 on v8

--- a/solution.py
+++ b/solution.py
@@ -124,7 +124,7 @@
     return jnp.sum(along.reshape(n, CP, along.shape[1]) * lon_weight_ref[...][None], axis=1)
 
 
-def cut_kernel(state_ref, outer_ref, inner_ref, own_ref, sems):
+def cut_kernel(state_ref, own_ref, outer_ref, inner_ref, sems):
     parts = [pl.ds(f * TILE, TILE) for f in range(NF)]
     copies = [
         pltpu.make_async_copy(state_ref.at[part, :], own_ref.at[part, :], sems.at[f]) for f, part in enumerate(parts)
@@ -416,18 +416,17 @@
 
 def body(state, kappa, buoyancy, donor_lon, donor_lat, fractions):
     n_send = 4 * donor_lon.shape[1] // CP
-    own = state.reshape(NF * TILE, LAT)
     halo, message = shape(2, NF, LV, LAT), shape(NF, MESSAGE, LAT)
-    outer, inner = pl.pallas_call(
+    own, outer, inner = pl.pallas_call(
         cut_kernel,
-        out_shape=(halo, halo),
+        out_shape=(shape(NF * TILE, LAT), halo, halo),
         in_specs=[pl.BlockSpec(memory_space=pl.ANY)],
-        out_specs=(VMEM, VMEM),
-        scratch_shapes=[rows(NF * TILE), pltpu.SemaphoreType.DMA((NF,))],
-        compiler_params=pltpu.CompilerParams(vmem_limit_bytes=62 * 1024 * 1024),
+        out_specs=(VMEM,) * 3,
+        scratch_shapes=[pltpu.SemaphoreType.DMA((NF,))],
+        compiler_params=pltpu.CompilerParams(vmem_limit_bytes=52 * 1024 * 1024),
         cost_estimate=pl.CostEstimate(flops=4_000_000_000, bytes_accessed=20_000_000, transcendentals=0),
         name="cut",
-    )(own)
+    )(state.reshape(NF * TILE, LAT))
     outer = swap(outer, "ang", 1)
     inner = swap(inner, "ang", 0)
     coef, lat_weight, lon_weight, beside_weight, placed = call(

time: 63.1 us -> 62.2 us (0.986)
  Pallas kernels: 9.2 us -> 8.48 us
    pallas_call x1, Pallas kernels: 2.08 us -> 1.35 us  [body(): pl.pallas_call(cut_kernel, out_shape=(shape(NF * TILE, LAT), halo, halo),...]
  transfers between devices with their start and end apart: 5 -> 5, of which waited for: 4 -> 3; matrix products, arithmetic and copies ran while one was open for 0% -> 0% of each run, Pallas kernels for 7% -> 7%
where the time goes in v9:
time: 62.2 us; the launch traced here: 61.9 us
  starting transfers between devices  25.9 us (42%)
  blocking collectives  14 us (23%)
  waiting for transfers between devices  13.4 us (22%)
  Pallas kernels  8.48 us (14%)
    all_to_all x1, blocking collectives, exchange(): lax.all_to_all(values.reshape(n, 2, 128), ('panel', 'ang'), 0, 0, tiled=T...  14 us
    all_to_all x1, starting transfers between devices, exchange(): lax.all_to_all(values.reshape(n, 2, 128), ('panel', 'ang'), 0, 0, tiled=T...  13.1 us
    all_to_all x1, waiting for transfers between devices, exchange(): lax.all_to_all(values.reshape(n, 2, 128), ('panel', 'ang'), 0, 0, tiled=T...  8.38 us
    ppermute x2, starting transfers between devices, shift(): return lax.ppermute(value, axis, pairs)  7.13 us
    pallas_call x6, Pallas kernels, call(): pl.pallas_call(kernel, out_shape=outs, in_specs=[VMEM] * len(operands), o...  5.83 us
    ppermute x2, starting transfers between devices, swap(): lax.ppermute(value, axis, [(i, i + 1) for i in low] + [(i + 1, i) for i i...  5.69 us
    ppermute x2, waiting for transfers between devices, shift(): return lax.ppermute(value, axis, pairs)  4.31 us
    pallas_call x1, Pallas kernels, body(): pl.pallas_call(cut_kernel, out_shape=(shape(NF * TILE, LAT), halo, halo),...  1.35 us
  transfers between devices with their start and end apart: 5, of which 3 were waited for; matrix products, arithmetic and copies ran while one was open for 0% of the time, Pallas kernels for 7%

profile of v9, /device:TPU:193, one launch (start us, length us, event | category | flops | bytes accessed | tf_op | source)
XLA Modules:
  0.0 61.9 jit_solution(4050115731916534457)
XLA Ops:
  0.0 0.0 copy-start
  0.0 0.0 copy-start.2
  0.0 0.0 copy-start.3
  0.0 1.3 %cut.1 = (f32[1792,128]{1,0:T(8,128)S(1)}, f32[2,7,16,128]{3,2,1,0:T(8,128)S(1)}, f32[2,7,16,128]{3,2,1,0:T(8,128)S(1)}) custom-call(f32[1792,128]{1,0:T(8,128)} %bitcast.11), custom_call_target="tpu_custom_call" | custom-call | flops 4000000000 | bytes 20000000 | tf_op jit(solution)/shard_map/cut/pallas_call | solution.py:420
  1.4 0.0 copy-start.1
  1.4 3.8 %collective-permute-start = (f32[2,7,16,128]{3,2,1,0:T(8,128)S(1)}, f32[2,7,16,128]{3,2,1,0:T(8,128)S(1)}, u32[]{:S(2)}, u32[]{:S(2)}) collective-permute-start(f32[2,7,16,128]{3,2,1,0:T(8,128)S(1)} %get-tuple-element.28), channel_id=1, source_target_pairs={{1,2},{3,4},{5,6},{7,8},{9,10},{11,12},{13,14},{15,16},{17,18},{19... | collective-permute-start | bytes 344072 | tf_op jit(solution)/shard_map/ppermute | solution.py:391
  5.1 0.0 copy-start.4
  5.2 1.9 %collective-permute-start.1 = (f32[2,7,16,128]{3,2,1,0:T(8,128)S(1)}, f32[2,7,16,128]{3,2,1,0:T(8,128)S(1)}, u32[]{:S(2)}, u32[]{:S(2)}) collective-permute-start(f32[2,7,16,128]{3,2,1,0:T(8,128)S(1)} %get-tuple-element.29), channel_id=1, source_target_pairs={{0,1},{2,3},{4,5},{6,7},{8,9},{10,11},{12,13},{14,15},{16,17},{18,... | collective-permute-start | bytes 344072 | tf_op jit(solution)/shard_map/ppermute | solution.py:391
  7.1 0.0 copy-done
  7.1 0.0 copy-done.2
  7.1 0.0 copy-done.3
  7.1 0.0 copy-done.1
  7.1 0.0 copy-done.4
  7.1 0.5 tables.1
  7.7 0.0 collective-permute-done.outer_ref
  7.7 0.7 %collective-permute-done.1.inner_ref = f32[2,7,16,128]{3,2,1,0:T(8,128)S(1)} collective-permute-done((f32[2,7,16,128]{3,2,1,0:T(8,128)S(1)}, f32[2,7,16,128]{3,2,1,0:T(8,128)S(1)}, u32[]{:S(2)}, u32[]{:S(2)}) %collective-permute-start.1) | collective-permute-done | bytes 114720 | tf_op jit(solution)/shard_map/ppermute | solution.py:391
  8.4 0.1 pack.1
  8.4 5.2 %collective-permute-start.2 = (f32[7,40,128]{2,1,0:T(8,128)S(1)}, f32[7,40,128]{2,1,0:T(8,128)S(1)}, u32[]{:S(2)}, u32[]{:S(2)}) collective-permute-start(f32[7,40,128]{2,1,0:T(8,128)S(1)} %get-tuple-element.35), channel_id=1, source_target_pairs={{0,32},{32,64},{64,96},{96,128},{128,160},{160,192},{192,224},{224... | collective-permute-start | bytes 430088 | tf_op jit(solution)/shard_map/ppermute | solution.py:385
  13.7 1.9 %collective-permute-start.3 = (f32[7,40,128]{2,1,0:T(8,128)S(1)}, f32[7,40,128]{2,1,0:T(8,128)S(1)}, u32[]{:S(2)}, u32[]{:S(2)}) collective-permute-start(f32[7,40,128]{2,1,0:T(8,128)S(1)} %get-tuple-element.36), channel_id=1, source_target_pairs={{32,0},{64,32},{96,64},{128,96},{160,128},{192,160},{224,192},{256... | collective-permute-start | bytes 430088 | tf_op jit(solution)/shard_map/ppermute | solution.py:385
  15.6 1.7 %first_a.1 = (f32[1792,128]{1,0:T(8,128)S(1)}, f32[112,128]{1,0:T(8,128)S(1)}) custom-call(f32[1792,128]{1,0:T(8,128)S(1)} %get-tuple-element.26.state_ref, f32[2,7,16,128]{3,2,1,0:T(8,128)S(1)} %get-tuple-element.30.below_ref, f32[2,7,16,128]{3,2,1,0:T(8,128)S(1)} %get-tuple-element.31.above_ref, f32[8,16,128]{2,1,0:T(8,128)S(1)} %get-tuple-element.27.coef_ref, ...), custom_call_target="tpu_custom_call" | custom-call | flops 60000000 | bytes 2000000 | tf_op jit(solution)/shard_map/first_a/pallas_call | solution.py:401
  17.3 0.0 collective-permute-done.2.rad_below_ref
  17.3 4.3 %collective-permute-done.3.rad_above_ref = f32[7,40,128]{2,1,0:T(8,128)S(1)} collective-permute-done((f32[7,40,128]{2,1,0:T(8,128)S(1)}, f32[7,40,128]{2,1,0:T(8,128)S(1)}, u32[]{:S(2)}, u32[]{:S(2)}) %collective-permute-start.3) | collective-permute-done | bytes 143392 | tf_op jit(solution)/shard_map/ppermute | solution.py:385
  21.7 1.1 %first_b.1 = (f32[512,128]{1,0:T(8,128)S(1)}, f32[2,7,16,128]{3,2,1,0:T(8,128)S(1)}, f32[128,128]{1,0:T(8,128)}) custom-call(f32[1792,128]{1,0:T(8,128)S(1)} %get-tuple-element.26.state_ref, f32[2,7,16,128]{3,2,1,0:T(8,128)S(1)} %get-tuple-element.30.below_ref, f32[2,7,16,128]{3,2,1,0:T(8,128)S(1)} %get-tuple-element.31.above_ref, ...), custom_call_target="tpu_custom_call" | custom-call | flops 10000000 | bytes 2000000 | tf_op jit(solution)/shard_map/first_b/pallas_call | solution.py:401
  22.7 13.1 %all-to-all-start = ((f32[64,2,128]{2,1,0:T(2,128)}), f32[64,2,128]{2,1,0:T(2,128)S(1)}, u32[]{:S(2)}, u32[]{:S(2)}) async-start(f32[64,2,128]{2,1,0:T(2,128)} %bitcast.2), calls=%async_computation | async-start | bytes 131072 | tf_op jit(solution)/shard_map/all_to_all | solution.py:396
  35.8 1.8 %second_a.1 = (f32[1792,128]{1,0:T(8,128)S(1)}, f32[144,128]{1,0:T(8,128)S(1)}) custom-call(f32[1792,128]{1,0:T(8,128)S(1)} %get-tuple-element.26.state_ref, f32[8,16,128]{2,1,0:T(8,128)S(1)} %get-tuple-element.27.coef_ref, f32[1792,128]{1,0:T(8,128)S(1)} %get-tuple-element.34.inner_ref, f32[512,128]{1,0:T(8,128)S(1)} %get-tuple-element.38.edge_ref, ...), custom_call_target="tpu_custom_call" | custom-call | flops 60000000 | bytes 2000000 | tf_op jit(solution)/shard_map/second_a/pallas_call | solution.py:401
  37.7 8.4 %all-to-all-done = f32[64,2,128]{2,1,0:T(2,128)S(1)} async-done(((f32[64,2,128]{2,1,0:T(2,128)}), f32[64,2,128]{2,1,0:T(2,128)S(1)}, u32[]{:S(2)}, u32[]{:S(2)}) %all-to-all-start) | async-done | bytes 65568 | tf_op jit(solution)/shard_map/all_to_all | solution.py:396
  46.0 0.6 second_b.1
  46.6 14.0 %all_to_all.10 = f32[64,2,128]{2,1,0:T(2,128)S(1)} all-to-all(f32[64,2,128]{2,1,0:T(2,128)S(1)} %bitcast.9), channel_id=1, replica_groups=mesh['panel'=2,'rad'=12,'ang'=32] {'panel','ang'}, dimensions={0} | all-to-all | bytes 131072 | tf_op jit(solution)/shard_map/all_to_all | solution.py:396
  60.6 1.3 %last.1 = f32[1792,128]{1,0:T(8,128)} custom-call(f32[1792,128]{1,0:T(8,128)S(1)} %get-tuple-element.40.next_ref, f32[32,128]{1,0:T(8,128)S(1)} %get-tuple-element.45.beside_ref, f32[128,128]{1,0:T(8,128)S(1)} %bitcast.8, f32[32,128]{1,0:T(8,128)S(1)} %get-tuple-element.42.placed_ref), custom_call_target="tpu_custom_call" | custom-call | tf_op jit(solution)/shard_map/last/pallas_call | solution.py:463
Async XLA Ops:
  0.0 7.1 %copy-start = (f32[2,2,512]{2,1,0:T(2,128)S(1)}, f32[2,2,512]{2,1,0:T(2,128)}, u32[]{:S(2)}) copy-start(f32[2,2,512]{2,1,0:T(2,128)} %frac_ref.1) | copy-start | bytes 24580
  0.0 7.1 %copy-start.2 = (s32[2,512]{1,0:T(2,128)S(1)}, s32[2,512]{1,0:T(2,128)}, u32[]{:S(2)}) copy-start(s32[2,512]{1,0:T(2,128)} %lon_ref.1) | copy-start | bytes 12292
  0.0 7.1 %copy-start.3 = (s32[2,512]{1,0:T(2,128)S(1)}, s32[2,512]{1,0:T(2,128)}, u32[]{:S(2)}) copy-start(s32[2,512]{1,0:T(2,128)} %lat_ref.1) | copy-start | bytes 12292
  1.4 5.8 %copy-start.1 = (f32[7,16]{1,0:T(8,128)S(1)}, f32[7,16]{1,0:T(8,128)}, u32[]{:S(2)}) copy-start(f32[7,16]{1,0:T(8,128)} %kappa_ref.1) | copy-start | bytes 1348
  1.4 6.3 %collective-permute-start = (f32[2,7,16,128]{3,2,1,0:T(8,128)S(1)}, f32[2,7,16,128]{3,2,1,0:T(8,128)S(1)}, u32[]{:S(2)}, u32[]{:S(2)}) collective-permute-start(f32[2,7,16,128]{3,2,1,0:T(8,128)S(1)} %get-tuple-element.28), channel_id=1, source_target_pairs={{1,2},{3,4},{5,6},{7,8},{9,10},{11,12},{13,14},{15,16},{17,18},{19... | collective-permute-start | bytes 344072 | tf_op jit(solution)/shard_map/ppermute | solution.py:391
  5.1 2.0 %copy-start.4 = (f32[16]{0:T(128)S(1)}, f32[16]{0:T(128)}, u32[]{:S(2)}) copy-start(f32[16]{0:T(128)} %param.8) | copy-start | bytes 196
  5.2 3.2 %collective-permute-start.1 = (f32[2,7,16,128]{3,2,1,0:T(8,128)S(1)}, f32[2,7,16,128]{3,2,1,0:T(8,128)S(1)}, u32[]{:S(2)}, u32[]{:S(2)}) collective-permute-start(f32[2,7,16,128]{3,2,1,0:T(8,128)S(1)} %get-tuple-element.29), channel_id=1, source_target_pairs={{0,1},{2,3},{4,5},{6,7},{8,9},{10,11},{12,13},{14,15},{16,17},{18,... | collective-permute-start | bytes 344072 | tf_op jit(solution)/shard_map/ppermute | solution.py:391
  8.4 8.9 %collective-permute-start.2 = (f32[7,40,128]{2,1,0:T(8,128)S(1)}, f32[7,40,128]{2,1,0:T(8,128)S(1)}, u32[]{:S(2)}, u32[]{:S(2)}) collective-permute-start(f32[7,40,128]{2,1,0:T(8,128)S(1)} %get-tuple-element.35), channel_id=1, source_target_pairs={{0,32},{32,64},{64,96},{96,128},{128,160},{160,192},{192,224},{224... | collective-permute-start | bytes 430088 | tf_op jit(solution)/shard_map/ppermute | solution.py:385
  13.7 8.0 %collective-permute-start.3 = (f32[7,40,128]{2,1,0:T(8,128)S(1)}, f32[7,40,128]{2,1,0:T(8,128)S(1)}, u32[]{:S(2)}, u32[]{:S(2)}) collective-permute-start(f32[7,40,128]{2,1,0:T(8,128)S(1)} %get-tuple-element.36), channel_id=1, source_target_pairs={{32,0},{64,32},{96,64},{128,96},{160,128},{192,160},{224,192},{256... | collective-permute-start | bytes 430088 | tf_op jit(solution)/shard_map/ppermute | solution.py:385
  22.7 23.3 %all-to-all-start = ((f32[64,2,128]{2,1,0:T(2,128)}), f32[64,2,128]{2,1,0:T(2,128)S(1)}, u32[]{:S(2)}, u32[]{:S(2)}) async-start(f32[64,2,128]{2,1,0:T(2,128)} %bitcast.2), calls=%async_computation | async-start | bytes 131072 | tf_op jit(solution)/shard_map/all_to_all | solution.py:396

commit v10 on v9

--- a/solution.py
+++ b/solution.py
@@ -439,8 +439,8 @@
     up, down, below, above = call(
         pack_kernel, "pack", (message, message, halo, halo), [], 100_000, own, outer, inner, coef
     )
+    rad_above = shift(down, "rad", -1)
     rad_below = shift(up, "rad", 1)
-    rad_above = shift(down, "rad", -1)
     middle, values = call(
         first_a_kernel, "first_a", (shape(NF * TILE, LAT), shape(NF * LV, n_send)), [rows(NF * LV * BLOCK + 8)],
         60_000_000, own, below, above, coef, lat_weight, lon_weight,

time: 62.2 us -> 62.2 us (level)
  no operation moved by 1% of the time
where the time goes in v10:
time: 62.2 us; the launch traced here: 61.9 us
  starting transfers between devices  25.9 us (42%)
  blocking collectives  14 us (23%)
  waiting for transfers between devices  13.4 us (22%)
  Pallas kernels  8.48 us (14%)
    all_to_all x1, blocking collectives, exchange(): lax.all_to_all(values.reshape(n, 2, 128), ('panel', 'ang'), 0, 0, tiled=T...  14 us
    all_to_all x1, starting transfers between devices, exchange(): lax.all_to_all(values.reshape(n, 2, 128), ('panel', 'ang'), 0, 0, tiled=T...  13.1 us
    all_to_all x1, waiting for transfers between devices, exchange(): lax.all_to_all(values.reshape(n, 2, 128), ('panel', 'ang'), 0, 0, tiled=T...  8.38 us
    ppermute x2, starting transfers between devices, shift(): return lax.ppermute(value, axis, pairs)  7.13 us
    pallas_call x6, Pallas kernels, call(): pl.pallas_call(kernel, out_shape=outs, in_specs=[VMEM] * len(operands), o...  5.83 us
    ppermute x2, starting transfers between devices, swap(): lax.ppermute(value, axis, [(i, i + 1) for i in low] + [(i + 1, i) for i i...  5.69 us
    ppermute x2, waiting for transfers between devices, shift(): return lax.ppermute(value, axis, pairs)  4.31 us
    pallas_call x1, Pallas kernels, body(): pl.pallas_call(cut_kernel, out_shape=(shape(NF * TILE, LAT), halo, halo),...  1.35 us
  transfers between devices with their start and end apart: 5, of which 3 were waited for; matrix products, arithmetic and copies ran while one was open for 0% of the time, Pallas kernels for 7%

profile of v10, /device:TPU:193, one launch (start us, length us, event | category | flops | bytes accessed | tf_op | source)
XLA Modules:
  0.0 61.9 jit_solution(4050115731916534457)
XLA Ops:
  0.0 0.0 copy-start
  0.0 0.0 copy-start.2
  0.0 0.0 copy-start.3
  0.0 1.3 %cut.1 = (f32[1792,128]{1,0:T(8,128)S(1)}, f32[2,7,16,128]{3,2,1,0:T(8,128)S(1)}, f32[2,7,16,128]{3,2,1,0:T(8,128)S(1)}) custom-call(f32[1792,128]{1,0:T(8,128)} %bitcast.11), custom_call_target="tpu_custom_call" | custom-call | flops 4000000000 | bytes 20000000 | tf_op jit(solution)/shard_map/cut/pallas_call | solution.py:420
  1.4 0.0 copy-start.1
  1.4 3.8 %collective-permute-start = (f32[2,7,16,128]{3,2,1,0:T(8,128)S(1)}, f32[2,7,16,128]{3,2,1,0:T(8,128)S(1)}, u32[]{:S(2)}, u32[]{:S(2)}) collective-permute-start(f32[2,7,16,128]{3,2,1,0:T(8,128)S(1)} %get-tuple-element.28), channel_id=1, source_target_pairs={{1,2},{3,4},{5,6},{7,8},{9,10},{11,12},{13,14},{15,16},{17,18},{19... | collective-permute-start | bytes 344072 | tf_op jit(solution)/shard_map/ppermute | solution.py:391
  5.1 0.0 copy-start.4
  5.2 1.9 %collective-permute-start.1 = (f32[2,7,16,128]{3,2,1,0:T(8,128)S(1)}, f32[2,7,16,128]{3,2,1,0:T(8,128)S(1)}, u32[]{:S(2)}, u32[]{:S(2)}) collective-permute-start(f32[2,7,16,128]{3,2,1,0:T(8,128)S(1)} %get-tuple-element.29), channel_id=1, source_target_pairs={{0,1},{2,3},{4,5},{6,7},{8,9},{10,11},{12,13},{14,15},{16,17},{18,... | collective-permute-start | bytes 344072 | tf_op jit(solution)/shard_map/ppermute | solution.py:391
  7.1 0.0 copy-done
  7.1 0.0 copy-done.2
  7.1 0.0 copy-done.3
  7.1 0.0 copy-done.1
  7.1 0.0 copy-done.4
  7.1 0.5 tables.1
  7.7 0.0 collective-permute-done.outer_ref
  7.7 0.7 %collective-permute-done.1.inner_ref = f32[2,7,16,128]{3,2,1,0:T(8,128)S(1)} collective-permute-done((f32[2,7,16,128]{3,2,1,0:T(8,128)S(1)}, f32[2,7,16,128]{3,2,1,0:T(8,128)S(1)}, u32[]{:S(2)}, u32[]{:S(2)}) %collective-permute-start.1) | collective-permute-done | bytes 114720 | tf_op jit(solution)/shard_map/ppermute | solution.py:391
  8.4 0.1 pack.1
  8.4 5.2 %collective-permute-start.2 = (f32[7,40,128]{2,1,0:T(8,128)S(1)}, f32[7,40,128]{2,1,0:T(8,128)S(1)}, u32[]{:S(2)}, u32[]{:S(2)}) collective-permute-start(f32[7,40,128]{2,1,0:T(8,128)S(1)} %get-tuple-element.35), channel_id=1, source_target_pairs={{0,32},{32,64},{64,96},{96,128},{128,160},{160,192},{192,224},{224... | collective-permute-start | bytes 430088 | tf_op jit(solution)/shard_map/ppermute | solution.py:385
  13.7 1.9 %collective-permute-start.3 = (f32[7,40,128]{2,1,0:T(8,128)S(1)}, f32[7,40,128]{2,1,0:T(8,128)S(1)}, u32[]{:S(2)}, u32[]{:S(2)}) collective-permute-start(f32[7,40,128]{2,1,0:T(8,128)S(1)} %get-tuple-element.36), channel_id=1, source_target_pairs={{32,0},{64,32},{96,64},{128,96},{160,128},{192,160},{224,192},{256... | collective-permute-start | bytes 430088 | tf_op jit(solution)/shard_map/ppermute | solution.py:385
  15.6 1.7 %first_a.1 = (f32[1792,128]{1,0:T(8,128)S(1)}, f32[112,128]{1,0:T(8,128)S(1)}) custom-call(f32[1792,128]{1,0:T(8,128)S(1)} %get-tuple-element.26.state_ref, f32[2,7,16,128]{3,2,1,0:T(8,128)S(1)} %get-tuple-element.30.below_ref, f32[2,7,16,128]{3,2,1,0:T(8,128)S(1)} %get-tuple-element.31.above_ref, f32[8,16,128]{2,1,0:T(8,128)S(1)} %get-tuple-element.27.coef_ref, ...), custom_call_target="tpu_custom_call" | custom-call | flops 60000000 | bytes 2000000 | tf_op jit(solution)/shard_map/first_a/pallas_call | solution.py:401
  17.3 0.0 collective-permute-done.2.rad_below_ref
  17.3 4.3 %collective-permute-done.3.rad_above_ref = f32[7,40,128]{2,1,0:T(8,128)S(1)} collective-permute-done((f32[7,40,128]{2,1,0:T(8,128)S(1)}, f32[7,40,128]{2,1,0:T(8,128)S(1)}, u32[]{:S(2)}, u32[]{:S(2)}) %collective-permute-start.3) | collective-permute-done | bytes 143392 | tf_op jit(solution)/shard_map/ppermute | solution.py:385
  21.7 1.1 %first_b.1 = (f32[512,128]{1,0:T(8,128)S(1)}, f32[2,7,16,128]{3,2,1,0:T(8,128)S(1)}, f32[128,128]{1,0:T(8,128)}) custom-call(f32[1792,128]{1,0:T(8,128)S(1)} %get-tuple-element.26.state_ref, f32[2,7,16,128]{3,2,1,0:T(8,128)S(1)} %get-tuple-element.30.below_ref, f32[2,7,16,128]{3,2,1,0:T(8,128)S(1)} %get-tuple-element.31.above_ref, ...), custom_call_target="tpu_custom_call" | custom-call | flops 10000000 | bytes 2000000 | tf_op jit(solution)/shard_map/first_b/pallas_call | solution.py:401
  22.7 13.1 %all-to-all-start = ((f32[64,2,128]{2,1,0:T(2,128)}), f32[64,2,128]{2,1,0:T(2,128)S(1)}, u32[]{:S(2)}, u32[]{:S(2)}) async-start(f32[64,2,128]{2,1,0:T(2,128)} %bitcast.2), calls=%async_computation | async-start | bytes 131072 | tf_op jit(solution)/shard_map/all_to_all | solution.py:396
  35.8 1.8 %second_a.1 = (f32[1792,128]{1,0:T(8,128)S(1)}, f32[144,128]{1,0:T(8,128)S(1)}) custom-call(f32[1792,128]{1,0:T(8,128)S(1)} %get-tuple-element.26.state_ref, f32[8,16,128]{2,1,0:T(8,128)S(1)} %get-tuple-element.27.coef_ref, f32[1792,128]{1,0:T(8,128)S(1)} %get-tuple-element.34.inner_ref, f32[512,128]{1,0:T(8,128)S(1)} %get-tuple-element.38.edge_ref, ...), custom_call_target="tpu_custom_call" | custom-call | flops 60000000 | bytes 2000000 | tf_op jit(solution)/shard_map/second_a/pallas_call | solution.py:401
  37.7 8.4 %all-to-all-done = f32[64,2,128]{2,1,0:T(2,128)S(1)} async-done(((f32[64,2,128]{2,1,0:T(2,128)}), f32[64,2,128]{2,1,0:T(2,128)S(1)}, u32[]{:S(2)}, u32[]{:S(2)}) %all-to-all-start) | async-done | bytes 65568 | tf_op jit(solution)/shard_map/all_to_all | solution.py:396
  46.0 0.6 second_b.1
  46.6 14.0 %all_to_all.10 = f32[64,2,128]{2,1,0:T(2,128)S(1)} all-to-all(f32[64,2,128]{2,1,0:T(2,128)S(1)} %bitcast.9), channel_id=1, replica_groups=mesh['panel'=2,'rad'=12,'ang'=32] {'panel','ang'}, dimensions={0} | all-to-all | bytes 131072 | tf_op jit(solution)/shard_map/all_to_all | solution.py:396
  60.6 1.3 %last.1 = f32[1792,128]{1,0:T(8,128)} custom-call(f32[1792,128]{1,0:T(8,128)S(1)} %get-tuple-element.40.next_ref, f32[32,128]{1,0:T(8,128)S(1)} %get-tuple-element.45.beside_ref, f32[128,128]{1,0:T(8,128)S(1)} %bitcast.8, f32[32,128]{1,0:T(8,128)S(1)} %get-tuple-element.42.placed_ref), custom_call_target="tpu_custom_call" | custom-call | tf_op jit(solution)/shard_map/last/pallas_call | solution.py:463
Async XLA Ops:
  0.0 7.1 %copy-start = (f32[2,2,512]{2,1,0:T(2,128)S(1)}, f32[2,2,512]{2,1,0:T(2,128)}, u32[]{:S(2)}) copy-start(f32[2,2,512]{2,1,0:T(2,128)} %frac_ref.1) | copy-start | bytes 24580
  0.0 7.1 %copy-start.2 = (s32[2,512]{1,0:T(2,128)S(1)}, s32[2,512]{1,0:T(2,128)}, u32[]{:S(2)}) copy-start(s32[2,512]{1,0:T(2,128)} %lon_ref.1) | copy-start | bytes 12292
  0.0 7.1 %copy-start.3 = (s32[2,512]{1,0:T(2,128)S(1)}, s32[2,512]{1,0:T(2,128)}, u32[]{:S(2)}) copy-start(s32[2,512]{1,0:T(2,128)} %lat_ref.1) | copy-start | bytes 12292
  1.4 5.8 %copy-start.1 = (f32[7,16]{1,0:T(8,128)S(1)}, f32[7,16]{1,0:T(8,128)}, u32[]{:S(2)}) copy-start(f32[7,16]{1,0:T(8,128)} %kappa_ref.1) | copy-start | bytes 1348
  1.4 6.3 %collective-permute-start = (f32[2,7,16,128]{3,2,1,0:T(8,128)S(1)}, f32[2,7,16,128]{3,2,1,0:T(8,128)S(1)}, u32[]{:S(2)}, u32[]{:S(2)}) collective-permute-start(f32[2,7,16,128]{3,2,1,0:T(8,128)S(1)} %get-tuple-element.28), channel_id=1, source_target_pairs={{1,2},{3,4},{5,6},{7,8},{9,10},{11,12},{13,14},{15,16},{17,18},{19... | collective-permute-start | bytes 344072 | tf_op jit(solution)/shard_map/ppermute | solution.py:391
  5.1 2.0 %copy-start.4 = (f32[16]{0:T(128)S(1)}, f32[16]{0:T(128)}, u32[]{:S(2)}) copy-start(f32[16]{0:T(128)} %param.8) | copy-start | bytes 196
  5.2 3.2 %collective-permute-start.1 = (f32[2,7,16,128]{3,2,1,0:T(8,128)S(1)}, f32[2,7,16,128]{3,2,1,0:T(8,128)S(1)}, u32[]{:S(2)}, u32[]{:S(2)}) collective-permute-start(f32[2,7,16,128]{3,2,1,0:T(8,128)S(1)} %get-tuple-element.29), channel_id=1, source_target_pairs={{0,1},{2,3},{4,5},{6,7},{8,9},{10,11},{12,13},{14,15},{16,17},{18,... | collective-permute-start | bytes 344072 | tf_op jit(solution)/shard_map/ppermute | solution.py:391
  8.4 8.9 %collective-permute-start.2 = (f32[7,40,128]{2,1,0:T(8,128)S(1)}, f32[7,40,128]{2,1,0:T(8,128)S(1)}, u32[]{:S(2)}, u32[]{:S(2)}) collective-permute-start(f32[7,40,128]{2,1,0:T(8,128)S(1)} %get-tuple-element.35), channel_id=1, source_target_pairs={{0,32},{32,64},{64,96},{96,128},{128,160},{160,192},{192,224},{224... | collective-permute-start | bytes 430088 | tf_op jit(solution)/shard_map/ppermute | solution.py:385
  13.7 8.0 %collective-permute-start.3 = (f32[7,40,128]{2,1,0:T(8,128)S(1)}, f32[7,40,128]{2,1,0:T(8,128)S(1)}, u32[]{:S(2)}, u32[]{:S(2)}) collective-permute-start(f32[7,40,128]{2,1,0:T(8,128)S(1)} %get-tuple-element.36), channel_id=1, source_target_pairs={{32,0},{64,32},{96,64},{128,96},{160,128},{192,160},{224,192},{256... | collective-permute-start | bytes 430088 | tf_op jit(solution)/shard_map/ppermute | solution.py:385
  22.7 23.3 %all-to-all-start = ((f32[64,2,128]{2,1,0:T(2,128)}), f32[64,2,128]{2,1,0:T(2,128)S(1)}, u32[]{:S(2)}, u32[]{:S(2)}) async-start(f32[64,2,128]{2,1,0:T(2,128)} %bitcast.2), calls=%async_computation | async-start | bytes 131072 | tf_op jit(solution)/shard_map/all_to_all | solution.py:396
